TPU v7x, 32 devices: a whole 2x2x4 slice. The times are simulated.
32 devices in a mesh: seq: 8 (over z, x), blk: 4 (over y, core).
Axes of the slice: x: 2, y: 2, z: 4, core: 2. Of those that a mesh axis runs over, the one named last changes fastest.
Arguments:
- words: bfloat16 [8, 512, 768], P('seq', 'blk'), may hold values from -6 to 6
- entities: bfloat16 [8, 128, 768], P('seq'), may hold values from -6 to 6
- segments: int32 [8, 512], P('seq'), may hold values from 0 to 2, as said below
- entity_counts: int32 [8], P('seq'), may hold values from 32 to 128, as said below
- entity_anchor: int32 [8, 128], P('seq'), may hold values from 0 to 511
- query_weights: bfloat16 [1, 4, 768, 768], P(None, None, ('seq', 'blk')), may hold values from -0.21875 to 0.21875
- kv_weights: bfloat16 [1, 2, 768, 768], P(None, None, ('seq', 'blk')), may hold values from -0.21875 to 0.21875
- out_weight: bfloat16 [1, 768, 768], P(None, ('seq', 'blk')), may hold values from -2.5 to 2.5
- ff_in: bfloat16 [1, 768, 3072], P(None, ('seq', 'blk')), may hold values from -0.21875 to 0.21875
- ff_out: bfloat16 [1, 3072, 768], P(None, ('seq', 'blk')), may hold values from -0.109375 to 0.109375
- norm_gain: bfloat16 [1, 2, 768], P(None, None, ('seq', 'blk')), may hold values from 0.5 to 1.5
- norm_bias: bfloat16 [1, 2, 768], P(None, None, ('seq', 'blk')), may hold values from -1.5 to 1.5
- grad_words: bfloat16 [8, 512, 768], P('seq', 'blk'), may hold values from -6 to 6
- grad_entities: bfloat16 [8, 128, 768], P('seq'), may hold values from -6 to 6
Outputs:
- out_words: bfloat16 [8, 512, 768], P('seq', 'blk')
- out_entities: bfloat16 [8, 128, 768], P('seq')
- input_grad_words: float32 [8, 512, 768], P('seq', 'blk')
- input_grad_entities: float32 [8, 128, 768], P('seq')
- grad_query: float32 [1, 4, 768, 768], P(None, None, ('seq', 'blk'))
- grad_kv: float32 [1, 2, 768, 768], P(None, None, ('seq', 'blk'))
- grad_out: float32 [1, 768, 768], P(None, ('seq', 'blk'))
- grad_ff_in: float32 [1, 768, 3072], P(None, ('seq', 'blk'))
- grad_ff_out: float32 [1, 3072, 768], P(None, ('seq', 'blk'))
- grad_gain: float32 [1, 2, 768], P(None, None, ('seq', 'blk'))
- grad_bias: float32 [1, 2, 768], P(None, None, ('seq', 'blk'))
Inputs may be any that keep to these rules, and one draw needn't show every extreme that they name: `segments`: within a sequence segment numbers never fall: 0, then 1 from one of the words 1 to 64, then 2 from one of the last 64 words. `entity_counts`: entities at and past a sequence's count are padding; some sequence has 128 and some has 32.
All inputs are finite; a program needn't handle non-finite values.
Results may differ from a plain program's by a relative error of at most 0.025.
Values may be sent and summed in bfloat16 or wider, within the bound.
No kernel may reach another device: no remote copies, remote signals or barrier semaphores. Data moves between devices by JAX's collectives and lax.ppermute only.
A program may use at most 192 MiB of HBM per device.

v0:
```python
import jax
import jax.numpy as jnp
from jax import lax
from jax.sharding import PartitionSpec as P

HEADS = 12
LAYERS = 1


masked_score = -1e30
epsilon = 1e-05


def shifted(block, axis, distance):
    devices = range(lax.axis_size(axis))
    route = [((i - distance) % len(devices), i) for i in devices]
    return lax.ppermute(block, axis, route)


def joined(x, axis, join):
    gathered = jax.tree.map(
        lambda a, kind: lax.all_gather(a.astype(kind), axis),
        x,
        (jnp.bfloat16, jnp.bfloat16, jnp.bfloat16),
    )

    def take(source):
        return jax.tree.map(
            lambda a, own: lax.dynamic_index_in_dim(a, source, 0, False).astype(own.dtype),
            gathered,
            x,
        )

    return lax.fori_loop(
        1, lax.axis_size(axis), lambda source, state: join(state, take(source)), take(0)
    )


def heads_view(tensor):
    return tensor.reshape(tensor.shape[0], tensor.shape[1], HEADS, tensor.shape[2] // HEADS)


def merge_heads(tensor):
    return tensor.reshape(tensor.shape[0], tensor.shape[1], tensor.shape[2] * tensor.shape[3])


def row_factor(tensor):
    return jnp.transpose(tensor, (0, 2, 1))[..., None]


def scores_of(queries, key_rows):
    return jnp.einsum(
        "sqhd,skhd->shqk",
        heads_view(queries),
        heads_view(key_rows),
        preferred_element_type=jnp.float32,
    )


def same_segment(query_segs, key_segs):
    return (query_segs[:, :, None] == key_segs[:, None, :])[:, None]


def partial_block(queries, key_rows, values, allowed):
    scores = scores_of(queries, key_rows)
    row_top = jnp.max(jnp.where(allowed, scores, masked_score), axis=-1)
    weights = jnp.where(allowed, jnp.exp(scores - row_top[..., None]), 0.0)
    row_total = jnp.sum(weights, axis=-1)
    row_accum = jnp.einsum(
        "shqk,skhd->sqhd",
        weights.astype(jnp.bfloat16),
        heads_view(values),
        preferred_element_type=jnp.float32,
    )
    return (row_top, row_total, row_accum)


def combine_partial(first_part, second):
    top_one, total_one, accum_one = first_part
    top_two, total_two, accum_two = second
    row_top = jnp.maximum(top_one, top_two)
    factor_one = jnp.exp(top_one - row_top)
    factor_two = jnp.exp(top_two - row_top)
    row_total = total_one * factor_one + total_two * factor_two
    row_accum = accum_one * row_factor(factor_one) + accum_two * row_factor(factor_two)
    return (row_top, row_total, row_accum)


def block_back(queries, key_rows, values, upstream, log_total, row_delta, allowed):
    scores = scores_of(queries, key_rows)
    probabilities = jnp.where(allowed, jnp.exp(scores - log_total[..., None]), 0.0)
    grad_probs = jnp.einsum(
        "sqhd,skhd->shqk",
        heads_view(upstream),
        heads_view(values),
        preferred_element_type=jnp.float32,
    )
    grad_scores = (probabilities * (grad_probs - row_delta[..., None])).astype(jnp.bfloat16)
    grad_query = jnp.einsum(
        "shqk,skhd->sqhd", grad_scores, heads_view(key_rows), preferred_element_type=jnp.float32
    )
    grad_key = jnp.einsum(
        "shqk,sqhd->skhd", grad_scores, heads_view(queries), preferred_element_type=jnp.float32
    )
    grad_value = jnp.einsum(
        "shqk,sqhd->skhd",
        probabilities.astype(jnp.bfloat16),
        heads_view(upstream),
        preferred_element_type=jnp.float32,
    )
    return (merge_heads(grad_query), merge_heads(grad_key), merge_heads(grad_value))


def flat_rows(tensor):
    return tensor.reshape(-1, tensor.shape[-1])


def forward_product(operand, matrix):
    return jnp.dot(operand, matrix, preferred_element_type=jnp.float32)


def backward_product(upstream, matrix):
    return lax.dot_general(
        upstream, matrix, (((1,), (1,)), ((), ())), preferred_element_type=jnp.float32
    )


def weight_product(operand, upstream):
    return lax.dot_general(
        operand, upstream, (((0,), (0,)), ((), ())), preferred_element_type=jnp.float32
    )


def layer_norm(tensor, norm_scale, norm_shift):
    center = tensor - jnp.mean(tensor, axis=-1, keepdims=True)
    inverse = lax.rsqrt(jnp.mean(center * center, axis=-1, keepdims=True) + epsilon)
    normed = center * inverse
    return (normed * norm_scale + norm_shift, normed, inverse)


def norm_back(upstream, normed, inverse, norm_scale, row_weight):
    grad_scale = jnp.sum(upstream * normed * row_weight, axis=0)
    grad_shift = jnp.sum(upstream * row_weight, axis=0)
    scaled = upstream * norm_scale
    result = inverse * (
        scaled
        - jnp.mean(scaled, axis=-1, keepdims=True)
        - normed * jnp.mean(scaled * normed, axis=-1, keepdims=True)
    )
    return (result, grad_scale, grad_shift)


def gelu_exact(tensor):
    return jax.nn.gelu(tensor, approximate=False)


def head_delta(upstream, context):
    return jnp.transpose(
        jnp.sum(heads_view(upstream.astype(jnp.float32) * context), axis=-1), (0, 2, 1)
    )


def per_device(
    words,
    entities,
    segments,
    entity_counts,
    entity_anchor,
    query_weights,
    kv_weights,
    out_weight,
    ff_in,
    ff_out,
    norm_gain,
    norm_bias,
    grad_words,
    grad_entities,
):
    blocks = lax.axis_size("blk")
    position = lax.axis_index("blk")
    seq_count, word_rows, model_width = words.shape
    ent_rows = entities.shape[1]
    factor = (model_width // HEADS) ** (-0.5)
    entity_share = 1.0 / blocks
    word_count = seq_count * word_rows
    ent_count = seq_count * ent_rows
    seg_local = lax.dynamic_slice_in_dim(segments, position * word_rows, word_rows, 1)
    seg_ents = jnp.take_along_axis(segments, entity_anchor, axis=1)
    live_ents = jnp.arange(ent_rows, dtype=jnp.int32)[None, :] < entity_counts[:, None]
    allow_we = same_segment(seg_local, seg_ents) & live_ents[:, None, None, :]
    allow_ew = same_segment(seg_ents, seg_local)
    allow_ee = same_segment(seg_ents, seg_ents) & live_ents[:, None, None, :]
    row_weight = jnp.concatenate(
        [
            jnp.ones((word_count, 1), jnp.float32),
            jnp.full((ent_count, 1), entity_share, jnp.float32),
        ],
        axis=0,
    )
    row_weight_low = row_weight.astype(jnp.bfloat16)

    def word_mask(first_row, row_total):
        return same_segment(seg_local, lax.dynamic_slice_in_dim(segments, first_row, row_total, 1))

    def project(rows_flat, matrix, multiplier, row_total):
        return (
            (forward_product(rows_flat, matrix) * multiplier)
            .astype(jnp.bfloat16)
            .reshape(seq_count, row_total, model_width)
        )

    word_state = words
    entity_state = entities
    layer_index = 0
    weights = (
        lax.all_gather(query_weights[layer_index], ("seq", "blk"), axis=1, tiled=True),
        lax.all_gather(kv_weights[layer_index], ("seq", "blk"), axis=1, tiled=True),
        lax.all_gather(out_weight[layer_index], ("seq", "blk"), axis=0, tiled=True),
        lax.all_gather(ff_in[layer_index], ("seq", "blk"), axis=0, tiled=True),
        lax.all_gather(ff_out[layer_index], ("seq", "blk"), axis=0, tiled=True),
        lax.all_gather(norm_gain[layer_index], ("seq", "blk"), axis=1, tiled=True),
        lax.all_gather(norm_bias[layer_index], ("seq", "blk"), axis=1, tiled=True),
    )
    query_full, kv_full, out_full, ff_in_full, ff_out_full, gain_full, shift_full = weights
    word_low = word_state
    entity_low = entity_state
    word_flat = flat_rows(word_low)
    entity_flat = flat_rows(entity_low)
    word_word_query = project(word_flat, query_full[0], factor, word_rows)
    word_entity_query = project(word_flat, query_full[1], factor, word_rows)
    entity_word_query = project(entity_flat, query_full[2], factor, ent_rows)
    entity_entity_query = project(entity_flat, query_full[3], factor, ent_rows)
    word_keys = project(word_flat, kv_full[0], 1.0, word_rows)
    word_values = project(word_flat, kv_full[1], 1.0, word_rows)
    entity_keys = project(entity_flat, kv_full[0], 1.0, ent_rows)
    entity_values = project(entity_flat, kv_full[1], 1.0, ent_rows)
    start_part = partial_block(word_entity_query, entity_keys, entity_values, allow_we)
    running = start_part
    travel = jnp.stack((word_keys, word_values))
    for cycle_step in range(blocks):
        owner_block = (position - cycle_step) % blocks
        pieces = (travel[0], travel[1])
        running = combine_partial(
            running,
            partial_block(
                word_word_query,
                pieces[0],
                pieces[1],
                word_mask(owner_block * word_rows, pieces[0].shape[1]),
            ),
        )
        if cycle_step + 1 < blocks:
            travel = shifted(travel, "blk", 1)
    word_top, word_total, word_accum = running
    word_context = merge_heads(word_accum / row_factor(word_total))
    word_logsum = word_top + jnp.log(word_total)
    local_part = partial_block(entity_word_query, word_keys, word_values, allow_ew)
    merged_top, merged_total, merged_accum = joined(
        (local_part[0], local_part[1], local_part[2]), "blk", combine_partial
    )
    entity_top, entity_total, entity_accum = combine_partial(
        (merged_top, merged_total, merged_accum),
        partial_block(entity_entity_query, entity_keys, entity_values, allow_ee),
    )
    entity_context = merge_heads(entity_accum / row_factor(entity_total))
    entity_logsum = entity_top + jnp.log(entity_total)
    context_low = jnp.concatenate(
        [flat_rows(word_context), flat_rows(entity_context)], axis=0
    ).astype(jnp.bfloat16)
    residual = jnp.concatenate([flat_rows(word_state), flat_rows(entity_state)], axis=0).astype(
        jnp.float32
    )
    mixed_rows, normed_one, inverse_one = layer_norm(
        residual + forward_product(context_low, out_full),
        gain_full[0].astype(jnp.float32),
        shift_full[0].astype(jnp.float32),
    )
    mixed_low = mixed_rows.astype(jnp.bfloat16)
    hidden = forward_product(mixed_low, ff_in_full)
    active = gelu_exact(hidden).astype(jnp.bfloat16)
    result, normed_two, inverse_two = layer_norm(
        mixed_rows + forward_product(active, ff_out_full),
        gain_full[1].astype(jnp.float32),
        shift_full[1].astype(jnp.float32),
    )
    stored = (
        word_flat,
        entity_flat,
        word_word_query,
        word_entity_query,
        entity_word_query,
        entity_entity_query,
        word_keys,
        word_values,
        entity_keys,
        entity_values,
        word_context,
        entity_context,
        word_logsum,
        entity_logsum,
        context_low,
        normed_one,
        inverse_one,
        mixed_low,
        hidden,
        normed_two,
        inverse_two,
    )
    result, stored = (result, stored)
    weights_kept = [weights]
    stored_kept = [stored]
    word_state = result[:word_count].reshape(seq_count, word_rows, model_width)
    entity_state = result[word_count:].reshape(seq_count, ent_rows, model_width)
    upstream = jnp.concatenate([flat_rows(grad_words), flat_rows(grad_entities)], axis=0).astype(
        jnp.float32
    )
    reduced = [None] * LAYERS
    for layer_index in reversed(range(LAYERS)):
        (
            backward_query_full,
            backward_kv_full,
            backward_out_full,
            backward_ff_in_full,
            backward_ff_out_full,
            backward_gain_full,
            backward_shift_full,
        ) = weights_kept[layer_index]
        (
            backward_word_flat,
            backward_entity_flat,
            backward_word_word_query,
            backward_word_entity_query,
            backward_entity_word_query,
            backward_entity_entity_query,
            backward_word_keys,
            backward_word_values,
            backward_entity_keys,
            backward_entity_values,
            backward_word_context,
            backward_entity_context,
            backward_word_logsum,
            backward_entity_logsum,
            backward_context_low,
            backward_normed_one,
            backward_inverse_one,
            backward_mixed_low,
            backward_hidden,
            backward_normed_two,
            backward_inverse_two,
        ) = stored_kept[layer_index]
        grad_pre_two, grad_gain_two, grad_shift_two = norm_back(
            upstream,
            backward_normed_two,
            backward_inverse_two,
            backward_gain_full[1].astype(jnp.float32),
            row_weight,
        )
        grad_branch = grad_pre_two.astype(jnp.bfloat16)
        backward_active = gelu_exact(backward_hidden).astype(jnp.bfloat16)
        grad_last_w = weight_product(backward_active, grad_branch * row_weight_low)
        grad_active = backward_product(grad_branch, backward_ff_out_full)
        unused_value, gelu_pull = jax.vjp(gelu_exact, backward_hidden)
        grad_hidden = gelu_pull(grad_active)[0].astype(jnp.bfloat16)
        grad_in_w = weight_product(backward_mixed_low, grad_hidden * row_weight_low)
        grad_mixed = grad_pre_two + backward_product(grad_hidden, backward_ff_in_full)
        grad_pre_one, grad_gain_one, grad_shift_one = norm_back(
            grad_mixed,
            backward_normed_one,
            backward_inverse_one,
            backward_gain_full[0].astype(jnp.float32),
            row_weight,
        )
        grad_attn = grad_pre_one.astype(jnp.bfloat16)
        grad_out_w = weight_product(backward_context_low, grad_attn * row_weight_low)
        grad_context = backward_product(grad_attn, backward_out_full).astype(jnp.bfloat16)
        grad_word_ctx = grad_context[:word_count].reshape(seq_count, word_rows, model_width)
        grad_entity_ctx = grad_context[word_count:].reshape(seq_count, ent_rows, model_width)
        word_delta = head_delta(grad_word_ctx, backward_word_context)
        entity_delta = head_delta(grad_entity_ctx, backward_entity_context)
        grad_wq_entity, grad_ek_words, grad_ev_words = block_back(
            backward_word_entity_query,
            backward_entity_keys,
            backward_entity_values,
            grad_word_ctx,
            backward_word_logsum,
            word_delta,
            allow_we,
        )
        grad_wq_word = jnp.zeros((seq_count, word_rows, model_width), jnp.float32)
        backward_travel = jnp.stack((backward_word_keys, backward_word_values))
        carried = jnp.zeros((2, seq_count, word_rows, model_width), jnp.float32)
        for backward_cycle_step in range(blocks):
            backward_owner_block = (position - backward_cycle_step) % blocks
            part_query, part_key, part_value = block_back(
                backward_word_word_query,
                backward_travel[0],
                backward_travel[1],
                grad_word_ctx,
                backward_word_logsum,
                word_delta,
                word_mask(backward_owner_block * word_rows, word_rows),
            )
            grad_wq_word = grad_wq_word + part_query
            carried = carried + jnp.stack((part_key, part_value))
            if backward_cycle_step + 1 < blocks:
                backward_travel = shifted(backward_travel, "blk", 1)
            carried = shifted(carried.astype(jnp.bfloat16), "blk", 1).astype(carried.dtype)
        grad_eq_word_part, grad_wk_ents, grad_wv_ents = block_back(
            backward_entity_word_query,
            backward_word_keys,
            backward_word_values,
            grad_entity_ctx,
            backward_entity_logsum,
            entity_delta,
            allow_ew,
        )
        grad_eq_entity, grad_ek_ents, grad_ev_ents = block_back(
            backward_entity_entity_query,
            backward_entity_keys,
            backward_entity_values,
            grad_entity_ctx,
            backward_entity_logsum,
            entity_delta,
            allow_ee,
        )
        summed_query = lax.psum(grad_eq_word_part.astype(jnp.bfloat16), "blk")
        summed_key = lax.psum(grad_ek_words.astype(jnp.bfloat16), "blk").astype(jnp.float32)
        summed_value = lax.psum(grad_ev_words.astype(jnp.bfloat16), "blk").astype(jnp.float32)
        low_ww = flat_rows(grad_wq_word.astype(jnp.bfloat16)) * factor
        low_we = flat_rows(grad_wq_entity.astype(jnp.bfloat16)) * factor
        low_ew = flat_rows(summed_query) * factor
        low_ee = flat_rows(grad_eq_entity.astype(jnp.bfloat16)) * factor
        low_word_key = flat_rows((carried[0] + grad_wk_ents).astype(jnp.bfloat16))
        low_word_value = flat_rows((carried[1] + grad_wv_ents).astype(jnp.bfloat16))
        low_entity_key = flat_rows((summed_key + grad_ek_ents).astype(jnp.bfloat16))
        low_entity_value = flat_rows((summed_value + grad_ev_ents).astype(jnp.bfloat16))
        grad_query_w = jnp.stack(
            [
                weight_product(backward_word_flat, low_ww),
                weight_product(backward_word_flat, low_we),
                weight_product(backward_entity_flat, low_ew * entity_share),
                weight_product(backward_entity_flat, low_ee * entity_share),
            ]
        )
        grad_kv_w = jnp.stack(
            [
                weight_product(backward_word_flat, low_word_key)
                + weight_product(backward_entity_flat, low_entity_key * entity_share),
                weight_product(backward_word_flat, low_word_value)
                + weight_product(backward_entity_flat, low_entity_value * entity_share),
            ]
        )
        grad_word_in = (
            grad_pre_one[:word_count]
            + backward_product(low_ww, backward_query_full[0])
            + backward_product(low_we, backward_query_full[1])
            + backward_product(low_word_key, backward_kv_full[0])
            + backward_product(low_word_value, backward_kv_full[1])
        )
        grad_entity_in = (
            grad_pre_one[word_count:]
            + backward_product(low_ew, backward_query_full[2])
            + backward_product(low_ee, backward_query_full[3])
            + backward_product(low_entity_key, backward_kv_full[0])
            + backward_product(low_entity_value, backward_kv_full[1])
        )
        gradients = (
            grad_query_w,
            grad_kv_w,
            grad_out_w,
            grad_in_w,
            grad_last_w,
            jnp.stack([grad_gain_one, grad_gain_two]),
            jnp.stack([grad_shift_one, grad_shift_two]),
        )
        gradients, upstream = (gradients, jnp.concatenate([grad_word_in, grad_entity_in], axis=0))
        sum_query, sum_kv, sum_out, sum_in, sum_last, sum_gain, sum_shift = gradients
        reduced[layer_index] = (
            lax.psum_scatter(sum_query, ("seq", "blk"), scatter_dimension=1, tiled=True),
            lax.psum_scatter(sum_kv, ("seq", "blk"), scatter_dimension=1, tiled=True),
            lax.psum_scatter(sum_out, ("seq", "blk"), scatter_dimension=0, tiled=True),
            lax.psum_scatter(sum_in, ("seq", "blk"), scatter_dimension=0, tiled=True),
            lax.psum_scatter(sum_last, ("seq", "blk"), scatter_dimension=0, tiled=True),
            lax.psum_scatter(sum_gain, ("seq", "blk"), scatter_dimension=1, tiled=True),
            lax.psum_scatter(sum_shift, ("seq", "blk"), scatter_dimension=1, tiled=True),
        )
    stacked = [jnp.stack([reduced[0][member]]) for member in range(7)]
    input_word_grad = upstream[:word_count].reshape(seq_count, word_rows, model_width)
    input_entity_grad = upstream[word_count:].reshape(seq_count, ent_rows, model_width)
    return (
        word_state.astype(jnp.bfloat16),
        entity_state.astype(jnp.bfloat16),
        input_word_grad,
        input_entity_grad,
        stacked[0],
        stacked[1],
        stacked[2],
        stacked[3],
        stacked[4],
        stacked[5],
        stacked[6],
    )


def solution(mesh):
    placed = (
        P("seq", "blk", None),
        P("seq", None, None),
        P("seq", None),
        P("seq"),
        P("seq", None),
        P(None, None, ("seq", "blk"), None),
        P(None, None, ("seq", "blk"), None),
        P(None, ("seq", "blk"), None),
        P(None, ("seq", "blk"), None),
        P(None, ("seq", "blk"), None),
        P(None, None, ("seq", "blk")),
        P(None, None, ("seq", "blk")),
        P("seq", "blk", None),
        P("seq", None, None),
    )
    return jax.shard_map(
        per_device,
        mesh=mesh,
        in_specs=placed,
        out_specs=(
            P("seq", "blk", None),
            P("seq", None, None),
            P("seq", "blk", None),
            P("seq", None, None),
            P(None, None, ("seq", "blk"), None),
            P(None, None, ("seq", "blk"), None),
            P(None, ("seq", "blk"), None),
            P(None, ("seq", "blk"), None),
            P(None, ("seq", "blk"), None),
            P(None, None, ("seq", "blk")),
            P(None, None, ("seq", "blk")),
        ),
        check_vma=False,
    )
```

profile of v0, /device:TPU:0, one launch (start us, length us, event | category | flops | bytes accessed | tf_op | source)
XLA Modules:
  0.0 1107.4 jit_solution(3509475098257513881)
XLA Ops:
  15.8 44.6 %all-gather.7 = bf16[1,2,768]{1,0,2:T(2,128)(2,1)S(1)} all-gather(bf16[1,2,24]{1,0,2:T(2,128)(2,1)S(1)} %copy.284), channel_id=9, replica_groups=mesh['seq'=8,'blk'=4] {'seq','blk'}, dimensions={2}, use_global_device_ids=true | all-gather | bytes 3168 | tf_op jit(solution)/shard_map/all_gather | solution.py:222
  60.5 5.2 fusion.127
  65.6 38.0 %all-gather.6 = bf16[1,2,768]{1,0,2:T(2,128)(2,1)S(1)} all-gather(bf16[1,2,24]{1,0,2:T(2,128)(2,1)S(1)} %copy.283), channel_id=8, replica_groups=mesh['seq'=8,'blk'=4] {'seq','blk'}, dimensions={2}, use_global_device_ids=true | all-gather | bytes 3168 | tf_op jit(solution)/shard_map/all_gather | solution.py:221
  121.9 9.9 collective-permute-done.1
  143.5 5.2 all-gather.10
  148.7 5.2 all-gather.11
  154.1 9.1 all-gather.4
  164.7 7.7 while.19
  189.2 7.0 all-gather.22.cloned.1.call-done
  200.3 61.2 %all-gather.24.cloned.1.call-done = bf16[1,768,3072]{2,1,0:T(8,128)(2,1)} async-done(((bf16[1,24,3072]{2,1,0:T(8,128)(2,1)}), bf16[1,768,3072]{2,1,0:T(8,128)(2,1)}) %all-gather.24.cloned.1.call-update) | async-done | bytes 4718608 | tf_op jit(solution)/shard_map/all_gather | solution.py:219
  261.6 22.7 %multiply_convert_fusion = (bf16[256,3072]{1,0:T(8,128)(2,1)}, f32[256,3072]{1,0:T(8,128)}, f32[256,3072]{1,0:T(8,128)}) fusion(bf16[1,768,3072]{2,1,0:T(8,128)(2,1)} %all-gather.24.cloned.1.call-done, f32[256,768]{1,0:T(8,128)} %copy-done.12, f32[768]{0:T(1024)} %get-tuple-element.275, f32[768]{0:T(1024)} %get-tuple-element.273, ...), kind=kOutput, calls=%fused_computation.25 | convolution fusion | flops 1260060672 | bytes 13377536 | tf_op jit(solution)/shard_map/dot_general | solution.py:119
  284.3 42.4 %all-gather.26.cloned.1.call-done = bf16[1,3072,768]{2,1,0:T(8,128)(2,1)} async-done(((bf16[1,96,768]{2,1,0:T(8,128)(2,1)}), bf16[1,3072,768]{2,1,0:T(8,128)(2,1)}) %all-gather.26.cloned.1.call-update) | async-done | bytes 4718608 | tf_op jit(solution)/shard_map/all_gather | solution.py:220
  392.0 29.2 %all-reduce.12.cloned.1.call-done = (bf16[1,128,768]{1,2,0:T(8,128)(2,1)}, bf16[1,128,768]{1,2,0:T(8,128)(2,1)}, bf16[1,128,768]{1,2,0:T(8,128)(2,1)}) async-done(((bf16[1,128,768]{1,2,0:T(8,128)(2,1)}, bf16[1,128,768]{1,2,0:T(8,128)(2,1)}, bf16[1,128,768]{1,2,0:T(8,128)(2,1)}), (bf16[1,128,768]{1,2,0:T(8,128)(2,1)}, bf16[1,128,768]{1,2,0:T(8,128)(2,1)}, ...) | async-done | bytes 589840 | tf_op jit(solution)/shard_map/psum | solution.py:426
  423.8 6.3 pad_maximum_fusion
  430.1 12.2 %copy.319 = f32[4,768,768]{2,0,1:T(4,128)} copy(f32[4,768,768]{1,2,0:T(8,128)} %pad_maximum_fusion) | data formatting | bytes 18874368 | tf_op jit(solution)/shard_map/stack | solution.py:437
  443.9 6.8 collective-permute-done.6
  455.5 8.2 copy.320
  467.9 5.8 fusion.21
  475.5 6.4 fusion.133
  482.6 40.9 %all-reduce.4 = (f32[2,768]{1,0:T(2,128)S(1)}, f32[2,768]{1,0:T(2,128)S(1)}) all-reduce(f32[2,768]{1,0:T(2,128)S(1)} %pad_maximum_fusion.8, f32[2,768]{1,0:T(2,128)S(1)} %pad_maximum_fusion.9), channel_id=17, replica_groups=mesh['seq'=8,'blk'=4] {'seq','blk'}, use_global_device_ids=true, to_apply=%region_36.37.clone | all-reduce | flops 3072 | bytes 24576
  536.8 175.4 %all-reduce.10.cloned.1.call-done = (f32[4,768,768]{2,0,1:T(4,128)}, f32[2,768,768]{2,0,1:T(2,128)}) async-done(((f32[4,768,768]{2,0,1:T(4,128)}, f32[2,768,768]{2,0,1:T(2,128)}), (f32[4,768,768]{2,0,1:T(4,128)}, f32[2,768,768]{2,0,1:T(2,128)})) %all-reduce.10.cloned.1.call-update) | async-done | bytes 14155792
  715.6 101.6 %reduce-scatter.6.cloned.1.call-done = f32[24,768]{1,0:T(8,128)} async-done(((f32[768,768]{1,0:T(8,128)}), f32[24,768]{1,0:T(8,128)}) %reduce-scatter.6.cloned.1.call-update) | async-done | bytes 73744 | tf_op jit(solution)/shard_map/reduce_scatter | solution.py:481
  817.1 142.1 %reduce-scatter.8.cloned.1.call-done = f32[24,3072]{1,0:T(8,128)} async-done(((f32[768,3072]{1,0:T(8,128)}), f32[24,3072]{1,0:T(8,128)}) %reduce-scatter.8.cloned.1.call-update) | async-done | bytes 294928 | tf_op jit(solution)/shard_map/reduce_scatter | solution.py:482
  959.3 141.0 %reduce-scatter.10.cloned.1.call-done = f32[96,768]{1,0:T(8,128)} async-done(((f32[3072,768]{1,0:T(8,128)}), f32[96,768]{1,0:T(8,128)}) %reduce-scatter.10.cloned.1.call-update) | async-done | bytes 294928 | tf_op jit(solution)/shard_map/reduce_scatter | solution.py:483
  (505 shorter events, 163.4 us)
Async XLA Ops:
  7.2 99.0 %copy-start.32 = (bf16[1,128,768]{2,1,0:T(8,128)(2,1)S(1)}, bf16[1,128,768]{2,1,0:T(8,128)(2,1)}, u32[]{:S(2)}) copy-start(bf16[1,128,768]{2,1,0:T(8,128)(2,1)} %param.16) | copy-start | bytes 589828
  7.2 97.2 %all-gather.18.cloned.1.call-start = ((), (), s32[]{:S(2)}) async-start(), calls=%async_computation.6 | async-start | bytes 2433024 | tf_op jit(solution)/shard_map/all_gather | solution.py:217
  7.9 133.2 %all-gather.20.cloned.1.call-start = ((), (), s32[]{:S(2)}) async-start(), calls=%async_computation.7 | async-start | bytes 4866048 | tf_op jit(solution)/shard_map/all_gather | solution.py:216
  8.7 187.6 %all-gather.22.cloned.1.call-start = ((), (), s32[]{:S(2)}) async-start(), calls=%async_computation.8 | async-start | bytes 1216512 | tf_op jit(solution)/shard_map/all_gather | solution.py:218
  9.4 252.1 %all-gather.24.cloned.1.call-start = ((), (), s32[]{:S(2)}) async-start(), calls=%async_computation.9 | async-start | bytes 4866048 | tf_op jit(solution)/shard_map/all_gather | solution.py:219
  10.0 316.7 %all-gather.26.cloned.1.call-start = ((), (), s32[]{:S(2)}) async-start(), calls=%async_computation.10 | async-start | bytes 4866048 | tf_op jit(solution)/shard_map/all_gather | solution.py:220
  10.6 410.7 %all-reduce.12.cloned.1.call-start = ((), (), s32[]{:S(2)}) async-start(), calls=%async_computation.12 | async-start | bytes 1179648 | tf_op jit(solution)/shard_map/psum | solution.py:426
  108.6 7.4 collective-permute-start
  116.0 15.9 %collective-permute-start.1 = (bf16[2,1,128,768]{3,2,1,0:T(8,128)(2,1)}, bf16[2,1,128,768]{3,2,1,0:T(8,128)(2,1)}, u32[]{:S(2)}, u32[]{:S(2)}) collective-permute-start(bf16[2,1,128,768]{3,2,1,0:T(8,128)(2,1)} %collective-permute-done), channel_id=1, source_target_pairs={{3,0},{0,1},{1,2},{2,3},{7,4},{4,5},{5,6},{6,7},{11,8},{8,9},{9,10... | collective-permute-start | bytes 1179656 | tf_op jit(solution)/shard_map/ppermute | solution.py:17
  117.8 67.7 %copy-start.15 = (bf16[128,768]{0,1:T(8,128)(2,1)}, bf16[128,768]{0,1:T(8,128)(2,1)S(1)}, u32[]{:S(2)}) copy-start(bf16[128,768]{0,1:T(8,128)(2,1)S(1)} %copy.263) | copy-start | bytes 589828
  121.9 59.8 %copy-start.22 = (bf16[128,768]{0,1:T(8,128)(2,1)}, bf16[128,768]{0,1:T(8,128)(2,1)S(1)}, u32[]{:S(2)}) copy-start(bf16[128,768]{0,1:T(8,128)(2,1)S(1)} %copy.259) | copy-start | bytes 589828
  131.8 7.6 collective-permute-start.2
  198.3 86.0 %copy-start.119 = (f32[256]{0:T(256)}, f32[256]{0:T(256)S(1)}, u32[]{:S(2)}) copy-start(f32[256]{0:T(256)S(1)} %broadcast_multiply_fusion.7) | copy-start | bytes 3076
  199.4 84.9 %copy-start.127 = (f32[256]{0:T(256)}, f32[256]{0:T(256)S(1)}, u32[]{:S(2)}) copy-start(f32[256]{0:T(256)S(1)} %add_rsqrt_fusion.1) | copy-start | bytes 3076
  261.5 65.2 %copy-start.107 = (f32[768]{0:T(1024)S(1)}, f32[768]{0:T(1024)}, u32[]{:S(2)}) copy-start(f32[768]{0:T(1024)} %get-tuple-element.273) | copy-start | bytes 9220
  261.5 65.2 %copy-start.109 = (f32[768]{0:T(1024)S(1)}, f32[768]{0:T(1024)}, u32[]{:S(2)}) copy-start(f32[768]{0:T(1024)} %get-tuple-element.275) | copy-start | bytes 9220
  382.6 7.5 collective-permute-start.3
  386.6 325.6 %all-reduce.10.cloned.1.call-start = ((), (), s32[]{:S(2)}) async-start(), calls=%async_computation.11 | async-start | bytes 28311552
  391.3 31.3 %collective-permute-start.4 = (bf16[2,1,128,768]{2,3,1,0:T(8,128)(2,1)S(1)}, bf16[2,1,128,768]{2,3,1,0:T(8,128)(2,1)}, u32[]{:S(2)}, u32[]{:S(2)}) collective-permute-start(bf16[2,1,128,768]{2,3,1,0:T(8,128)(2,1)S(1)} %fusion.80), channel_id=1, source_target_pairs={{3,0},{0,1},{1,2},{2,3},{7,4},{4,5},{5,6},{6,7},{11,8},{8,9},{9,10... | collective-permute-start | bytes 1179656 | tf_op jit(solution)/shard_map/ppermute | solution.py:17
  423.7 18.6 %collective-permute-start.5 = (bf16[2,1,128,768]{2,3,1,0:T(8,128)(2,1)S(1)}, bf16[2,1,128,768]{2,3,1,0:T(8,128)(2,1)}, u32[]{:S(2)}, u32[]{:S(2)}) collective-permute-start(bf16[2,1,128,768]{2,3,1,0:T(8,128)(2,1)S(1)} %fusion.81), channel_id=1, source_target_pairs={{3,0},{0,1},{1,2},{2,3},{7,4},{4,5},{5,6},{6,7},{11,8},{8,9},{9,10... | collective-permute-start | bytes 1179656 | tf_op jit(solution)/shard_map/ppermute | solution.py:17
  443.5 7.3 collective-permute-start.6
  463.8 353.3 %reduce-scatter.6.cloned.1.call-start = ((), (), s32[]{:S(2)}) async-start(), calls=%async_computation.3 | async-start | bytes 2433024 | tf_op jit(solution)/shard_map/reduce_scatter | solution.py:481
  467.8 491.4 %reduce-scatter.8.cloned.1.call-start = ((), (), s32[]{:S(2)}) async-start(), calls=%async_computation.4 | async-start | bytes 9732096 | tf_op jit(solution)/shard_map/reduce_scatter | solution.py:482
  473.8 626.4 %reduce-scatter.10.cloned.1.call-start = ((), (), s32[]{:S(2)}) async-start(), calls=%async_computation.5 | async-start | bytes 9732096 | tf_op jit(solution)/shard_map/reduce_scatter | solution.py:483
  (136 other events, 897.3 us)
Sparse Core Ops, SparseCore 0:
  10.9 60.2 all-gather.17
  74.0 65.4 all-gather.19
  142.4 53.7 all-gather.21
  199.0 62.5 all-gather.23
  264.3 62.3 all-gather.25
  386.7 34.4 all-reduce.11
  463.9 248.2 all-reduce.9
  718.1 99.0 reduce-scatter.5
  824.6 134.5 reduce-scatter.7
  965.6 134.5 reduce-scatter.9
where the time goes:
time: 1120 us; the launch traced here: 1110 us
  waiting for transfers between devices  724 us (65%)
  blocking collectives  143 us (13%)
  matrix products  112 us (10%)
  local copies, waits for them, and re-layouts  67.1 us (6%)
  other arithmetic  40.9 us (4%)
  between operations  17.4 us (2%)
    unnamed x11, waiting for transfers between devices  179 us
    reduce_scatter x1, waiting for transfers between devices, per_device(): lax.psum_scatter(sum_in, ('seq', 'blk'), scatter_dimension=0, tiled=True)  142 us
    reduce_scatter x1, waiting for transfers between devices, per_device(): lax.psum_scatter(sum_last, ('seq', 'blk'), scatter_dimension=0, tiled=True)  141 us
    reduce_scatter x1, waiting for transfers between devices, per_device(): lax.psum_scatter(sum_out, ('seq', 'blk'), scatter_dimension=0, tiled=True)  102 us
    all_gather x1, waiting for transfers between devices, per_device(): lax.all_gather(ff_in[layer_index], ('seq', 'blk'), axis=0, tiled=True)  61.2 us
    all_gather x1, blocking collectives, per_device(): lax.all_gather(norm_bias[layer_index], ('seq', 'blk'), axis=1, tiled=True)  44.6 us
    all_gather x1, waiting for transfers between devices, per_device(): lax.all_gather(ff_out[layer_index], ('seq', 'blk'), axis=0, tiled=True)  42.4 us
    unnamed x1, blocking collectives  40.9 us
  transfers between devices with their start and end apart: 17, of which 13 were waited for; matrix products, arithmetic and copies ran while one was open for 13% of the time, Pallas kernels for 0%

commit v1 on v0

v1 whole, which is shorter than its diff:
```python
import jax
import jax.numpy as jnp
from jax import lax
from jax.experimental import pallas as pl
from jax.experimental.pallas import tpu as pltpu
from jax.sharding import PartitionSpec as P

HEADS = 12
RANKS = 4
epsilon = 1e-05
masked_score = -1e30
bf16 = jnp.bfloat16
f32 = jnp.float32


def dot_nn(a, b):
    return jnp.dot(a, b, preferred_element_type=f32)


def dot_nt(a, b):
    return lax.dot_general(a, b, (((1,), (1,)), ((), ())), preferred_element_type=f32)


def dot_tn(a, b):
    return lax.dot_general(a, b, (((0,), (0,)), ((), ())), preferred_element_type=f32)


def block(ref, index, size):
    return pl.ds(pl.multiple_of(index * size, size), size)


def call(body, name, outs, scratch=(), vmem=10, us=1, held=0, same=0):
    def run(*args):
        return pl.pallas_call(
            body,
            name=name,
            out_shape=[jax.ShapeDtypeStruct(s, t) for s, t in outs],
            in_specs=[pl.BlockSpec(memory_space=pltpu.HBM)] * held
            + [pl.BlockSpec(memory_space=pltpu.VMEM)] * (len(args) - held),
            out_specs=[pl.BlockSpec(memory_space=pltpu.VMEM)] * len(outs),
            scratch_shapes=list(scratch),
            input_output_aliases={i: i for i in range(same)},
            compiler_params=pltpu.CompilerParams(vmem_limit_bytes=vmem << 20),
            cost_estimate=pl.CostEstimate(
                flops=int(us * 1e6), bytes_accessed=int(us * 1e3), transcendentals=0
            ),
        )(*args)

    return run


def partner(k):
    return jnp.bitwise_xor(lax.axis_index("blk"), k)


def ring_seat(k, e):
    s = lax.axis_index("seq")
    z = lax.div(s, 2)
    at = lax.rem(jnp.bitwise_xor(z, lax.div(z, 2)) + (k + 4), 4)
    return 2 * jnp.bitwise_xor(at, lax.div(at, 2)) + jnp.bitwise_xor(lax.rem(s, 2), e)


def ff_rank():
    return 2 * lax.rem(lax.axis_index("seq"), 2) + lax.rem(lax.axis_index("blk"), 2)


def ff_seat(k, e):
    z = lax.div(lax.axis_index("seq"), 2)
    at = lax.rem(jnp.bitwise_xor(z, lax.div(z, 2)) + (k + 4), 4)
    y = jnp.bitwise_xor(lax.div(lax.axis_index("blk"), 2), e)
    return 2 * jnp.bitwise_xor(at, lax.div(at, 2)) + y


def ff_column(rank, j, part):
    return (8 * (j // 2) + 4 * (rank // 2) + 2 * (j % 2) + rank % 2) * part


def ff_rows(seat, x, rows):
    at = 4 * lax.div(seat, 2) + 2 * x + lax.rem(seat, 2)
    return pl.ds(pl.multiple_of(2 * rows * at, 16), 2 * rows)


def norm_stats(u):
    center = u - jnp.mean(u, axis=-1, keepdims=True)
    inverse = lax.rsqrt(jnp.mean(center * center, axis=-1, keepdims=True) + epsilon)
    return center * inverse, inverse


def norm_pull(scaled, normed, inverse):
    return inverse * (
        scaled
        - jnp.mean(scaled, axis=-1, keepdims=True)
        - normed * jnp.mean(scaled * normed, axis=-1, keepdims=True)
    )


def pack_body(*refs):
    sources, firsts, seconds = refs[:6], refs[6:10], refs[10:14]
    scr, scr_ff, here, sems = refs[14], refs[15], refs[16:22], refs[22]
    copies = [
        pltpu.make_async_copy(source, target, sems.at[i])
        for i, (source, target) in enumerate(zip(sources, here))
    ]
    for copy in copies:
        copy.start()
    for copy in copies:
        copy.wait()
    q, kv, wo, gain, bias, ff = here
    rows, wide = q.shape[1], q.shape[2] // RANKS
    part = ff.shape[1] // (8 * RANKS)
    eye = lax.broadcasted_iota(jnp.int32, (rows, rows), 0) == lax.broadcasted_iota(
        jnp.int32, (rows, rows), 1
    )
    lane = lax.broadcasted_iota(jnp.int32, (rows, 64), 1)
    vec = jnp.zeros((rows, 64), f32)
    for j, row in enumerate((gain[0:1], gain[1:2], bias[0:1], bias[1:2])):
        column = jnp.sum(jnp.where(eye, row.astype(f32), 0.0), axis=1, keepdims=True)
        vec = jnp.where(lane == j, column, vec)
    for t in range(RANKS):
        cut = slice(wide * t, wide * t + wide)
        for j, piece in enumerate((q[0], q[1], kv[0], kv[1], q[2], q[3], wo[...])):
            scr[t, :, wide * j : wide * j + wide] = piece[:, cut]
        scr[t, :, 7 * wide :] = vec.astype(bf16)
        for j in range(8):
            at = ff_column(t, j, part)
            scr_ff[t, :, part * j : part * j + part] = ff[:, at : at + part]
    for k in range(RANKS):
        firsts[k][...] = scr[partner(k)]
        seconds[k][...] = scr_ff[jnp.bitwise_xor(ff_rank(), k)]


def arrange_own_body(p0, out):
    out[block(out, partner(0), p0.shape[0])] = p0[...].astype(f32)


def arrange_body(own, p1, p2, p3, slab, scr):
    rows = p1.shape[0]
    scr[...] = own[...]
    for k, p in ((1, p1), (2, p2), (3, p3)):
        scr[block(scr, partner(k), rows)] = p[...].astype(f32)
    slab[...] = scr[...].astype(bf16)


def arrange_ff_body(p0, p1, p2, p3, ff_out, slab, scr):
    rows, cols = p0.shape
    for k, p in enumerate((p0, p1, p2, p3)):
        scr[block(scr, jnp.bitwise_xor(ff_rank(), k), rows)] = p[...].astype(f32)
    slab[:, :cols] = scr[...].astype(bf16)
    slab[:, cols:] = ff_out[...]


def place_body(slots, *refs):
    shards, (wq, wo_first, rest) = refs[-3 - len(slots) : -3], refs[-3:]
    rows, first = shards[0].shape[0], wq.shape[1]
    for j, shard in zip(slots, shards):
        at = block(shard, ring_seat(-(j // 2), j % 2) if rows < wq.shape[0] else 0, rows)
        wq[at] = shard[:, :first]
        wo_first[at] = shard[:, first : first + 128]
        rest[at] = shard[:, first + 128 :]


def place_last_body(slots, *refs):
    wide = refs[0].shape[1] // 6
    ins, (wq, wo_first, rest, wo_col, norms) = refs[:-5], refs[-5:]
    place_body(slots, *ins, wq, wo_first, rest)
    width = wq.shape[0]
    half = width // 2
    tail = rest[...]
    wo_col[:width] = wo_first[...]
    wo_col[width:] = jnp.concatenate([tail[:half, : wide - 128], tail[half:, : wide - 128]], 1)
    norms[...] = tail.astype(f32).T[wide - 128 : wide - 120]


def place_ff_body(slots, *refs):
    shards, w1, w2 = refs[-2 - len(slots) : -2], refs[-2], refs[-1]
    rows, cut = shards[0].shape[0], w1.shape[1]
    if rows == w1.shape[0]:
        w1[...] = shards[0][:, :cut]
        w2[...] = shards[0][:, cut:]
        return
    for j, shard in zip(slots, shards):
        seat = ff_seat(-(j // 2), j % 2)
        for x in (0, 1):
            w1[ff_rows(seat, x, rows // 4)] = shard[rows // 2 * x : rows // 2 * (x + 1), :cut]
        w2[block(shard, seat, rows)] = shard[:, cut:]


def join_out_body(w0, w1, w2, w3, wo, scr):
    wide = wo.shape[1] // RANKS
    half = wo.shape[0] // 2
    for k, w in enumerate((w0, w1, w2, w3)):
        scr[partner(k)] = w[...]
    for t in range(RANKS):
        wo[:, wide * t : wide * t + 128] = scr[t, : 2 * half]
        tail = scr[t, 2 * half :]
        wo[:half, wide * t + 128 : wide * t + wide] = tail[:, : wide - 128]
        wo[half:, wide * t + 128 : wide * t + wide] = tail[:, wide - 128 :]


def join_rows_body(x0, x1, x2, x3, xw):
    local = x0.shape[0]
    for k, x in enumerate((x0, x1, x2, x3)):
        xw[block(xw, partner(k), local)] = x[...]


def attend_body(wide, factor, xw, xe, wq, segq, segk, c0, c1, c2, c3, qw, qe, kk, vv, p_ref, c_scr):
    words, ents = xw.shape[0], xe.shape[0]
    local = words // RANKS
    share = ents // RANKS
    hl = HEADS // RANKS
    dh = wide // hl
    rows = words + ents
    w = dot_nn(xw[...], wq[:, : 4 * wide])
    e_kv = dot_nn(xe[...], wq[:, 2 * wide : 4 * wide])
    e_q = dot_nn(xe[...], wq[:, 4 * wide :])
    qw[:words] = (w[:, :wide] * factor).astype(bf16)
    qe[:words] = (w[:, wide : 2 * wide] * factor).astype(bf16)
    kk[:words] = w[:, 2 * wide : 3 * wide].astype(bf16)
    vv[:words] = w[:, 3 * wide :].astype(bf16)
    qw[words:] = (e_q[:, :wide] * factor).astype(bf16)
    qe[words:] = (e_q[:, wide:] * factor).astype(bf16)
    kk[words:] = e_kv[:, :wide].astype(bf16)
    vv[words:] = e_kv[:, wide:].astype(bf16)
    values_t = vv[...].astype(f32).T.astype(bf16)
    lane_head = lax.broadcasted_iota(jnp.int32, (128, wide), 1) // dh
    segcol = segk[...]

    def query_block(i, carry):
        at = pl.ds(pl.multiple_of(i * 128, 128), 128)
        q_word, q_ent = qw[at], qe[at]
        zero = jnp.zeros_like(q_word)
        stack_w = jnp.concatenate([jnp.where(lane_head == h, q_word, zero) for h in range(hl)], 0)
        stack_e = jnp.concatenate([jnp.where(lane_head == h, q_ent, zero) for h in range(hl)], 0)
        s_w = dot_nt(kk[:words], stack_w)
        s_e = dot_nt(kk[words:], stack_e)
        allowed = segcol == segq[0:1, at]
        probs = []
        for h in range(hl):
            lanes = slice(128 * h, 128 * h + 128)
            s = jnp.concatenate([s_w[:, lanes], s_e[:, lanes]], 0)
            s = jnp.where(allowed, s, masked_score)
            top = jnp.max(s, axis=0, keepdims=True)
            e = jnp.exp(s - top)
            probs.append((e * (1.0 / jnp.sum(e, axis=0, keepdims=True))).astype(bf16))
        prob = jnp.concatenate(probs, 1)
        p_ref[i] = prob
        ctx = dot_nn(values_t, prob)
        ctx = jnp.concatenate(
            [ctx[dh * h : dh * h + dh, 128 * h : 128 * h + 128] for h in range(hl)], 0
        )
        c_scr[at] = ctx.T.astype(bf16)
        return carry

    lax.fori_loop(0, rows // 128, query_block, 0)
    b = lax.axis_index("blk")
    for k, out in enumerate((c0, c1, c2, c3)):
        to = jnp.bitwise_xor(b, k)
        out[:local] = c_scr[block(c_scr, to, local)]
        out[local:] = c_scr[pl.ds(pl.multiple_of(words + to * share, share), share)]


def mix_body(c0, c1, c2, c3, w0, w1, w2, w3, norms, xw, xe, hr, n1, i1, scr):
    b = lax.axis_index("blk")
    rows = c0.shape[0]
    width = xw.shape[1]
    share = rows - xw.shape[0]
    half = width // 2
    cs, ws = (c0, c1, c2, c3), (w0, w1, w2, w3)
    for rank in range(RANKS):

        @pl.when(b == rank)
        def _():
            ctx = jnp.concatenate([cs[rank ^ q][...] for q in range(RANKS)], 1)
            u = []
            for t in range(RANKS):
                w = ws[rank ^ t]
                low = dot_nn(ctx[:, :half], w[width:])[:, :64]
                high = dot_nn(ctx[:, half:], w[width:])[:, 64:]
                u += [dot_nn(ctx, w[:width]), low + high]
            scr[...] = jnp.concatenate(u, 1)

    u = scr[...] + jnp.concatenate([xw[...].astype(f32), xe[block(xe, b, share)].astype(f32)], 0)
    normed, inverse = norm_stats(u)
    n1[...] = normed
    i1[...] = inverse
    hr[...] = (normed * norms[0:1] + norms[2:3]).astype(bf16)


def feed_body(h0, h1, h2, h3, w1, w2, own, across, core, g_all, gp_all):
    outs = (own, core.at[1], across, core.at[0])
    for k, h in enumerate((h0, h1, h2, h3)):
        z = dot_nn(h[...], w1[...])
        cdf = 0.5 * (1.0 + lax.erf(z * 0.7071067811865476))
        g = (z * cdf).astype(bf16)
        g_all[k] = g
        gp_all[k] = (cdf + z * (0.3989422804014327 * jnp.exp(-0.5 * z * z))).astype(bf16)
        outs[k][...] = dot_nn(g, w2[...]).astype(outs[k].dtype)


def turn_body(f0, f1, f2, n1, norms, gw, ge, yw, ye, df, du2, sums):
    b = lax.axis_index("blk")
    local = gw.shape[0]
    rows = n1.shape[0]
    share = rows - local
    n = norms[...]
    u = n1[...] * n[0:1] + n[2:3]
    u = u + (f0[...] + f1[1].astype(f32) + f2[...].astype(f32))
    normed, inverse = norm_stats(u)
    y = (normed * n[1:2] + n[3:4]).astype(bf16)
    yw[...] = y[:local]
    ye[...] = y[local:]
    dy = jnp.concatenate([gw[...].astype(f32), ge[block(ge, b, share)].astype(f32)], 0)
    sums[...] = jnp.concatenate(
        [jnp.sum(dy * normed, axis=0, keepdims=True), jnp.sum(dy, axis=0, keepdims=True)]
        + [jnp.zeros((6, dy.shape[1]), f32)],
        0,
    )
    d = norm_pull(dy * n[1:2], normed, inverse)
    du2[...] = d
    df[...] = d.astype(bf16)


def feed_back_near_body(d0, d1, gp_all, w1, w2, own, beside, dz):
    for k, (d, out) in enumerate(((d0, own), (d1, beside))):
        z = (dot_nt(d[...], w2[...]) * gp_all[k].astype(f32)).astype(bf16)
        dz[k] = z
        out[...] = dot_nt(z, w1[...]).astype(out.dtype)


def feed_back_far_body(d2, d3, gp_all, w1, w2, beside, across, core, dz):
    core[1] = beside[...]
    for k, (d, out) in enumerate(((d2, across), (d3, core.at[0]))):
        z = (dot_nt(d[...], w2[...]) * gp_all[2 + k].astype(f32)).astype(bf16)
        dz[k] = z
        out[...] = dot_nt(z, w1[...]).astype(out.dtype)


def feed_grads_body(d0, d1, d2, d3, h0, h1, h2, h3, g_all, dz_near, dz_far, *refs):
    outs, g_in, g_out = refs[:-2], refs[-2], refs[-1]
    d = jnp.concatenate([x[...] for x in (d0, d1, d2, d3)], 0)
    h = jnp.concatenate([x[...] for x in (h0, h1, h2, h3)], 0)
    g = jnp.concatenate([g_all[k] for k in range(RANKS)], 0)
    z = jnp.concatenate([dz_near[0], dz_near[1], dz_far[0], dz_far[1]], 0)
    g_in[...] = dot_tn(h, z).astype(bf16)
    g_out[...] = dot_tn(g, d).astype(bf16)
    cut = g_in.shape[1]
    if len(outs) == 1:
        outs[0][:, :cut] = g_in[...]
        outs[0][:, cut:] = g_out[...]
        return
    for j, out in enumerate(outs):
        seat = ff_seat(j // 2, j % 2)
        rows = out.shape[0]
        for x in (0, 1):
            out[rows // 2 * x : rows // 2 * (x + 1), :cut] = g_in[ff_rows(seat, x, rows // 4)]
        out[:, cut:] = g_out[block(out, seat, rows)]


def norm_one_body(h0, h1, h2, du2, n1, i1, norms, two, wo, c0, c1, c2, c3, *refs):
    d0, d2, d3, core, du1, w_own, w_across, scr = refs
    wide = d0.shape[1]
    dh = du2[...] + (h0[...] + h1[1].astype(f32) + h2[...].astype(f32))
    width = dh.shape[1]
    normed = n1[...]
    d = norm_pull(dh * norms[0:1], normed, i1[...])
    du1[...] = d
    low = d.astype(bf16)
    dc = [dot_nt(low, wo[block(wo, partner(k), wide)]).astype(bf16) for k in range(RANKS)]
    d0[...] = dc[0]
    core[2 * width :, :wide] = dc[1]
    d2[...] = dc[2]
    d3[...] = dc[3]
    sums = jnp.concatenate(
        [jnp.sum(dh * normed, axis=0, keepdims=True), two[0:1]]
        + [jnp.sum(dh, axis=0, keepdims=True), two[1:2], jnp.zeros((124, width), f32)],
        0,
    )
    for k, c in enumerate((c0, c1, c2, c3)):
        g = dot_tn(c[...], low).astype(bf16)
        at = block(scr, partner(k), wide)
        for t in range(RANKS):
            scr[t, at, :wide] = g[:, wide * t : wide * t + wide]
    vec = sums.T.astype(bf16)
    for t in range(RANKS):
        scr[t, :, wide:] = vec[:, :64]
    w_own[...] = scr[partner(0)]
    core[:width] = scr[partner(3)]
    core[width : 2 * width] = scr[partner(1)]
    w_across[...] = scr[partner(2)]


def attend_back_body(factor, d0, core, d2, d3, qw, qe, kk, vv, p_ref, dqkv, dc, dqw, dqe, dk, dv):
    b = lax.axis_index("blk")
    rows, wide = qw.shape
    local = rows * 4 // 5 // RANKS
    words = local * RANKS
    share = (rows - words) // RANKS
    hl = HEADS // RANKS
    dh = wide // hl
    base = core.shape[0] - d0.shape[0]
    for k, d in enumerate((d0[...], core[base:, :wide], d2[...], d3[...])):
        to = jnp.bitwise_xor(b, k)
        dc[block(dc, to, local)] = d[:local]
        dc[pl.ds(pl.multiple_of(words + to * share, share), share)] = d[local:]
    keys_t = kk[...].astype(f32).T.astype(bf16)
    lane_head = lax.broadcasted_iota(jnp.int32, (128, wide), 1) // dh
    dk[...] = jnp.zeros_like(dk)
    dv[...] = jnp.zeros_like(dv)

    def query_block(i, carry):
        at = pl.ds(pl.multiple_of(i * 128, 128), 128)
        zero = jnp.zeros((128, wide), bf16)

        def stacked(x):
            return jnp.concatenate([jnp.where(lane_head == h, x, zero) for h in range(hl)], 0)

        stack_d = stacked(dc[at])
        prob = p_ref[i]
        dp = dot_nt(vv[...], stack_d)
        parts = []
        for h in range(hl):
            lanes = slice(128 * h, 128 * h + 128)
            p = prob[:, lanes].astype(f32)
            g = dp[:, lanes]
            delta = jnp.sum(p * g, axis=0, keepdims=True)
            parts.append((p * (g - delta)).astype(bf16))
        ds = jnp.concatenate(parts, 1)
        dv[...] += dot_nn(prob, stack_d)
        dk[:words] += dot_nn(ds[:words], stacked(qw[at]))
        dk[words:] += dot_nn(ds[words:], stacked(qe[at]))
        for keys, ds_part, out in ((keys_t[:, :words], ds[:words], dqw), (keys_t[:, words:], ds[words:], dqe)):
            t = dot_nn(keys, ds_part)
            t = jnp.concatenate(
                [t[dh * h : dh * h + dh, 128 * h : 128 * h + 128] for h in range(hl)], 0
            )
            out[at] = t.T
        return carry

    lax.fori_loop(0, rows // 128, query_block, 0)
    dqkv[:, :wide] = (dqw[...] * factor).astype(bf16)
    dqkv[:, wide : 2 * wide] = (dqe[...] * factor).astype(bf16)
    dqkv[:, 2 * wide : 3 * wide] = dk[...].astype(bf16)
    dqkv[:, 3 * wide :] = dv[...].astype(bf16)


def proj_grads_body(dqkv, xw, xe, o0, o1, o2, *refs):
    outs, scr = refs[:-1], refs[-1]
    words = xw.shape[0]
    out_rows = o0.shape[0]
    half = dqkv.shape[1] // 2
    w = dot_tn(xw[...], dqkv[:words])
    e = dot_tn(xe[...], dqkv[words:])
    scr[:, :half] = w[:, :half].astype(bf16)
    scr[:, half : 2 * half] = (w[:, half:] + e[:, half:]).astype(bf16)
    scr[:, 2 * half : 3 * half] = e[:, :half].astype(bf16)
    scr[:, 3 * half :] = (o0[...].astype(f32) + o1[out_rows : 2 * out_rows].astype(f32) + o2[...].astype(f32)).astype(bf16)
    for j, out in enumerate(outs):
        to = ring_seat(j // 2, j % 2) if len(outs) > 1 else 0
        out[...] = scr[block(scr, to, out.shape[0])]


def total_of(parts):
    return parts[0][...].astype(f32) + (parts[1][...].astype(f32) + parts[2][...].astype(f32))


def last_ff_body(a0, a1, a2, w_out, c0, c1, c2, c3, scr):
    rows = c0.shape[0]
    width = c0.shape[1]
    t = total_of((a0, a1, a2))
    w_out[...] = t[:, width:]
    scr[...] = t[:, :width]
    for k, c in enumerate((c0, c1, c2, c3)):
        c[...] = scr[block(scr, jnp.bitwise_xor(ff_rank(), k), rows)].astype(bf16)


def spread_ff_body(c0, c1, c2, c3, out, scr):
    part = out.shape[1] // (8 * RANKS)
    for k, c in enumerate((c0, c1, c2, c3)):
        scr[jnp.bitwise_xor(ff_rank(), k)] = c[...].astype(f32)
    for t in range(RANKS):
        for j in range(8):
            at = ff_column(t, j, part)
            out[:, at : at + part] = scr[t, :, part * j : part * j + part]


def last_body(a0, a1, a2, c0, c1, c2, c3, scr):
    rows = c0.shape[0]
    scr[...] = total_of((a0, a1, a2))
    for k, c in enumerate((c0, c1, c2, c3)):
        c[...] = scr[block(scr, partner(k), rows)].astype(bf16)


def finish_body(c0, c1, c2, c3, gq, gkv, go, gg, gb, scr):
    wide = go.shape[1] // RANKS
    for k, c in enumerate((c0, c1, c2, c3)):
        scr[partner(k)] = c[...].astype(f32)
    for t in range(RANKS):
        cut = slice(wide * t, wide * t + wide)
        for j, (out, i) in enumerate(((gq, 0), (gq, 1), (gkv, 0), (gkv, 1), (gq, 2), (gq, 3))):
            out[i, :, cut] = scr[t, :, wide * j : wide * j + wide]
        go[:, cut] = scr[t, :, 6 * wide : 7 * wide]
    at = 7 * wide + 64 - 128
    v = c0[:, at:].astype(f32).T
    gg[...] = v[64:66]
    gb[...] = v[66:68]


def input_body(dqkv, wq, du1, ye, own, across, core, part):
    b = lax.axis_index("blk")
    local, share = own.shape[0], ye.shape[0]
    words = RANKS * local
    half = dqkv.shape[1] // 2
    part[:words] = dot_nt(dqkv[:words], wq[:, : 2 * half])
    part[words:] = dot_nt(dqkv[words:, half:], wq[:, half : 2 * half]) + dot_nt(
        dqkv[words:, :half], wq[:, 2 * half :]
    )
    part[pl.ds(pl.multiple_of(words + b * share, share), share)] += du1[local:]
    own[...] = part[block(part, b, local)] + du1[:local]
    low = part[words:].astype(bf16)
    core[:local] = part[block(part, partner(3), local)].astype(bf16)
    core[local : 2 * local] = part[block(part, partner(1), local)].astype(bf16)
    core[2 * local : -share] = low
    core[-share:] = ye[...]
    across[:local] = part[block(part, partner(2), local)].astype(bf16)
    across[local:-share] = low
    across[-share:] = ye[...]


def input_pair_body(across, came, sent):
    share = sent.shape[0] - across.shape[0]
    local = came.shape[0] - across.shape[0]
    sent[:local] = (across[:local].astype(f32) + came[:local].astype(f32)).astype(bf16)
    pair = across[local:-share].astype(f32) + came[2 * local : -share].astype(f32)
    sent[local : -2 * share] = pair.astype(bf16)
    sent[-2 * share : -share] = across[-share:]
    sent[-share:] = came[-share:]


def input_sum_body(own, core, sent, came, gw, ge, ye):
    local = own.shape[0]
    share = ye.shape[0] // RANKS
    two = 2 * share
    gw[...] = own[...] + core[local : 2 * local].astype(f32) + came[:local].astype(f32)
    ge[...] = sent[local:-two].astype(f32) + came[local:-two].astype(f32)
    for k, rows in enumerate((sent[-two:-share], sent[-share:], came[-two:-share], came[-share:])):
        ye[block(ye, partner(k), share)] = rows


def swap(x, k):
    return lax.ppermute(x, "blk", [(i, i ^ k) for i in range(RANKS)])


def swapped(send):
    return [swap(send[k - 1], k) for k in (1, 2, 3)]


def spread(x):
    across = swap(x, 2)
    beside = swap(x, 1)
    return [beside, across, swap(across, 1)]


def plus(*parts):
    total = parts[0].astype(f32)
    for part in parts[1:]:
        total = total + part.astype(f32)
    return total.astype(bf16)


def over_x(x):
    return lax.ppermute(x, "seq", [(i, i ^ 1) for i in range(8)])


ring = (0, 1, 3, 2)


def swap_ff(x, k, direct):
    if not direct or k == 1:
        return swap(x, k)
    if k == 2:
        return over_x(x)
    return lax.ppermute(x, ("seq", "blk"), [(i, i ^ 5) for i in range(32)])


def along_ring(x, step=1):
    route = [(ring[i], ring[(i + step) % 4]) for i in range(4)]
    return lax.ppermute(x, "seq", [(2 * z + i, 2 * to + i) for z, to in route for i in (0, 1)])


def fence(*groups):
    return lax.optimization_barrier(groups)


def after(x, *before):
    return lax.optimization_barrier((x, before))[0]


def per_device(
    words,
    entities,
    segments,
    entity_counts,
    entity_anchor,
    query_weights,
    kv_weights,
    out_weight,
    ff_in,
    ff_out,
    norm_gain,
    norm_bias,
    grad_words,
    grad_entities,
):
    seqs = lax.axis_size("seq")
    direct = seqs == 8
    _, local, width = words.shape
    ents = entities.shape[1]
    share = ents // RANKS
    total = local * RANKS
    rows = total + ents
    mine = local + share
    wide = width // RANKS
    hl = HEADS // RANKS
    factor = (width // HEADS) ** (-0.5)
    part_rows = query_weights.shape[2]
    ff_part = ff_out.shape[1]
    ff = ff_part * seqs
    shards = 8 if direct else 1
    slab_cols = 7 * wide + 64
    xw_own, xe = words[0], entities[0]

    seg_ents = jnp.take_along_axis(segments, entity_anchor, axis=1)
    live = jnp.arange(ents, dtype=jnp.int32)[None, :] < entity_counts[:, None]
    segq = jnp.concatenate([segments, seg_ents], 1)
    segk = jnp.concatenate([segments, jnp.where(live, seg_ents, -1)], 1).T
    join_rows = call(join_rows_body, "join_rows", [((total, width), bf16)])

    if direct:
        pack = call(
            pack_body,
            "pack",
            [((part_rows, slab_cols), bf16)] * 4 + [((part_rows, ff), bf16)] * 4,
            [pltpu.VMEM((RANKS, part_rows, n), bf16) for n in (slab_cols, ff)]
            + [pltpu.VMEM((n, part_rows, width), bf16) for n in (4, 2)]
            + [pltpu.VMEM((part_rows, width), bf16)]
            + [pltpu.VMEM((2, part_rows), bf16)] * 2
            + [pltpu.VMEM((part_rows, RANKS * ff), bf16), pltpu.SemaphoreType.DMA((6,))],
            held=6,
            vmem=60,
        )
        pieces = pack(
            query_weights[0],
            kv_weights[0],
            out_weight[0],
            norm_gain[0],
            norm_bias[0],
            ff_in[0],
        )
        pieces, ff_pieces = pieces[:4], pieces[4:]
        own = call(
            arrange_own_body, "arrange_own", [((RANKS * part_rows, slab_cols), f32)]
        )(pieces[0])
        pieces = [own[0], *swapped(pieces[1:])]

        arrange = call(
            arrange_body,
            "arrange",
            [((RANKS * part_rows, slab_cols), bf16)],
            [pltpu.VMEM((RANKS * part_rows, slab_cols), f32)],
        )
        arrange_ff = call(
            arrange_ff_body,
            "arrange_ff",
            [((RANKS * part_rows, ff + width), bf16)],
            [pltpu.VMEM((RANKS * part_rows, ff), f32)],
        )
        (slab,) = arrange(*pieces)
        xw_own, slab = fence(xw_own, slab)
        xb, xa = swap(xw_own, 1), swap(xw_own, 2)
        x0, g1 = over_x(slab), along_ring(slab)
        g1, x0, xb, ff_pieces = fence(g1, x0, xb, ff_pieces)
        x1, g2 = over_x(g1), along_ring(g1)
        came = [swap_ff(ff_pieces[k], k, direct) for k in (1, 2, 3)]
        (ff_slab,) = arrange_ff(ff_pieces[0], *came, ff_out[0])
        g2, x1, ff_slab, xa = fence(g2, x1, ff_slab, xa)
        x2, g3 = over_x(g2), along_ring(g2)
        y0, xc = swap(ff_slab, 2), swap(xa, 1)
        g3, x2, xc, segq, segk = fence(g3, x2, xc, segq, segk)
        f1, x3 = along_ring(after(ff_slab, g3)), over_x(g3)
        (xw,) = join_rows(xw_own, xb, xa, xc)
        x3, f1, y0, xw = fence(x3, f1, y0, xw)
        f2 = along_ring(f1)
        slabs = [slab, x0, g1, x1, g2, x2, g3, x3]
    else:
        vec = jnp.concatenate([norm_gain[0], norm_bias[0]], 0).T
        vec = jnp.pad(vec, ((0, 0), (0, 60)))
        six = jnp.concatenate(
            [query_weights[0, :2], kv_weights[0], query_weights[0, 2:], out_weight], 0
        )
        six = six.reshape(7, part_rows, RANKS, wide).transpose(2, 1, 0, 3)
        six = six.reshape(RANKS, part_rows, 7 * wide)
        ff_cols = ff_in[0].reshape(part_rows, seqs, RANKS, ff_part).transpose(2, 0, 1, 3)
        ff_cols = ff_cols.reshape(RANKS, part_rows, ff)
        pack = jnp.concatenate(
            [six, jnp.broadcast_to(vec, (RANKS, part_rows, 64)), ff_cols], 2
        )
        pack = lax.all_to_all(pack, "blk", 0, 0, tiled=True).reshape(RANKS * part_rows, -1)
        pack = jnp.concatenate([pack, ff_out[0]], 1)
        pack = lax.all_gather(pack, "seq", axis=0, tiled=True)
        slabs, ff_slabs = [pack[:, :slab_cols]], [pack[:, slab_cols:]]
        (xw,) = join_rows(xw_own, *spread(xw_own))

    def place(slots, last, *args):
        outs = [((width, 6 * wide), bf16), ((width, 128), bf16), ((width, wide - 64), bf16)]
        if last:
            outs += [((width * 3 // 2, 128), bf16), ((8, width), f32)]
        body = place_last_body if last else place_body
        same = len(args) - len(slots)
        name = "place_last" if last else "place"
        return call(lambda *r: body(slots, *r), name, outs, same=same)(*args)

    if direct:
        ready = place((0, 1, 2, 3, 4), False, *slabs[:5])
        wq, _, _, wo_col, norms = place((5, 6, 7), True, *ready, *slabs[5:])
    else:
        blank = [jnp.zeros((width, n), bf16) for n in (6 * wide, 128, wide - 64)]
        wq, _, _, wo_col, norms = place((0,), True, *blank, slabs[0])
    wa, wb = swap(wo_col, 2), swap(wo_col, 1)
    attend = call(
        lambda *r: attend_body(wide, factor, *r),
        "attend",
        [((mine, wide), bf16)] * 4
        + [((rows, wide), bf16)] * 4
        + [((rows // 128, rows, 128 * hl), bf16)],
        [pltpu.VMEM((rows, wide), bf16)],
        us=7,
        vmem=16,
    )
    *ctx, qw, qe, kk, vv, prob = attend(xw, xe, wq, segq, segk)
    if direct:
        ctx = after(ctx, wb)
    ctx = [ctx[0]] + swapped(ctx[1:])
    wos = [wo_col, wb, wa, swap(after(wa, ctx), 1)]
    if direct:
        f3, y1 = along_ring(f2), swap(after(f1, ctx), 2)
        wos = after(wos, f3)
    join_out = call(
        join_out_body,
        "join_out",
        [((width, width), bf16)],
        [pltpu.VMEM((RANKS, width * 3 // 2, 128), bf16)],
    )
    (wo,) = join_out(*wos)
    mix = call(
        mix_body,
        "mix",
        [((mine, width), bf16), ((mine, width), f32), ((mine, 1), f32)],
        [pltpu.VMEM((mine, width), f32)],
    )
    hr, n1, i1 = mix(*ctx, *wos, norms, xw_own, xe)
    across, beside = swap_ff(hr, 2, direct), swap(hr, 1)
    if direct:
        fb, y2 = along_ring(after(y0, hr), -1), swap(after(f2, hr), 2)
        across = after(across, y1)
        ff_slabs = [ff_slab, y0, f1, y1, f2, y2, f3, fb]
    hs = [hr, beside, across, swap(across, 1)]
    def place_ff(slots, *args):
        outs = [((width, ff), bf16), ((ff, width), bf16)]
        same = len(args) - len(slots)
        return call(lambda *r: place_ff_body(slots, *r), "place_ff", outs, same=same)(*args)

    if direct:
        early = (0, 1, 2, 3, 4)
        ready = place_ff(early, *(ff_slabs[j] for j in early))
        w1, w2 = place_ff((5, 6, 7), *ready, *ff_slabs[5:])
    else:
        w1, w2 = place_ff((0,), ff_slabs[0])
    feed = call(
        feed_body,
        "feed",
        [((mine, width), f32), ((mine, width), bf16), ((2, mine, width), bf16)]
        + [((RANKS, mine, ff), bf16)] * 2,
        us=3,
        vmem=14,
    )
    own, across, core, g_all, gp_all = feed(*hs, w1, w2)
    core = swap(core, 1)
    fs = [own, core, swap_ff(plus(across, core[0]), 2, direct)]
    turn = call(
        turn_body,
        "turn",
        [((local, width), bf16), ((share, width), bf16), ((mine, width), bf16)]
        + [((mine, width), f32), ((8, width), f32)],
    )
    yw, ye, df, du2, sums = turn(*fs, n1, norms, grad_words[0], grad_entities[0])

    across, beside = swap_ff(df, 2, direct), swap(df, 1)
    ds = [df, beside, across, swap(across, 1)]
    half_dz = ((2, mine, ff), bf16)
    feed_back_near = call(
        feed_back_near_body,
        "feed_back_near",
        [((mine, width), f32), ((mine, width), bf16), half_dz],
        vmem=12,
    )
    feed_back_far = call(
        feed_back_far_body,
        "feed_back_far",
        [((mine, width), bf16), ((2, mine, width), bf16), half_dz],
        vmem=12,
    )
    own, beside, dz_near = feed_back_near(*ds[:2], gp_all, w1, w2)
    across, core, dz_far = feed_back_far(*ds[2:], gp_all, w1, w2, beside)
    core = swap(core, 1)
    feed_grads = call(
        feed_grads_body,
        "feed_grads",
        [((width // shards, ff + width), bf16)] * shards,
        [pltpu.VMEM((width, ff), bf16), pltpu.VMEM((ff, width), bf16)],
        us=3,
        vmem=16,
    )
    ff_chunks = feed_grads(*ds, *hs, g_all, dz_near, dz_far)
    sent = plus(across, after(core, ff_chunks)[0])
    dhs = [own, core, swap_ff(sent, 2, direct)]
    if direct:
        fz, fy = along_ring(ff_chunks[2], -1), swap(ff_chunks[5], 2)
        dhs[2] = after(dhs[2], fz, fy)
        fz = along_ring(plus(ff_chunks[4], fz, fy), -1)

    norm_one = call(
        norm_one_body,
        "norm_one",
        [((mine, wide), bf16)] * 3
        + [((2 * width + mine, wide + 64), bf16), ((mine, width), f32)]
        + [((width, wide + 64), bf16)] * 2,
        [pltpu.VMEM((RANKS, width, wide + 64), bf16)],
        vmem=12,
    )
    d0, d2, d3, core, du1, wo_own, across = norm_one(
        *dhs, du2, n1, i1, norms, sums, wo, *ctx
    )
    dcs = [d0, swap(core, 1), swap(d2, 2), swap(d3, 3)]
    sent = plus(across, after(dcs[1], dcs[2], dcs[3])[:width])
    outs = [wo_own, dcs[1], swap(sent, 2)]
    if direct:
        fb = along_ring(after(ff_chunks[3], du1))
    dcs = after(dcs, sent)
    attend_back = call(
        lambda *r: attend_back_body(factor, *r),
        "attend_back",
        [((rows, 4 * wide), bf16)],
        [pltpu.VMEM((rows, wide), bf16)] + [pltpu.VMEM((rows, wide), f32)] * 4,
        us=7,
        vmem=16,
    )
    (dqkv,) = attend_back(*dcs, qw, qe, kk, vv, prob)
    to_input = call(
        input_body,
        "to_input",
        [((local, width), f32)]
        + [((n * local + ents + share, width), bf16) for n in (1, 2)],
        [pltpu.VMEM((rows, width), f32)],
        us=2,
        vmem=12,
    )
    own, across, core = to_input(dqkv, wq, du1, ye)
    if direct:
        own = after(own, fb)
        fz = along_ring(plus(ff_chunks[6], after(fz, dqkv)), -1)
        fc = along_ring(after(ff_chunks[7], dqkv), -1)
    core = swap(core, 1)
    proj_grads = call(
        proj_grads_body,
        "proj_grads",
        [((width // shards, slab_cols), bf16)] * shards,
        [pltpu.VMEM((width, slab_cols), bf16)],
        us=2,
        vmem=14,
    )
    chunks = proj_grads(after(dqkv, own), xw, xe, *outs)
    if direct:
        part = plus(chunks[2], after(over_x(chunks[3]), fz, fc))
        fy = swap(plus(ff_chunks[1], fb, after(fc, part)), 2)
        cx, cz = over_x(after(chunks[5], part)), along_ring(part, -1)
        core = after(core, part)
    (sent,) = call(input_pair_body, "input_pair", [((local + ents + 2 * share, width), bf16)])(across, core)
    came = swap(sent, 2)
    input_sum = call(
        input_sum_body,
        "input_sum",
        [((local, width), f32), ((ents, width), f32), ((ents, width), bf16)],
    )
    if not direct:
        gxw, gxe, ye = input_sum(own, core, sent, came)

    if direct:
        last_ff = call(
            last_ff_body,
            "last_ff",
            [((ff_part, width), f32)] + [((part_rows, ff), bf16)] * 4,
            [pltpu.VMEM((RANKS * part_rows, ff), f32)],
        )
        part = plus(chunks[4], cz, cx)
        cx, cz = over_x(after(chunks[7], part)), along_ring(part, -1)
        grad_ff_out, *back = last_ff(ff_chunks[0], after(fz, part), fy)
        part = plus(chunks[6], after(cz, came), cx)
        cx, cz = over_x(after(chunks[1], part)), along_ring(part, -1)
        back = [back[0]] + [swap_ff(back[k], k, direct) for k in (1, 2, 3)]
        spread_ff = call(
            spread_ff_body,
            "spread_ff",
            [((part_rows, RANKS * ff), f32)],
            [pltpu.VMEM((RANKS, part_rows, ff), f32)],
        )
        (grad_ff_in,) = spread_ff(*back)
        gxw, gxe, ye = input_sum(own, core, sent, after(came, part))
        last = call(
            last_body,
            "last",
            [((part_rows, slab_cols), bf16)] * 4,
            [pltpu.VMEM((RANKS * part_rows, slab_cols), f32)],
        )
        back = last(chunks[0], after(cz, grad_ff_in, gxw), cx)
        back = [back[0]] + swapped(back[1:])
        finish = call(
            finish_body,
            "finish",
            [((4, part_rows, width), f32), ((2, part_rows, width), f32), ((part_rows, width), f32)]
            + [((2, part_rows), f32)] * 2,
            [pltpu.VMEM((RANKS, part_rows, slab_cols), f32)],
        )
        grad_query, grad_kv, grad_out, grad_gain, grad_bias = finish(*back)
    else:
        both = jnp.concatenate([chunks[0], ff_chunks[0]], 1)
        both = lax.psum_scatter(both, "seq", scatter_dimension=0, tiled=True)
        grad_ff_out = both[:, slab_cols + ff :].astype(f32)
        both = both[:, : slab_cols + ff].reshape(RANKS, part_rows, slab_cols + ff)
        both = lax.all_to_all(both, "blk", 0, 0, tiled=True).astype(f32)
        seven = both[:, :, : 7 * wide].reshape(RANKS, part_rows, 7, wide)
        seven = seven.transpose(2, 1, 0, 3).reshape(7, part_rows, width)
        grad_query = jnp.concatenate([seven[:2], seven[4:6]], 0)
        grad_kv, grad_out = seven[2:4], seven[6]
        vecs = both[0, :, 7 * wide : 7 * wide + 4].T
        grad_gain, grad_bias = vecs[:2], vecs[2:]
        grad_ff_in = both[:, :, slab_cols:].reshape(RANKS, part_rows, seqs, ff_part)
        grad_ff_in = grad_ff_in.transpose(1, 2, 0, 3).reshape(part_rows, RANKS * ff)
    return (
        yw[None],
        ye[None],
        gxw[None],
        gxe[None],
        grad_query[None],
        grad_kv[None],
        grad_out[None],
        grad_ff_in[None],
        grad_ff_out[None],
        grad_gain[None],
        grad_bias[None],
    )


def solution(mesh):
    placed = (
        P("seq", "blk", None),
        P("seq", None, None),
        P("seq", None),
        P("seq"),
        P("seq", None),
        P(None, None, ("seq", "blk"), None),
        P(None, None, ("seq", "blk"), None),
        P(None, ("seq", "blk"), None),
        P(None, ("seq", "blk"), None),
        P(None, ("seq", "blk"), None),
        P(None, None, ("seq", "blk")),
        P(None, None, ("seq", "blk")),
        P("seq", "blk", None),
        P("seq", None, None),
    )
    return jax.shard_map(
        per_device,
        mesh=mesh,
        in_specs=placed,
        out_specs=(
            P("seq", "blk", None),
            P("seq", None, None),
            P("seq", "blk", None),
            P("seq", None, None),
            P(None, None, ("seq", "blk"), None),
            P(None, None, ("seq", "blk"), None),
            P(None, ("seq", "blk"), None),
            P(None, ("seq", "blk"), None),
            P(None, ("seq", "blk"), None),
            P(None, None, ("seq", "blk")),
            P(None, None, ("seq", "blk")),
        ),
        check_vma=False,
    )
```

time: 1120 us -> 191 us (0.17); the launches traced: 1110 us -> 190 us
  waiting for transfers between devices: 724 us -> 81.9 us
  blocking collectives: 143 us -> 0 us
  matrix products: 112 us -> 0 us
  local copies, waits for them, and re-layouts: 67.1 us -> 7.21 us
  starting transfers between devices: 2.29 us -> 61.6 us
  other arithmetic: 40.9 us -> 0.88 us
  Pallas kernels: 0 us -> 37 us
  between operations: 17.4 us -> 1.83 us
    reduce_scatter x3 -> x0, waiting for transfers between devices: 385 us -> none  [the longest x1 142 us: per_device(): lax.psum_scatter(sum_in, ('seq', 'blk'), scatter_dimension=0, tiled=True)]
    unnamed x11 -> x0, waiting for transfers between devices: 179 us -> none
    dot_general x75 -> x0, matrix products: 112 us -> none  [the longest x11 40.9 us: forward_product(): return jnp.dot(operand, matrix, preferred_element_type=jnp.float32)]
    all_gather x5 -> x0, waiting for transfers between devices: 111 us -> none  [the longest x1 61.2 us: per_device(): lax.all_gather(ff_in[layer_index], ('seq', 'blk'), axis=0, tiled=True)]
    all_gather x5 -> x0, blocking collectives: 102 us -> none  [the longest x1 44.6 us: per_device(): lax.all_gather(norm_bias[layer_index], ('seq', 'blk'), axis=1, tiled=True)]
    ppermute x7 -> x65, waiting for transfers between devices: 20.9 us -> 81.9 us  [the longest x14 41.9 us: over_x(): return lax.ppermute(x, 'seq', [(i, i ^ 1) for i in range(8)])]
    ppermute x7 -> x65, starting transfers between devices: 1.9 us -> 61.6 us  [the longest x15 23.2 us: along_ring(): lax.ppermute(x, 'seq', [(2 * z + i, 2 * to + i) for z, to in route for i...]
    unnamed x1 -> x0, blocking collectives: 40.9 us -> none
  transfers between devices with their start and end apart: 17 -> 65, of which waited for: 13 -> 34; matrix products, arithmetic and copies ran while one was open for 13% -> 1% of each run, Pallas kernels for 0% -> 14%
where the time goes in v1:
time: 191 us; the launch traced here: 190 us
  waiting for transfers between devices  81.9 us (43%)
  starting transfers between devices  61.6 us (32%)
  Pallas kernels  37 us (19%)
  local copies, waits for them, and re-layouts  7.21 us (4%)
    ppermute x14, waiting for transfers between devices, over_x(): return lax.ppermute(x, 'seq', [(i, i ^ 1) for i in range(8)])  41.9 us
    pallas_call x27, Pallas kernels, run(): pl.pallas_call(body, name=name, out_shape=[jax.ShapeDtypeStruct(s, t) for...  37 us
    ppermute x15, starting transfers between devices, along_ring(): lax.ppermute(x, 'seq', [(2 * z + i, 2 * to + i) for z, to in route for i...  23.2 us
    ppermute x34, starting transfers between devices, swap(): return lax.ppermute(x, 'blk', [(i, i ^ k) for i in range(RANKS)])  21.6 us
    ppermute x15, waiting for transfers between devices, along_ring(): lax.ppermute(x, 'seq', [(2 * z + i, 2 * to + i) for z, to in route for i...  21.4 us
    ppermute x34, waiting for transfers between devices, swap(): return lax.ppermute(x, 'blk', [(i, i ^ k) for i in range(RANKS)])  18.6 us
    ppermute x14, starting transfers between devices, over_x(): return lax.ppermute(x, 'seq', [(i, i ^ 1) for i in range(8)])  15 us
    unnamed x46, local copies, waits for them, and re-layouts  5.77 us
  transfers between devices with their start and end apart: 65, of which 34 were waited for; matrix products, arithmetic and copies ran while one was open for 1% of the time, Pallas kernels for 14%

profile of v1, /device:TPU:0, one launch (start us, length us, event | category | flops | bytes accessed | tf_op | source)
XLA Modules:
  0.0 190.4 jit_solution(964269866155461363)
XLA Ops:
  0.7 2.4 %pack.1 = (bf16[24,1408]{1,0:T(8,128)(2,1)}, bf16[24,1408]{1,0:T(8,128)(2,1)}, bf16[24,1408]{1,0:T(8,128)(2,1)}, bf16[24,1408]{1,0:T(8,128)(2,1)}, bf16[24,768]{...) custom-call(bf16[4,24,768]{2,1,0:T(8,128)(2,1)} %bitcast.52, ...), custom_call_target="tpu_custom_call" | custom-call | flops 1000000 | bytes 1000 | tf_op jit(solution)/shard_map/pack/pallas_call | solution.py:34
  3.6 2.6 %collective-permute-start.1 = (bf16[24,1408]{1,0:T(8,128)(2,1)}, bf16[24,1408]{1,0:T(8,128)(2,1)S(1)}, u32[]{:S(2)}, u32[]{:S(2)}) collective-permute-start(bf16[24,1408]{1,0:T(8,128)(2,1)} %get-tuple-element.160), channel_id=1, source_target_pairs={{0,2},{1,3},{2,0},{3,1},{4,6},{5,7},{6,4},{7,5},{8,10},{9,11},{10,... | collective-permute-start | bytes 202760 | tf_op jit(solution)/shard_map/ppermute | solution.py:550
  15.2 4.0 %collective-permute-done.4.r_1_ = bf16[96,1408]{1,0:T(8,128)(2,1)S(1)} collective-permute-done((bf16[96,1408]{1,0:T(8,128)(2,1)S(1)}, bf16[96,1408]{1,0:T(8,128)(2,1)S(1)}, u32[]{:S(2)}, u32[]{:S(2)}) %collective-permute-start.4) | collective-permute-done | bytes 270368 | tf_op jit(solution)/shard_map/ppermute | solution.py:571
  27.1 2.8 %collective-permute-done.9.p2 = bf16[24,768]{1,0:T(8,128)(2,1)S(1)} collective-permute-done((bf16[24,768]{1,0:T(8,128)(2,1)S(1)}, bf16[24,768]{1,0:T(8,128)(2,1)S(1)}, u32[]{:S(2)}, u32[]{:S(2)}) %collective-permute-start.9) | collective-permute-done | bytes 36896 | tf_op jit(solution)/shard_map/ppermute | solution.py:571
  36.0 3.4 %collective-permute-done.13.r_3_ = bf16[96,1408]{1,0:T(8,128)(2,1)S(1)} collective-permute-done((bf16[96,1408]{1,0:T(8,128)(2,1)S(1)}, bf16[96,1408]{1,0:T(8,128)(2,1)S(1)}, u32[]{:S(2)}, u32[]{:S(2)}) %collective-permute-start.13) | collective-permute-done | bytes 270368 | tf_op jit(solution)/shard_map/ppermute | solution.py:571
  45.7 3.3 %collective-permute-done.15.r_5_ = bf16[96,1408]{1,0:T(8,128)(2,1)S(1)} collective-permute-done((bf16[96,1408]{1,0:T(8,128)(2,1)S(1)}, bf16[96,1408]{1,0:T(8,128)(2,1)S(1)}, u32[]{:S(2)}, u32[]{:S(2)}) %collective-permute-start.15) | collective-permute-done | bytes 270368 | tf_op jit(solution)/shard_map/ppermute | solution.py:571
  50.4 2.4 %collective-permute-start.24 = (bf16[96,1536]{1,0:T(8,128)(2,1)}, bf16[96,1536]{1,0:T(8,128)(2,1)}, u32[]{:S(2)}, u32[]{:S(2)}) collective-permute-start(bf16[96,1536]{1,0:T(8,128)(2,1)} %collective-permute-done.16.r_2_), channel_id=1, source_target_pairs={{0,8},{4,12},{8,24},{12,28},{24,16},{28,20},{16,0},{20,4},{1,9},{5... | collective-permute-start | bytes 884744 | tf_op jit(solution)/shard_map/ppermute | solution.py:587
  54.6 5.8 %attend.1 = (bf16[160,192]{1,0:T(8,128)(2,1)S(1)}, bf16[160,192]{1,0:T(8,128)(2,1)S(1)}, bf16[160,192]{1,0:T(8,128)(2,1)S(1)}, bf16[160,192]{1,0:T(8,128)(2,1)S(...) custom-call(bf16[512,768]{1,0:T(8,128)(2,1)S(1)} %join_rows.1.r_0_.x, ...), custom_call_target="tpu_custom_call" | custom-call | flops 7000000 | bytes 7000 | tf_op jit(solution)/shard_map/attend/pallas_call | solution.py:34
  67.7 5.1 %collective-permute-done.25.r_3_ = bf16[96,1536]{1,0:T(8,128)(2,1)S(1)} collective-permute-done((bf16[96,1536]{1,0:T(8,128)(2,1)}, bf16[96,1536]{1,0:T(8,128)(2,1)S(1)}, u32[]{:S(2)}, u32[]{:S(2)}) %collective-permute-start.25) | collective-permute-done | bytes 294944 | tf_op jit(solution)/shard_map/ppermute | solution.py:587
  72.8 2.1 %mix.1 = (bf16[160,768]{1,0:T(8,128)(2,1)S(1)}, f32[160,768]{1,0:T(8,128)S(1)}, f32[160,1]{1,0:T(8,128)S(1)}) custom-call(bf16[160,192]{1,0:T(8,128)(2,1)S(1)} %get-tuple-element.196.c0, bf16[160,192]{1,0:T(8,128)(2,1)S(1)} %collective-permute-done.19.c1, bf16[160,192]{1,0:T(8,128)(2,1)S(1)} %collective-permute-done.20.c2, ...), custom_call_target="tpu_custom_call" | custom-call | flops 1000000 | bytes 1000 | tf_op jit(solution)/shard_map/mix/pallas_call | solution.py:34
  77.0 5.5 %collective-permute-done.27.h2 = bf16[160,768]{1,0:T(8,128)(2,1)S(1)} collective-permute-done((bf16[160,768]{1,0:T(8,128)(2,1)S(1)}, bf16[160,768]{1,0:T(8,128)(2,1)S(1)}, u32[]{:S(2)}, u32[]{:S(2)}) %collective-permute-start.27) | collective-permute-done | bytes 245792 | tf_op jit(solution)/shard_map/ppermute | solution.py:571
  84.5 2.3 %feed.1 = (f32[160,768]{1,0:T(8,128)S(1)}, bf16[160,768]{1,0:T(8,128)(2,1)S(1)}, bf16[2,160,768]{2,1,0:T(8,128)(2,1)S(1)}, bf16[4,160,768]{2,1,0:T(8,128)(2,1)S(1)}, bf16[4,160,768]{2,1,0:T(8,128)(2,1)S(1)}) custom-call(bf16[160,768]{1,0:T(8,128)(2,1)S(1)} %get-tuple-element.207.h0, bf16[160,768]{1,0:T(8,128)(2,1)S(1)} %collective-permute-done.26.h1, ...), custom_call_target="tpu_custom_call" | custom-call | flops 3000000 | bytes 3000 | tf_op jit(solution)/shard_map/feed/pallas_call | solution.py:34
  90.0 6.9 %collective-permute-done.33.f2 = bf16[160,768]{1,0:T(8,128)(2,1)S(1)} collective-permute-done((bf16[160,768]{1,0:T(8,128)(2,1)S(1)}, bf16[160,768]{1,0:T(8,128)(2,1)S(1)}, u32[]{:S(2)}, u32[]{:S(2)}) %collective-permute-start.33) | collective-permute-done | bytes 245792 | tf_op jit(solution)/shard_map/ppermute | solution.py:571
  99.1 6.1 %collective-permute-done.35.d2 = bf16[160,768]{1,0:T(8,128)(2,1)S(1)} collective-permute-done((bf16[160,768]{1,0:T(8,128)(2,1)S(1)}, bf16[160,768]{1,0:T(8,128)(2,1)S(1)}, u32[]{:S(2)}, u32[]{:S(2)}) %collective-permute-start.35) | collective-permute-done | bytes 245792 | tf_op jit(solution)/shard_map/ppermute | solution.py:571
  108.9 2.1 %feed_grads.1 = (bf16[96,1536]{1,0:T(8,128)(2,1)S(1)}, bf16[96,1536]{1,0:T(8,128)(2,1)S(1)}, bf16[96,1536]{1,0:T(8,128)(2,1)S(1)}, bf16[96,1536]{1,0:T(8,128)(2,...) custom-call(bf16[160,768]{1,0:T(8,128)(2,1)S(1)} %get-tuple-element., ...), custom_call_target="tpu_custom_call" | custom-call | flops 3000000 | bytes 3000 | tf_op jit(solution)/shard_map/feed_grads/pallas_call | solution.py:34
  116.7 3.3 %collective-permute-done.39 = bf16[96,1536]{1,0:T(8,128)(2,1)S(1)} collective-permute-done((bf16[96,1536]{1,0:T(8,128)(2,1)S(1)}, bf16[96,1536]{1,0:T(8,128)(2,1)S(1)}, u32[]{:S(2)}, u32[]{:S(2)}) %collective-permute-start.39) | collective-permute-done | bytes 294944 | tf_op jit(solution)/shard_map/ppermute | solution.py:587
  130.4 6.1 %attend_back.1.dqkv = bf16[640,768]{1,0:T(8,128)(2,1)S(1)} custom-call(bf16[160,192]{1,0:T(8,128)(2,1)S(1)} %get-tuple-element.250.r_0_, bf16[1696,256]{1,0:T(8,128)(2,1)S(1)} %collective-permute-done.41.r_1_.o1, bf16[160,192]{1,0:T(8,128)(2,1)S(1)} %collective-permute-done.42.r_2_, bf16[160,192]{1,0:T(8,128)(2,1)S(1)} %collective-permute-done.43.r_3_, ...), custom_call_target="tpu_custom_call" | custom-call | flops 7000000 | bytes 7000 | tf_op jit(solution)/shard_map/attend_back/pallas_call | solution.py:34
  136.6 4.6 %collective-permute-start.49 = (bf16[96,1536]{1,0:T(8,128)(2,1)S(1)}, bf16[96,1536]{1,0:T(8,128)(2,1)S(1)}, u32[]{:S(2)}, u32[]{:S(2)}) collective-permute-start(bf16[96,1536]{1,0:T(8,128)(2,1)S(1)} %add_convert_fusion.2), channel_id=1, source_target_pairs={{0,16},{4,20},{8,0},{12,4},{24,8},{28,12},{16,24},{20,28},{1,17},{... | collective-permute-start | bytes 884744 | tf_op jit(solution)/shard_map/ppermute | solution.py:587
  141.2 2.9 %collective-permute-start.50 = (bf16[96,1536]{1,0:T(8,128)(2,1)S(1)}, bf16[96,1536]{1,0:T(8,128)(2,1)S(1)}, u32[]{:S(2)}, u32[]{:S(2)}) collective-permute-start(bf16[96,1536]{1,0:T(8,128)(2,1)S(1)} %get-tuple-element.270), channel_id=1, source_target_pairs={{0,16},{4,20},{8,0},{12,4},{24,8},{28,12},{16,24},{20,28},{1,17},{... | collective-permute-start | bytes 884744 | tf_op jit(solution)/shard_map/ppermute | solution.py:587
  148.4 6.3 %collective-permute-done.50 = bf16[96,1536]{1,0:T(8,128)(2,1)S(1)} collective-permute-done((bf16[96,1536]{1,0:T(8,128)(2,1)S(1)}, bf16[96,1536]{1,0:T(8,128)(2,1)S(1)}, u32[]{:S(2)}, u32[]{:S(2)}) %collective-permute-start.50) | collective-permute-done | bytes 294944 | tf_op jit(solution)/shard_map/ppermute | solution.py:587
  157.9 5.3 %collective-permute-done.53 = bf16[96,1408]{1,0:T(8,128)(2,1)S(1)} collective-permute-done((bf16[96,1408]{1,0:T(8,128)(2,1)S(1)}, bf16[96,1408]{1,0:T(8,128)(2,1)S(1)}, u32[]{:S(2)}, u32[]{:S(2)}) %collective-permute-start.53) | collective-permute-done | bytes 270368 | tf_op jit(solution)/shard_map/ppermute | solution.py:571
  168.0 2.4 %collective-permute-done.51.came = bf16[320,768]{1,0:T(8,128)(2,1)S(1)} collective-permute-done((bf16[320,768]{1,0:T(8,128)(2,1)S(1)}, bf16[320,768]{1,0:T(8,128)(2,1)S(1)}, u32[]{:S(2)}, u32[]{:S(2)}) %collective-permute-start.51) | collective-permute-done | bytes 491552 | tf_op jit(solution)/shard_map/ppermute | solution.py:550
  178.0 3.4 %collective-permute-done.59.c2 = bf16[24,768]{1,0:T(8,128)(2,1)S(1)} collective-permute-done((bf16[24,768]{1,0:T(8,128)(2,1)S(1)}, bf16[24,768]{1,0:T(8,128)(2,1)S(1)}, u32[]{:S(2)}, u32[]{:S(2)}) %collective-permute-start.59) | collective-permute-done | bytes 36896 | tf_op jit(solution)/shard_map/ppermute | solution.py:571
  185.4 2.7 %collective-permute-done.63.c2 = bf16[24,1408]{1,0:T(8,128)(2,1)S(1)} collective-permute-done((bf16[24,1408]{1,0:T(8,128)(2,1)S(1)}, bf16[24,1408]{1,0:T(8,128)(2,1)S(1)}, u32[]{:S(2)}, u32[]{:S(2)}) %collective-permute-start.63) | collective-permute-done | bytes 67616 | tf_op jit(solution)/shard_map/ppermute | solution.py:550
  (194 shorter events, 94.8 us)
Async XLA Ops:
  12.2 9.1 %collective-permute-start.3 = (bf16[96,1408]{1,0:T(8,128)(2,1)S(1)}, bf16[96,1408]{1,0:T(8,128)(2,1)S(1)}, u32[]{:S(2)}, u32[]{:S(2)}) collective-permute-start(bf16[96,1408]{1,0:T(8,128)(2,1)S(1)} %arrange.1.r_0_), channel_id=1, source_target_pairs={{0,8},{4,12},{8,24},{12,28},{24,16},{28,20},{16,0},{20,4},{1,9},{5... | collective-permute-start | bytes 811016 | tf_op jit(solution)/shard_map/ppermute | solution.py:587
  13.8 16.2 %collective-permute-start.11 = (bf16[128,768]{1,0:T(8,128)(2,1)S(1)}, bf16[128,768]{1,0:T(8,128)(2,1)S(1)}, u32[]{:S(2)}, u32[]{:S(2)}) collective-permute-start(bf16[128,768]{1,0:T(8,128)(2,1)S(1)} %bitcast.44), channel_id=1, source_target_pairs={{0,2},{1,3},{2,0},{3,1},{4,6},{5,7},{6,4},{7,5},{8,10},{9,11},{10,... | collective-permute-start | bytes 589832 | tf_op jit(solution)/shard_map/ppermute | solution.py:550
  21.3 8.6 %collective-permute-start.7 = (bf16[96,1408]{1,0:T(8,128)(2,1)S(1)}, bf16[96,1408]{1,0:T(8,128)(2,1)S(1)}, u32[]{:S(2)}, u32[]{:S(2)}) collective-permute-start(bf16[96,1408]{1,0:T(8,128)(2,1)S(1)} %collective-permute-done.3.r_2_), channel_id=1, source_target_pairs={{0,4},{4,0},{8,12},{12,8},{16,20},{20,16},{24,28},{28,24},{1,5},{5... | collective-permute-start | bytes 811016 | tf_op jit(solution)/shard_map/ppermute | solution.py:571
  21.9 8.9 %collective-permute-start.6 = (bf16[96,1408]{1,0:T(8,128)(2,1)S(1)}, bf16[96,1408]{1,0:T(8,128)(2,1)S(1)}, u32[]{:S(2)}, u32[]{:S(2)}) collective-permute-start(bf16[96,1408]{1,0:T(8,128)(2,1)S(1)} %collective-permute-done.3.r_2_), channel_id=1, source_target_pairs={{0,8},{4,12},{8,24},{12,28},{24,16},{28,20},{16,0},{20,4},{1,9},{5... | collective-permute-start | bytes 811016 | tf_op jit(solution)/shard_map/ppermute | solution.py:587
  30.8 8.6 %collective-permute-start.13 = (bf16[96,1408]{1,0:T(8,128)(2,1)S(1)}, bf16[96,1408]{1,0:T(8,128)(2,1)S(1)}, u32[]{:S(2)}, u32[]{:S(2)}) collective-permute-start(bf16[96,1408]{1,0:T(8,128)(2,1)S(1)} %collective-permute-done.6.r_4_), channel_id=1, source_target_pairs={{0,4},{4,0},{8,12},{12,8},{16,20},{20,16},{24,28},{28,24},{1,5},{5... | collective-permute-start | bytes 811016 | tf_op jit(solution)/shard_map/ppermute | solution.py:571
  31.3 9.4 %collective-permute-start.12 = (bf16[96,1408]{1,0:T(8,128)(2,1)S(1)}, bf16[96,1408]{1,0:T(8,128)(2,1)S(1)}, u32[]{:S(2)}, u32[]{:S(2)}) collective-permute-start(bf16[96,1408]{1,0:T(8,128)(2,1)S(1)} %collective-permute-done.6.r_4_), channel_id=1, source_target_pairs={{0,8},{4,12},{8,24},{12,28},{24,16},{28,20},{16,0},{20,4},{1,9},{5... | collective-permute-start | bytes 811016 | tf_op jit(solution)/shard_map/ppermute | solution.py:587
  34.5 11.2 %collective-permute-start.17 = (bf16[96,1536]{1,0:T(8,128)(2,1)S(1)}, bf16[96,1536]{1,0:T(8,128)(2,1)S(1)}, u32[]{:S(2)}, u32[]{:S(2)}) collective-permute-start(bf16[96,1536]{1,0:T(8,128)(2,1)S(1)} %arrange_ff.1.r_0_), channel_id=1, source_target_pairs={{0,2},{1,3},{2,0},{3,1},{4,6},{5,7},{6,4},{7,5},{8,10},{9,11},{10,... | collective-permute-start | bytes 884744 | tf_op jit(solution)/shard_map/ppermute | solution.py:550
  40.8 9.3 %collective-permute-start.16 = (bf16[96,1536]{1,0:T(8,128)(2,1)S(1)}, bf16[96,1536]{1,0:T(8,128)(2,1)}, u32[]{:S(2)}, u32[]{:S(2)}) collective-permute-start(bf16[96,1536]{1,0:T(8,128)(2,1)S(1)} %arrange_ff.1.r_0_), channel_id=1, source_target_pairs={{0,8},{4,12},{8,24},{12,28},{24,16},{28,20},{16,0},{20,4},{1,9},{5... | collective-permute-start | bytes 884744 | tf_op jit(solution)/shard_map/ppermute | solution.py:587
  50.3 10.2 %collective-permute-start.18 = (bf16[1152,128]{1,0:T(8,128)(2,1)S(1)}, bf16[1152,128]{1,0:T(8,128)(2,1)}, u32[]{:S(2)}, u32[]{:S(2)}) collective-permute-start(bf16[1152,128]{1,0:T(8,128)(2,1)S(1)} %get-tuple-element.202.w0), channel_id=1, source_target_pairs={{0,1},{1,0},{2,3},{3,2},{4,5},{5,4},{6,7},{7,6},{8,9},{9,8},{10,11... | collective-permute-start | bytes 884744 | tf_op jit(solution)/shard_map/ppermute | solution.py:550
  50.4 12.1 %collective-permute-start.24 = (bf16[96,1536]{1,0:T(8,128)(2,1)}, bf16[96,1536]{1,0:T(8,128)(2,1)}, u32[]{:S(2)}, u32[]{:S(2)}) collective-permute-start(bf16[96,1536]{1,0:T(8,128)(2,1)} %collective-permute-done.16.r_2_), channel_id=1, source_target_pairs={{0,8},{4,12},{8,24},{12,28},{24,16},{28,20},{16,0},{20,4},{1,9},{5... | collective-permute-start | bytes 884744 | tf_op jit(solution)/shard_map/ppermute | solution.py:587
  52.8 11.5 %collective-permute-start.22 = (bf16[1152,128]{1,0:T(8,128)(2,1)S(1)}, bf16[1152,128]{1,0:T(8,128)(2,1)}, u32[]{:S(2)}, u32[]{:S(2)}) collective-permute-start(bf16[1152,128]{1,0:T(8,128)(2,1)S(1)} %get-tuple-element.202.w0), channel_id=1, source_target_pairs={{0,2},{1,3},{2,0},{3,1},{4,6},{5,7},{6,4},{7,5},{8,10},{9,11},{10,... | collective-permute-start | bytes 884744 | tf_op jit(solution)/shard_map/ppermute | solution.py:550
  62.5 10.4 %collective-permute-start.25 = (bf16[96,1536]{1,0:T(8,128)(2,1)}, bf16[96,1536]{1,0:T(8,128)(2,1)S(1)}, u32[]{:S(2)}, u32[]{:S(2)}) collective-permute-start(bf16[96,1536]{1,0:T(8,128)(2,1)} %collective-permute-done.24.r_4_), channel_id=1, source_target_pairs={{0,8},{4,12},{8,24},{12,28},{24,16},{28,20},{16,0},{20,4},{1,9},{5... | collective-permute-start | bytes 884744 | tf_op jit(solution)/shard_map/ppermute | solution.py:587
  67.3 9.7 %collective-permute-start.28 = (bf16[96,1536]{1,0:T(8,128)(2,1)}, bf16[96,1536]{1,0:T(8,128)(2,1)S(1)}, u32[]{:S(2)}, u32[]{:S(2)}) collective-permute-start(bf16[96,1536]{1,0:T(8,128)(2,1)} %collective-permute-done.16.r_2_), channel_id=1, source_target_pairs={{0,2},{1,3},{2,0},{3,1},{4,6},{5,7},{6,4},{7,5},{8,10},{9,11},{10,... | collective-permute-start | bytes 884744 | tf_op jit(solution)/shard_map/ppermute | solution.py:550
  111.0 9.0 %collective-permute-start.39 = (bf16[96,1536]{1,0:T(8,128)(2,1)S(1)}, bf16[96,1536]{1,0:T(8,128)(2,1)S(1)}, u32[]{:S(2)}, u32[]{:S(2)}) collective-permute-start(bf16[96,1536]{1,0:T(8,128)(2,1)S(1)} %get-tuple-element.233), channel_id=1, source_target_pairs={{0,16},{4,20},{8,0},{12,4},{24,8},{28,12},{16,24},{20,28},{1,17},{... | collective-permute-start | bytes 884744 | tf_op jit(solution)/shard_map/ppermute | solution.py:587
  112.2 8.7 %collective-permute-start.40 = (bf16[96,1536]{1,0:T(8,128)(2,1)S(1)}, bf16[96,1536]{1,0:T(8,128)(2,1)S(1)}, u32[]{:S(2)}, u32[]{:S(2)}) collective-permute-start(bf16[96,1536]{1,0:T(8,128)(2,1)S(1)} %get-tuple-element.236), channel_id=1, source_target_pairs={{0,2},{1,3},{2,0},{3,1},{4,6},{5,7},{6,4},{7,5},{8,10},{9,11},{10,... | collective-permute-start | bytes 884744 | tf_op jit(solution)/shard_map/ppermute | solution.py:550
  124.8 11.7 %collective-permute-start.48 = (bf16[96,1536]{1,0:T(8,128)(2,1)S(1)}, bf16[96,1536]{1,0:T(8,128)(2,1)S(1)}, u32[]{:S(2)}, u32[]{:S(2)}) collective-permute-start(bf16[96,1536]{1,0:T(8,128)(2,1)S(1)} %add_convert_fusion.3), channel_id=1, source_target_pairs={{0,16},{4,20},{8,0},{12,4},{24,8},{28,12},{16,24},{20,28},{1,17},{... | collective-permute-start | bytes 884744 | tf_op jit(solution)/shard_map/ppermute | solution.py:587
  125.7 19.6 %collective-permute-start.44 = (bf16[96,1536]{1,0:T(8,128)(2,1)S(1)}, bf16[96,1536]{1,0:T(8,128)(2,1)S(1)}, u32[]{:S(2)}, u32[]{:S(2)}) collective-permute-start(bf16[96,1536]{1,0:T(8,128)(2,1)S(1)} %get-tuple-element.262), channel_id=1, source_target_pairs={{0,8},{4,12},{8,24},{12,28},{24,16},{28,20},{16,0},{20,4},{1,9},{5... | collective-permute-start | bytes 884744 | tf_op jit(solution)/shard_map/ppermute | solution.py:587
  129.1 16.3 %collective-permute-start.46 = (bf16[768,256]{1,0:T(8,128)(2,1)S(1)}, bf16[768,256]{1,0:T(8,128)(2,1)S(1)}, u32[]{:S(2)}, u32[]{:S(2)}) collective-permute-start(bf16[768,256]{1,0:T(8,128)(2,1)S(1)} %add_convert_fusion), channel_id=1, source_target_pairs={{0,2},{1,3},{2,0},{3,1},{4,6},{5,7},{6,4},{7,5},{8,10},{9,11},{10,... | collective-permute-start | bytes 1179656 | tf_op jit(solution)/shard_map/ppermute | solution.py:550
  136.6 11.8 %collective-permute-start.49 = (bf16[96,1536]{1,0:T(8,128)(2,1)S(1)}, bf16[96,1536]{1,0:T(8,128)(2,1)S(1)}, u32[]{:S(2)}, u32[]{:S(2)}) collective-permute-start(bf16[96,1536]{1,0:T(8,128)(2,1)S(1)} %add_convert_fusion.2), channel_id=1, source_target_pairs={{0,16},{4,20},{8,0},{12,4},{24,8},{28,12},{16,24},{20,28},{1,17},{... | collective-permute-start | bytes 884744 | tf_op jit(solution)/shard_map/ppermute | solution.py:587
  141.2 13.4 %collective-permute-start.50 = (bf16[96,1536]{1,0:T(8,128)(2,1)S(1)}, bf16[96,1536]{1,0:T(8,128)(2,1)S(1)}, u32[]{:S(2)}, u32[]{:S(2)}) collective-permute-start(bf16[96,1536]{1,0:T(8,128)(2,1)S(1)} %get-tuple-element.270), channel_id=1, source_target_pairs={{0,16},{4,20},{8,0},{12,4},{24,8},{28,12},{16,24},{20,28},{1,17},{... | collective-permute-start | bytes 884744 | tf_op jit(solution)/shard_map/ppermute | solution.py:587
  156.3 14.1 %collective-permute-start.51 = (bf16[320,768]{1,0:T(8,128)(2,1)S(1)}, bf16[320,768]{1,0:T(8,128)(2,1)S(1)}, u32[]{:S(2)}, u32[]{:S(2)}) collective-permute-start(bf16[320,768]{1,0:T(8,128)(2,1)S(1)} %input_pair.1.sent), channel_id=1, source_target_pairs={{0,2},{1,3},{2,0},{3,1},{4,6},{5,7},{6,4},{7,5},{8,10},{9,11},{10,... | collective-permute-start | bytes 1474568 | tf_op jit(solution)/shard_map/ppermute | solution.py:550
  166.4 8.8 %collective-permute-start.57 = (bf16[96,1536]{1,0:T(8,128)(2,1)S(1)}, bf16[96,1536]{1,0:T(8,128)(2,1)S(1)}, u32[]{:S(2)}, u32[]{:S(2)}) collective-permute-start(bf16[96,1536]{1,0:T(8,128)(2,1)S(1)} %add_convert_fusion.1), channel_id=1, source_target_pairs={{0,2},{1,3},{2,0},{3,1},{4,6},{5,7},{6,4},{7,5},{8,10},{9,11},{10,... | collective-permute-start | bytes 884744 | tf_op jit(solution)/shard_map/ppermute | solution.py:550
  172.5 10.8 %collective-permute-start.56 = (bf16[96,1408]{1,0:T(8,128)(2,1)S(1)}, bf16[96,1408]{1,0:T(8,128)(2,1)S(1)}, u32[]{:S(2)}, u32[]{:S(2)}) collective-permute-start(bf16[96,1408]{1,0:T(8,128)(2,1)S(1)} %add_convert_fusion.4), channel_id=1, source_target_pairs={{0,16},{4,20},{8,0},{12,4},{24,8},{28,12},{16,24},{20,28},{1,17},{... | collective-permute-start | bytes 811016 | tf_op jit(solution)/shard_map/ppermute | solution.py:587
  173.7 9.6 %collective-permute-start.61 = (bf16[96,1408]{1,0:T(8,128)(2,1)S(1)}, bf16[96,1408]{1,0:T(8,128)(2,1)S(1)}, u32[]{:S(2)}, u32[]{:S(2)}) collective-permute-start(bf16[96,1408]{1,0:T(8,128)(2,1)S(1)} %get-tuple-element.294), channel_id=1, source_target_pairs={{0,4},{4,0},{8,12},{12,8},{16,20},{20,16},{24,28},{28,24},{1,5},{5... | collective-permute-start | bytes 811016 | tf_op jit(solution)/shard_map/ppermute | solution.py:571
  (64 other events, 494.5 us)

commit v2 on v1

--- a/solution.py
+++ b/solution.py
@@ -94,20 +94,23 @@
     )
 
 
-def pack_body(*refs):
-    sources, firsts, seconds = refs[:6], refs[6:10], refs[10:14]
-    scr, scr_ff, here, sems = refs[14], refs[15], refs[16:22], refs[22]
+def fetch(refs, sems):
+    half = len(refs) // 2
     copies = [
         pltpu.make_async_copy(source, target, sems.at[i])
-        for i, (source, target) in enumerate(zip(sources, here))
+        for i, (source, target) in enumerate(zip(refs[:half], refs[half:]))
     ]
     for copy in copies:
         copy.start()
     for copy in copies:
         copy.wait()
-    q, kv, wo, gain, bias, ff = here
+
+
+def pack_body(*refs):
+    sources, outs, scr, here, sems = refs[:5], refs[5:9], refs[9], refs[10:15], refs[15]
+    fetch((*sources, *here), sems)
+    q, kv, wo, gain, bias = here
     rows, wide = q.shape[1], q.shape[2] // RANKS
-    part = ff.shape[1] // (8 * RANKS)
     eye = lax.broadcasted_iota(jnp.int32, (rows, rows), 0) == lax.broadcasted_iota(
         jnp.int32, (rows, rows), 1
     )
@@ -121,12 +124,19 @@
         for j, piece in enumerate((q[0], q[1], kv[0], kv[1], q[2], q[3], wo[...])):
             scr[t, :, wide * j : wide * j + wide] = piece[:, cut]
         scr[t, :, 7 * wide :] = vec.astype(bf16)
+    for k in range(RANKS):
+        outs[k][...] = scr[partner(k)]
+
+
+def pack_ff_body(ff, *refs):
+    outs, scr = refs[:RANKS], refs[RANKS]
+    part = ff.shape[1] // (8 * RANKS)
+    for t in range(RANKS):
         for j in range(8):
             at = ff_column(t, j, part)
-            scr_ff[t, :, part * j : part * j + part] = ff[:, at : at + part]
+            scr[t, :, part * j : part * j + part] = ff[:, at : at + part]
     for k in range(RANKS):
-        firsts[k][...] = scr[partner(k)]
-        seconds[k][...] = scr_ff[jnp.bitwise_xor(ff_rank(), k)]
+        outs[k][...] = scr[jnp.bitwise_xor(ff_rank(), k)]
 
 
 def arrange_own_body(p0, out):
@@ -251,7 +261,7 @@
         c_scr[at] = ctx.T.astype(bf16)
         return carry
 
-    lax.fori_loop(0, rows // 128, query_block, 0)
+    lax.fori_loop(0, rows // 128, query_block, 0, unroll=True)
     b = lax.axis_index("blk")
     for k, out in enumerate((c0, c1, c2, c3)):
         to = jnp.bitwise_xor(b, k)
@@ -259,27 +269,13 @@
         out[local:] = c_scr[pl.ds(pl.multiple_of(words + to * share, share), share)]
 
 
-def mix_body(c0, c1, c2, c3, w0, w1, w2, w3, norms, xw, xe, hr, n1, i1, scr):
+def mix_body(c0, c1, c2, c3, wo, norms, xw, xe, hr, n1, i1):
     b = lax.axis_index("blk")
-    rows = c0.shape[0]
-    width = xw.shape[1]
-    share = rows - xw.shape[0]
-    half = width // 2
-    cs, ws = (c0, c1, c2, c3), (w0, w1, w2, w3)
-    for rank in range(RANKS):
-
-        @pl.when(b == rank)
-        def _():
-            ctx = jnp.concatenate([cs[rank ^ q][...] for q in range(RANKS)], 1)
-            u = []
-            for t in range(RANKS):
-                w = ws[rank ^ t]
-                low = dot_nn(ctx[:, :half], w[width:])[:, :64]
-                high = dot_nn(ctx[:, half:], w[width:])[:, 64:]
-                u += [dot_nn(ctx, w[:width]), low + high]
-            scr[...] = jnp.concatenate(u, 1)
-
-    u = scr[...] + jnp.concatenate([xw[...].astype(f32), xe[block(xe, b, share)].astype(f32)], 0)
+    wide = c0.shape[1]
+    share = hr.shape[0] - xw.shape[0]
+    u = jnp.concatenate([xw[...].astype(f32), xe[block(xe, b, share)].astype(f32)], 0)
+    for k, c in enumerate((c0, c1, c2, c3)):
+        u = u + dot_nn(c[...], wo[block(wo, partner(k), wide)])
     normed, inverse = norm_stats(u)
     n1[...] = normed
     i1[...] = inverse
@@ -436,7 +432,7 @@
             out[at] = t.T
         return carry
 
-    lax.fori_loop(0, rows // 128, query_block, 0)
+    lax.fori_loop(0, rows // 128, query_block, 0, unroll=True)
     dqkv[:, :wide] = (dqw[...] * factor).astype(bf16)
     dqkv[:, wide : 2 * wide] = (dqe[...] * factor).astype(bf16)
     dqkv[:, 2 * wide : 3 * wide] = dk[...].astype(bf16)
@@ -459,14 +455,17 @@
         out[...] = scr[block(scr, to, out.shape[0])]
 
 
-def total_of(parts):
-    return parts[0][...].astype(f32) + (parts[1][...].astype(f32) + parts[2][...].astype(f32))
-
-
-def last_ff_body(a0, a1, a2, w_out, c0, c1, c2, c3, scr):
+def total_of(*parts):
+    total = parts[0][...].astype(f32)
+    for part in parts[1:]:
+        total = total + part[...].astype(f32)
+    return total
+
+
+def last_ff_body(a0, a1, a2, a3, w_out, c0, c1, c2, c3, scr):
     rows = c0.shape[0]
     width = c0.shape[1]
-    t = total_of((a0, a1, a2))
+    t = total_of(a0, a1, a2, a3)
     w_out[...] = t[:, width:]
     scr[...] = t[:, :width]
     for k, c in enumerate((c0, c1, c2, c3)):
@@ -485,7 +484,7 @@
 
 def last_body(a0, a1, a2, c0, c1, c2, c3, scr):
     rows = c0.shape[0]
-    scr[...] = total_of((a0, a1, a2))
+    scr[...] = total_of(a0, a1, a2)
     for k, c in enumerate((c0, c1, c2, c3)):
         c[...] = scr[block(scr, partner(k), rows)].astype(bf16)
 
@@ -639,24 +638,25 @@
         pack = call(
             pack_body,
             "pack",
-            [((part_rows, slab_cols), bf16)] * 4 + [((part_rows, ff), bf16)] * 4,
-            [pltpu.VMEM((RANKS, part_rows, n), bf16) for n in (slab_cols, ff)]
+            [((part_rows, slab_cols), bf16)] * 4,
+            [pltpu.VMEM((RANKS, part_rows, slab_cols), bf16)]
             + [pltpu.VMEM((n, part_rows, width), bf16) for n in (4, 2)]
             + [pltpu.VMEM((part_rows, width), bf16)]
             + [pltpu.VMEM((2, part_rows), bf16)] * 2
-            + [pltpu.VMEM((part_rows, RANKS * ff), bf16), pltpu.SemaphoreType.DMA((6,))],
-            held=6,
+            + [pltpu.SemaphoreType.DMA((5,))],
+            held=5,
             vmem=60,
         )
         pieces = pack(
-            query_weights[0],
-            kv_weights[0],
-            out_weight[0],
-            norm_gain[0],
-            norm_bias[0],
-            ff_in[0],
-        )
-        pieces, ff_pieces = pieces[:4], pieces[4:]
+            query_weights[0], kv_weights[0], out_weight[0], norm_gain[0], norm_bias[0]
+        )
+        pack_ff = call(
+            pack_ff_body,
+            "pack_ff",
+            [((part_rows, ff), bf16)] * 4,
+            [pltpu.VMEM((RANKS, part_rows, ff), bf16)],
+        )
+        ff_pieces = pack_ff(after(ff_in[0], pieces[0]))
         own = call(
             arrange_own_body, "arrange_own", [((RANKS * part_rows, slab_cols), f32)]
         )(pieces[0])
@@ -743,7 +743,6 @@
     wos = [wo_col, wb, wa, swap(after(wa, ctx), 1)]
     if direct:
         f3, y1 = along_ring(f2), swap(after(f1, ctx), 2)
-        wos = after(wos, f3)
     join_out = call(
         join_out_body,
         "join_out",
@@ -755,24 +754,23 @@
         mix_body,
         "mix",
         [((mine, width), bf16), ((mine, width), f32), ((mine, 1), f32)],
-        [pltpu.VMEM((mine, width), f32)],
-    )
-    hr, n1, i1 = mix(*ctx, *wos, norms, xw_own, xe)
-    across, beside = swap_ff(hr, 2, direct), swap(hr, 1)
-    if direct:
-        fb, y2 = along_ring(after(y0, hr), -1), swap(after(f2, hr), 2)
-        across = after(across, y1)
-        ff_slabs = [ff_slab, y0, f1, y1, f2, y2, f3, fb]
-    hs = [hr, beside, across, swap(across, 1)]
+    )
+    hr, n1, i1 = mix(*ctx, after(wo, f3) if direct else wo, norms, xw_own, xe)
+
     def place_ff(slots, *args):
         outs = [((width, ff), bf16), ((ff, width), bf16)]
         same = len(args) - len(slots)
         return call(lambda *r: place_ff_body(slots, *r), "place_ff", outs, same=same)(*args)
 
-    if direct:
-        early = (0, 1, 2, 3, 4)
-        ready = place_ff(early, *(ff_slabs[j] for j in early))
-        w1, w2 = place_ff((5, 6, 7), *ready, *ff_slabs[5:])
+    across, beside = swap_ff(hr, 2, direct), swap(hr, 1)
+    if direct:
+        fb, y2 = along_ring(after(y0, hr), -1), swap(after(f2, hr), 2)
+        ready = place_ff((0, 1, 2, 3, 4, 6), ff_slab, y0, f1, y1, f2, f3)
+        across = after(across, ready)
+        ff_slabs = [ff_slab, y0, f1, y1, f2, y2, f3, fb]
+    hs = [hr, beside, across, swap(across, 1)]
+    if direct:
+        w1, w2 = place_ff((5, 7), *ready, ff_slabs[5], ff_slabs[7])
     else:
         w1, w2 = place_ff((0,), ff_slabs[0])
     feed = call(
@@ -824,9 +822,11 @@
     sent = plus(across, after(core, ff_chunks)[0])
     dhs = [own, core, swap_ff(sent, 2, direct)]
     if direct:
-        fz, fy = along_ring(ff_chunks[2], -1), swap(ff_chunks[5], 2)
-        dhs[2] = after(dhs[2], fz, fy)
-        fz = along_ring(plus(ff_chunks[4], fz, fy), -1)
+        ff0, ff1, ff2, ff3, ff4, ff5, ff6, ff7 = ff_chunks
+        fy, fz = swap(ff5, 2), along_ring(ff2)
+        part = plus(ff4, fy)
+        dhs[2] = after(dhs[2], part, fz)
+        fl = along_ring(part, -1)
 
     norm_one = call(
         norm_one_body,
@@ -844,7 +844,7 @@
     sent = plus(across, after(dcs[1], dcs[2], dcs[3])[:width])
     outs = [wo_own, dcs[1], swap(sent, 2)]
     if direct:
-        fb = along_ring(after(ff_chunks[3], du1))
+        fb, fc = along_ring(after(ff3, du1)), along_ring(after(ff7, du1), -1)
     dcs = after(dcs, sent)
     attend_back = call(
         lambda *r: attend_back_body(factor, *r),
@@ -866,9 +866,8 @@
     )
     own, across, core = to_input(dqkv, wq, du1, ye)
     if direct:
-        own = after(own, fb)
-        fz = along_ring(plus(ff_chunks[6], after(fz, dqkv)), -1)
-        fc = along_ring(after(ff_chunks[7], dqkv), -1)
+        own = after(own, fl)
+        fl = along_ring(plus(ff6, after(fl, dqkv)), -1)
     core = swap(core, 1)
     proj_grads = call(
         proj_grads_body,
@@ -880,8 +879,8 @@
     )
     chunks = proj_grads(after(dqkv, own), xw, xe, *outs)
     if direct:
-        part = plus(chunks[2], after(over_x(chunks[3]), fz, fc))
-        fy = swap(plus(ff_chunks[1], fb, after(fc, part)), 2)
+        part = plus(chunks[2], after(over_x(chunks[3]), fl, fb, fc))
+        fy = swap(plus(ff1, fb, after(fc, part)), 2)
         cx, cz = over_x(after(chunks[5], part)), along_ring(part, -1)
         core = after(core, part)
     (sent,) = call(input_pair_body, "input_pair", [((local + ents + 2 * share, width), bf16)])(across, core)
@@ -903,7 +902,7 @@
         )
         part = plus(chunks[4], cz, cx)
         cx, cz = over_x(after(chunks[7], part)), along_ring(part, -1)
-        grad_ff_out, *back = last_ff(ff_chunks[0], after(fz, part), fy)
+        grad_ff_out, *back = last_ff(ff0, fz, fl, after(fy, part))
         part = plus(chunks[6], after(cz, came), cx)
         cx, cz = over_x(after(chunks[1], part)), along_ring(part, -1)
         back = [back[0]] + [swap_ff(back[k], k, direct) for k in (1, 2, 3)]

time: 191 us -> 192 us (level)
  waiting for transfers between devices: 81.9 us -> 89.1 us
  starting transfers between devices: 61.6 us -> 57.2 us
  Pallas kernels: 37 us -> 33.6 us
    ppermute x34, waiting for transfers between devices: 18.6 us -> 28.8 us  [swap(): return lax.ppermute(x, 'blk', [(i, i ^ k) for i in range(RANKS)])]
    ppermute x14, waiting for transfers between devices: 41.9 us -> 36.6 us  [over_x(): return lax.ppermute(x, 'seq', [(i, i ^ 1) for i in range(8)])]
    pallas_call x27 -> x28, Pallas kernels: 37 us -> 33.6 us  [run(): pl.pallas_call(body, name=name, out_shape=[jax.ShapeDtypeStruct(s, t) for...]
    ppermute x15, starting transfers between devices: 23.2 us -> 21 us  [along_ring(): lax.ppermute(x, 'seq', [(2 * z + i, 2 * to + i) for z, to in route for i...]
    ppermute x34, starting transfers between devices: 21.6 us -> 19.5 us  [swap(): return lax.ppermute(x, 'blk', [(i, i ^ k) for i in range(RANKS)])]
    unnamed x46 -> x44, local copies, waits for them, and re-layouts: 5.77 us -> 7.59 us
  transfers between devices with their start and end apart: 65 -> 65, of which waited for: 34 -> 33; matrix products, arithmetic and copies ran while one was open for 1% -> 1% of each run, Pallas kernels for 14% -> 12%
where the time goes in v2:
time: 192 us
  waiting for transfers between devices  89.1 us (46%)
  starting transfers between devices  57.2 us (30%)
  Pallas kernels  33.6 us (18%)
  local copies, waits for them, and re-layouts  9.02 us (5%)
    ppermute x14, waiting for transfers between devices, over_x(): return lax.ppermute(x, 'seq', [(i, i ^ 1) for i in range(8)])  36.6 us
    pallas_call x28, Pallas kernels, run(): pl.pallas_call(body, name=name, out_shape=[jax.ShapeDtypeStruct(s, t) for...  33.6 us
    ppermute x34, waiting for transfers between devices, swap(): return lax.ppermute(x, 'blk', [(i, i ^ k) for i in range(RANKS)])  28.8 us
    ppermute x15, waiting for transfers between devices, along_ring(): lax.ppermute(x, 'seq', [(2 * z + i, 2 * to + i) for z, to in route for i...  23.2 us
    ppermute x15, starting transfers between devices, along_ring(): lax.ppermute(x, 'seq', [(2 * z + i, 2 * to + i) for z, to in route for i...  21 us
    ppermute x34, starting transfers between devices, swap(): return lax.ppermute(x, 'blk', [(i, i ^ k) for i in range(RANKS)])  19.5 us
    ppermute x14, starting transfers between devices, over_x(): return lax.ppermute(x, 'seq', [(i, i ^ 1) for i in range(8)])  14.9 us
    unnamed x44, local copies, waits for them, and re-layouts  7.59 us
  transfers between devices with their start and end apart: 65, of which 33 were waited for; matrix products, arithmetic and copies ran while one was open for 1% of the time, Pallas kernels for 12%

profile of v2, /device:TPU:0, one launch (start us, length us, event | category | flops | bytes accessed | tf_op | source)
XLA Modules:
  0.0 191.5 jit_solution(11042189007339596313)
XLA Ops:
  3.2 2.6 %collective-permute-start.1 = (bf16[24,1408]{1,0:T(8,128)(2,1)}, bf16[24,1408]{1,0:T(8,128)(2,1)S(1)}, u32[]{:S(2)}, u32[]{:S(2)}) collective-permute-start(bf16[24,1408]{1,0:T(8,128)(2,1)} %get-tuple-element.158), channel_id=1, source_target_pairs={{0,2},{1,3},{2,0},{3,1},{4,6},{5,7},{6,4},{7,5},{8,10},{9,11},{10,... | collective-permute-start | bytes 202760 | tf_op jit(solution)/shard_map/ppermute | solution.py:549
  14.9 3.9 %collective-permute-done.4.r_1_ = bf16[96,1408]{1,0:T(8,128)(2,1)S(1)} collective-permute-done((bf16[96,1408]{1,0:T(8,128)(2,1)S(1)}, bf16[96,1408]{1,0:T(8,128)(2,1)S(1)}, u32[]{:S(2)}, u32[]{:S(2)}) %collective-permute-start.4) | collective-permute-done | bytes 270368 | tf_op jit(solution)/shard_map/ppermute | solution.py:570
  18.8 2.1 %collective-permute-done.3.r_2_ = bf16[96,1408]{1,0:T(8,128)(2,1)S(1)} collective-permute-done((bf16[96,1408]{1,0:T(8,128)(2,1)S(1)}, bf16[96,1408]{1,0:T(8,128)(2,1)S(1)}, u32[]{:S(2)}, u32[]{:S(2)}) %collective-permute-start.3) | collective-permute-done | bytes 270368 | tf_op jit(solution)/shard_map/ppermute | solution.py:586
  26.7 2.8 %collective-permute-done.9.p2 = bf16[24,768]{1,0:T(8,128)(2,1)S(1)} collective-permute-done((bf16[24,768]{1,0:T(8,128)(2,1)S(1)}, bf16[24,768]{1,0:T(8,128)(2,1)S(1)}, u32[]{:S(2)}, u32[]{:S(2)}) %collective-permute-start.9) | collective-permute-done | bytes 36896 | tf_op jit(solution)/shard_map/ppermute | solution.py:570
  35.5 3.4 %collective-permute-done.13.r_3_ = bf16[96,1408]{1,0:T(8,128)(2,1)S(1)} collective-permute-done((bf16[96,1408]{1,0:T(8,128)(2,1)S(1)}, bf16[96,1408]{1,0:T(8,128)(2,1)S(1)}, u32[]{:S(2)}, u32[]{:S(2)}) %collective-permute-start.13) | collective-permute-done | bytes 270368 | tf_op jit(solution)/shard_map/ppermute | solution.py:570
  52.1 2.4 %collective-permute-start.24 = (bf16[96,1536]{1,0:T(8,128)(2,1)}, bf16[96,1536]{1,0:T(8,128)(2,1)}, u32[]{:S(2)}, u32[]{:S(2)}) collective-permute-start(bf16[96,1536]{1,0:T(8,128)(2,1)} %collective-permute-done.16.r_2_), channel_id=1, source_target_pairs={{0,8},{4,12},{8,24},{12,28},{24,16},{28,20},{16,0},{20,4},{1,9},{5... | collective-permute-start | bytes 884744 | tf_op jit(solution)/shard_map/ppermute | solution.py:586
  54.6 4.8 %attend.1 = (bf16[160,192]{1,0:T(8,128)(2,1)S(1)}, bf16[160,192]{1,0:T(8,128)(2,1)S(1)}, bf16[160,192]{1,0:T(8,128)(2,1)S(1)}, bf16[160,192]{1,0:T(8,128)(2,1)S(...) custom-call(bf16[512,768]{1,0:T(8,128)(2,1)S(1)} %join_rows.1.r_0_.x, ...), custom_call_target="tpu_custom_call" | custom-call | flops 7000000 | bytes 7000 | tf_op jit(solution)/shard_map/attend/pallas_call | solution.py:34
  61.4 3.4 %collective-permute-done.20.c2 = bf16[160,192]{1,0:T(8,128)(2,1)S(1)} collective-permute-done((bf16[160,192]{1,0:T(8,128)(2,1)S(1)}, bf16[160,192]{1,0:T(8,128)(2,1)S(1)}, u32[]{:S(2)}, u32[]{:S(2)}) %collective-permute-start.20) | collective-permute-done | bytes 61472 | tf_op jit(solution)/shard_map/ppermute | solution.py:549
  70.0 6.1 %collective-permute-done.25.r_5_ = bf16[96,1536]{1,0:T(8,128)(2,1)S(1)} collective-permute-done((bf16[96,1536]{1,0:T(8,128)(2,1)}, bf16[96,1536]{1,0:T(8,128)(2,1)S(1)}, u32[]{:S(2)}, u32[]{:S(2)}) %collective-permute-start.25) | collective-permute-done | bytes 294944 | tf_op jit(solution)/shard_map/ppermute | solution.py:586
  79.8 4.4 %collective-permute-done.27.h2 = bf16[160,768]{1,0:T(8,128)(2,1)S(1)} collective-permute-done((bf16[160,768]{1,0:T(8,128)(2,1)S(1)}, bf16[160,768]{1,0:T(8,128)(2,1)S(1)}, u32[]{:S(2)}, u32[]{:S(2)}) %collective-permute-start.27) | collective-permute-done | bytes 245792 | tf_op jit(solution)/shard_map/ppermute | solution.py:570
  86.6 2.3 %feed.1 = (f32[160,768]{1,0:T(8,128)S(1)}, bf16[160,768]{1,0:T(8,128)(2,1)S(1)}, bf16[2,160,768]{2,1,0:T(8,128)(2,1)S(1)}, bf16[4,160,768]{2,1,0:T(8,128)(2,1)S(1)}, bf16[4,160,768]{2,1,0:T(8,128)(2,1)S(1)}) custom-call(bf16[160,768]{1,0:T(8,128)(2,1)S(1)} %get-tuple-element.203.h0, bf16[160,768]{1,0:T(8,128)(2,1)S(1)} %collective-permute-done.26.h1, ...), custom_call_target="tpu_custom_call" | custom-call | flops 3000000 | bytes 3000 | tf_op jit(solution)/shard_map/feed/pallas_call | solution.py:34
  92.0 7.0 %collective-permute-done.33.f2 = bf16[160,768]{1,0:T(8,128)(2,1)S(1)} collective-permute-done((bf16[160,768]{1,0:T(8,128)(2,1)S(1)}, bf16[160,768]{1,0:T(8,128)(2,1)S(1)}, u32[]{:S(2)}, u32[]{:S(2)}) %collective-permute-start.33) | collective-permute-done | bytes 245792 | tf_op jit(solution)/shard_map/ppermute | solution.py:570
  101.0 6.2 %collective-permute-done.35.d2 = bf16[160,768]{1,0:T(8,128)(2,1)S(1)} collective-permute-done((bf16[160,768]{1,0:T(8,128)(2,1)S(1)}, bf16[160,768]{1,0:T(8,128)(2,1)S(1)}, u32[]{:S(2)}, u32[]{:S(2)}) %collective-permute-start.35) | collective-permute-done | bytes 245792 | tf_op jit(solution)/shard_map/ppermute | solution.py:570
  111.0 2.1 %feed_grads.1 = (bf16[96,1536]{1,0:T(8,128)(2,1)S(1)}, bf16[96,1536]{1,0:T(8,128)(2,1)S(1)}, bf16[96,1536]{1,0:T(8,128)(2,1)S(1)}, bf16[96,1536]{1,0:T(8,128)(2,...) custom-call(bf16[160,768]{1,0:T(8,128)(2,1)S(1)} %get-tuple-element., ...), custom_call_target="tpu_custom_call" | custom-call | flops 3000000 | bytes 3000 | tf_op jit(solution)/shard_map/feed_grads/pallas_call | solution.py:34
  117.4 4.8 %collective-permute-done.39 = bf16[96,1536]{1,0:T(8,128)(2,1)S(1)} collective-permute-done((bf16[96,1536]{1,0:T(8,128)(2,1)S(1)}, bf16[96,1536]{1,0:T(8,128)(2,1)S(1)}, u32[]{:S(2)}, u32[]{:S(2)}) %collective-permute-start.39) | collective-permute-done | bytes 294944 | tf_op jit(solution)/shard_map/ppermute | solution.py:549
  132.7 4.8 %attend_back.1.dqkv = bf16[640,768]{1,0:T(8,128)(2,1)S(1)} custom-call(bf16[160,192]{1,0:T(8,128)(2,1)S(1)} %get-tuple-element.246.r_0_, bf16[1696,256]{1,0:T(8,128)(2,1)S(1)} %collective-permute-done.41.r_1_.o1, bf16[160,192]{1,0:T(8,128)(2,1)S(1)} %collective-permute-done.42.r_2_, bf16[160,192]{1,0:T(8,128)(2,1)S(1)} %collective-permute-done.43.r_3_, ...), custom_call_target="tpu_custom_call" | custom-call | flops 7000000 | bytes 7000 | tf_op jit(solution)/shard_map/attend_back/pallas_call | solution.py:34
  140.6 2.8 %collective-permute-done.46.o2 = bf16[768,256]{1,0:T(8,128)(2,1)S(1)} collective-permute-done((bf16[768,256]{1,0:T(8,128)(2,1)S(1)}, bf16[768,256]{1,0:T(8,128)(2,1)S(1)}, u32[]{:S(2)}, u32[]{:S(2)}) %collective-permute-start.46) | collective-permute-done | bytes 393248 | tf_op jit(solution)/shard_map/ppermute | solution.py:549
  146.1 3.8 %collective-permute-done.50 = bf16[96,1536]{1,0:T(8,128)(2,1)S(1)} collective-permute-done((bf16[96,1536]{1,0:T(8,128)(2,1)S(1)}, bf16[96,1536]{1,0:T(8,128)(2,1)S(1)}, u32[]{:S(2)}, u32[]{:S(2)}) %collective-permute-start.50) | collective-permute-done | bytes 294944 | tf_op jit(solution)/shard_map/ppermute | solution.py:586
  149.9 5.8 %collective-permute-done.48.a2 = bf16[96,1536]{1,0:T(8,128)(2,1)S(1)} collective-permute-done((bf16[96,1536]{1,0:T(8,128)(2,1)S(1)}, bf16[96,1536]{1,0:T(8,128)(2,1)S(1)}, u32[]{:S(2)}, u32[]{:S(2)}) %collective-permute-start.48) | collective-permute-done | bytes 294944 | tf_op jit(solution)/shard_map/ppermute | solution.py:586
  159.5 4.2 %collective-permute-done.53 = bf16[96,1408]{1,0:T(8,128)(2,1)S(1)} collective-permute-done((bf16[96,1408]{1,0:T(8,128)(2,1)S(1)}, bf16[96,1408]{1,0:T(8,128)(2,1)S(1)}, u32[]{:S(2)}, u32[]{:S(2)}) %collective-permute-start.53) | collective-permute-done | bytes 270368 | tf_op jit(solution)/shard_map/ppermute | solution.py:570
  164.6 2.6 %collective-permute-start.54 = (bf16[96,1408]{1,0:T(8,128)(2,1)S(1)}, bf16[96,1408]{1,0:T(8,128)(2,1)S(1)}, u32[]{:S(2)}, u32[]{:S(2)}) collective-permute-start(bf16[96,1408]{1,0:T(8,128)(2,1)S(1)} %add_convert_fusion.5), channel_id=1, source_target_pairs={{0,16},{4,20},{8,0},{12,4},{24,8},{28,12},{16,24},{20,28},{1,17},{... | collective-permute-start | bytes 811016 | tf_op jit(solution)/shard_map/ppermute | solution.py:586
  169.3 3.5 %collective-permute-done.51.came = bf16[320,768]{1,0:T(8,128)(2,1)S(1)} collective-permute-done((bf16[320,768]{1,0:T(8,128)(2,1)S(1)}, bf16[320,768]{1,0:T(8,128)(2,1)S(1)}, u32[]{:S(2)}, u32[]{:S(2)}) %collective-permute-start.51) | collective-permute-done | bytes 491552 | tf_op jit(solution)/shard_map/ppermute | solution.py:549
  179.9 2.5 %collective-permute-done.59.c2 = bf16[24,768]{1,0:T(8,128)(2,1)S(1)} collective-permute-done((bf16[24,768]{1,0:T(8,128)(2,1)S(1)}, bf16[24,768]{1,0:T(8,128)(2,1)S(1)}, u32[]{:S(2)}, u32[]{:S(2)}) %collective-permute-start.59) | collective-permute-done | bytes 36896 | tf_op jit(solution)/shard_map/ppermute | solution.py:570
  187.0 3.2 %collective-permute-done.63.c2 = bf16[24,1408]{1,0:T(8,128)(2,1)S(1)} collective-permute-done((bf16[24,1408]{1,0:T(8,128)(2,1)S(1)}, bf16[24,1408]{1,0:T(8,128)(2,1)S(1)}, u32[]{:S(2)}, u32[]{:S(2)}) %collective-permute-start.63) | collective-permute-done | bytes 67616 | tf_op jit(solution)/shard_map/ppermute | solution.py:549
  (193 shorter events, 98.3 us)
Async XLA Ops:
  11.8 9.1 %collective-permute-start.3 = (bf16[96,1408]{1,0:T(8,128)(2,1)S(1)}, bf16[96,1408]{1,0:T(8,128)(2,1)S(1)}, u32[]{:S(2)}, u32[]{:S(2)}) collective-permute-start(bf16[96,1408]{1,0:T(8,128)(2,1)S(1)} %arrange.1.r_0_), channel_id=1, source_target_pairs={{0,8},{4,12},{8,24},{12,28},{24,16},{28,20},{16,0},{20,4},{1,9},{5... | collective-permute-start | bytes 811016 | tf_op jit(solution)/shard_map/ppermute | solution.py:586
  13.6 16.0 %collective-permute-start.11 = (bf16[128,768]{1,0:T(8,128)(2,1)S(1)}, bf16[128,768]{1,0:T(8,128)(2,1)S(1)}, u32[]{:S(2)}, u32[]{:S(2)}) collective-permute-start(bf16[128,768]{1,0:T(8,128)(2,1)S(1)} %bitcast.44), channel_id=1, source_target_pairs={{0,2},{1,3},{2,0},{3,1},{4,6},{5,7},{6,4},{7,5},{8,10},{9,11},{10,... | collective-permute-start | bytes 589832 | tf_op jit(solution)/shard_map/ppermute | solution.py:549
  21.5 8.8 %collective-permute-start.6 = (bf16[96,1408]{1,0:T(8,128)(2,1)S(1)}, bf16[96,1408]{1,0:T(8,128)(2,1)S(1)}, u32[]{:S(2)}, u32[]{:S(2)}) collective-permute-start(bf16[96,1408]{1,0:T(8,128)(2,1)S(1)} %collective-permute-done.3.r_2_), channel_id=1, source_target_pairs={{0,8},{4,12},{8,24},{12,28},{24,16},{28,20},{16,0},{20,4},{1,9},{5... | collective-permute-start | bytes 811016 | tf_op jit(solution)/shard_map/ppermute | solution.py:586
  31.0 9.4 %collective-permute-start.12 = (bf16[96,1408]{1,0:T(8,128)(2,1)S(1)}, bf16[96,1408]{1,0:T(8,128)(2,1)S(1)}, u32[]{:S(2)}, u32[]{:S(2)}) collective-permute-start(bf16[96,1408]{1,0:T(8,128)(2,1)S(1)} %collective-permute-done.6.r_4_), channel_id=1, source_target_pairs={{0,8},{4,12},{8,24},{12,28},{24,16},{28,20},{16,0},{20,4},{1,9},{5... | collective-permute-start | bytes 811016 | tf_op jit(solution)/shard_map/ppermute | solution.py:586
  34.0 13.1 %collective-permute-start.17 = (bf16[96,1536]{1,0:T(8,128)(2,1)S(1)}, bf16[96,1536]{1,0:T(8,128)(2,1)S(1)}, u32[]{:S(2)}, u32[]{:S(2)}) collective-permute-start(bf16[96,1536]{1,0:T(8,128)(2,1)S(1)} %arrange_ff.1.r_0_), channel_id=1, source_target_pairs={{0,2},{1,3},{2,0},{3,1},{4,6},{5,7},{6,4},{7,5},{8,10},{9,11},{10,... | collective-permute-start | bytes 884744 | tf_op jit(solution)/shard_map/ppermute | solution.py:549
  40.3 9.2 %collective-permute-start.16 = (bf16[96,1536]{1,0:T(8,128)(2,1)S(1)}, bf16[96,1536]{1,0:T(8,128)(2,1)}, u32[]{:S(2)}, u32[]{:S(2)}) collective-permute-start(bf16[96,1536]{1,0:T(8,128)(2,1)S(1)} %arrange_ff.1.r_0_), channel_id=1, source_target_pairs={{0,8},{4,12},{8,24},{12,28},{24,16},{28,20},{16,0},{20,4},{1,9},{5... | collective-permute-start | bytes 884744 | tf_op jit(solution)/shard_map/ppermute | solution.py:586
  50.4 9.0 %collective-permute-start.18 = (bf16[1152,128]{1,0:T(8,128)(2,1)}, bf16[1152,128]{1,0:T(8,128)(2,1)}, u32[]{:S(2)}, u32[]{:S(2)}) collective-permute-start(bf16[1152,128]{1,0:T(8,128)(2,1)} %get-tuple-element.194.w0), channel_id=1, source_target_pairs={{0,1},{1,0},{2,3},{3,2},{4,5},{5,4},{6,7},{7,6},{8,9},{9,8},{10,11... | collective-permute-start | bytes 884744 | tf_op jit(solution)/shard_map/ppermute | solution.py:549
  50.4 10.9 %collective-permute-start.22 = (bf16[1152,128]{1,0:T(8,128)(2,1)}, bf16[1152,128]{1,0:T(8,128)(2,1)}, u32[]{:S(2)}, u32[]{:S(2)}) collective-permute-start(bf16[1152,128]{1,0:T(8,128)(2,1)} %get-tuple-element.194.w0), channel_id=1, source_target_pairs={{0,2},{1,3},{2,0},{3,1},{4,6},{5,7},{6,4},{7,5},{8,10},{9,11},{10,... | collective-permute-start | bytes 884744 | tf_op jit(solution)/shard_map/ppermute | solution.py:549
  52.1 13.9 %collective-permute-start.24 = (bf16[96,1536]{1,0:T(8,128)(2,1)}, bf16[96,1536]{1,0:T(8,128)(2,1)}, u32[]{:S(2)}, u32[]{:S(2)}) collective-permute-start(bf16[96,1536]{1,0:T(8,128)(2,1)} %collective-permute-done.16.r_2_), channel_id=1, source_target_pairs={{0,8},{4,12},{8,24},{12,28},{24,16},{28,20},{16,0},{20,4},{1,9},{5... | collective-permute-start | bytes 884744 | tf_op jit(solution)/shard_map/ppermute | solution.py:586
  65.9 10.3 %collective-permute-start.25 = (bf16[96,1536]{1,0:T(8,128)(2,1)}, bf16[96,1536]{1,0:T(8,128)(2,1)S(1)}, u32[]{:S(2)}, u32[]{:S(2)}) collective-permute-start(bf16[96,1536]{1,0:T(8,128)(2,1)} %collective-permute-done.24.r_4_), channel_id=1, source_target_pairs={{0,8},{4,12},{8,24},{12,28},{24,16},{28,20},{16,0},{20,4},{1,9},{5... | collective-permute-start | bytes 884744 | tf_op jit(solution)/shard_map/ppermute | solution.py:586
  67.7 10.9 %collective-permute-start.28 = (bf16[96,1536]{1,0:T(8,128)(2,1)}, bf16[96,1536]{1,0:T(8,128)(2,1)S(1)}, u32[]{:S(2)}, u32[]{:S(2)}) collective-permute-start(bf16[96,1536]{1,0:T(8,128)(2,1)} %collective-permute-done.16.r_2_), channel_id=1, source_target_pairs={{0,2},{1,3},{2,0},{3,1},{4,6},{5,7},{6,4},{7,5},{8,10},{9,11},{10,... | collective-permute-start | bytes 884744 | tf_op jit(solution)/shard_map/ppermute | solution.py:549
  113.1 9.0 %collective-permute-start.39 = (bf16[96,1536]{1,0:T(8,128)(2,1)S(1)}, bf16[96,1536]{1,0:T(8,128)(2,1)S(1)}, u32[]{:S(2)}, u32[]{:S(2)}) collective-permute-start(bf16[96,1536]{1,0:T(8,128)(2,1)S(1)} %get-tuple-element.232), channel_id=1, source_target_pairs={{0,2},{1,3},{2,0},{3,1},{4,6},{5,7},{6,4},{7,5},{8,10},{9,11},{10,... | collective-permute-start | bytes 884744 | tf_op jit(solution)/shard_map/ppermute | solution.py:549
  114.4 9.6 %collective-permute-start.40 = (bf16[96,1536]{1,0:T(8,128)(2,1)S(1)}, bf16[96,1536]{1,0:T(8,128)(2,1)S(1)}, u32[]{:S(2)}, u32[]{:S(2)}) collective-permute-start(bf16[96,1536]{1,0:T(8,128)(2,1)S(1)} %get-tuple-element.229), channel_id=1, source_target_pairs={{0,8},{4,12},{8,24},{12,28},{24,16},{28,20},{16,0},{20,4},{1,9},{5... | collective-permute-start | bytes 884744 | tf_op jit(solution)/shard_map/ppermute | solution.py:586
  127.4 10.1 %collective-permute-start.44 = (bf16[96,1536]{1,0:T(8,128)(2,1)S(1)}, bf16[96,1536]{1,0:T(8,128)(2,1)S(1)}, u32[]{:S(2)}, u32[]{:S(2)}) collective-permute-start(bf16[96,1536]{1,0:T(8,128)(2,1)S(1)} %add_convert_fusion.3), channel_id=1, source_target_pairs={{0,16},{4,20},{8,0},{12,4},{24,8},{28,12},{16,24},{20,28},{1,17},{... | collective-permute-start | bytes 884744 | tf_op jit(solution)/shard_map/ppermute | solution.py:586
  128.2 17.8 %collective-permute-start.49 = (bf16[96,1536]{1,0:T(8,128)(2,1)S(1)}, bf16[96,1536]{1,0:T(8,128)(2,1)S(1)}, u32[]{:S(2)}, u32[]{:S(2)}) collective-permute-start(bf16[96,1536]{1,0:T(8,128)(2,1)S(1)} %get-tuple-element.265), channel_id=1, source_target_pairs={{0,8},{4,12},{8,24},{12,28},{24,16},{28,20},{16,0},{20,4},{1,9},{5... | collective-permute-start | bytes 884744 | tf_op jit(solution)/shard_map/ppermute | solution.py:586
  130.8 19.0 %collective-permute-start.50 = (bf16[96,1536]{1,0:T(8,128)(2,1)S(1)}, bf16[96,1536]{1,0:T(8,128)(2,1)S(1)}, u32[]{:S(2)}, u32[]{:S(2)}) collective-permute-start(bf16[96,1536]{1,0:T(8,128)(2,1)S(1)} %get-tuple-element.266), channel_id=1, source_target_pairs={{0,16},{4,20},{8,0},{12,4},{24,8},{28,12},{16,24},{20,28},{1,17},{... | collective-permute-start | bytes 884744 | tf_op jit(solution)/shard_map/ppermute | solution.py:586
  131.8 11.7 %collective-permute-start.46 = (bf16[768,256]{1,0:T(8,128)(2,1)S(1)}, bf16[768,256]{1,0:T(8,128)(2,1)S(1)}, u32[]{:S(2)}, u32[]{:S(2)}) collective-permute-start(bf16[768,256]{1,0:T(8,128)(2,1)S(1)} %add_convert_fusion), channel_id=1, source_target_pairs={{0,2},{1,3},{2,0},{3,1},{4,6},{5,7},{6,4},{7,5},{8,10},{9,11},{10,... | collective-permute-start | bytes 1179656 | tf_op jit(solution)/shard_map/ppermute | solution.py:549
  137.6 18.0 %collective-permute-start.48 = (bf16[96,1536]{1,0:T(8,128)(2,1)S(1)}, bf16[96,1536]{1,0:T(8,128)(2,1)S(1)}, u32[]{:S(2)}, u32[]{:S(2)}) collective-permute-start(bf16[96,1536]{1,0:T(8,128)(2,1)S(1)} %add_convert_fusion.2), channel_id=1, source_target_pairs={{0,16},{4,20},{8,0},{12,4},{24,8},{28,12},{16,24},{20,28},{1,17},{... | collective-permute-start | bytes 884744 | tf_op jit(solution)/shard_map/ppermute | solution.py:586
  145.0 10.7 %collective-permute-start.47 = (bf16[96,1408]{1,0:T(8,128)(2,1)S(1)}, bf16[96,1408]{1,0:T(8,128)(2,1)S(1)}, u32[]{:S(2)}, u32[]{:S(2)}) collective-permute-start(bf16[96,1408]{1,0:T(8,128)(2,1)S(1)} %get-tuple-element.263), channel_id=1, source_target_pairs={{0,4},{4,0},{8,12},{12,8},{16,20},{20,16},{24,28},{28,24},{1,5},{5... | collective-permute-start | bytes 811016 | tf_op jit(solution)/shard_map/ppermute | solution.py:570
  146.0 12.5 %collective-permute-start.45 = (bf16[416,768]{1,0:T(8,128)(2,1)S(1)}, bf16[416,768]{1,0:T(8,128)(2,1)S(1)}, u32[]{:S(2)}, u32[]{:S(2)}) collective-permute-start(bf16[416,768]{1,0:T(8,128)(2,1)S(1)} %get-tuple-element.259), channel_id=1, source_target_pairs={{0,1},{1,0},{2,3},{3,2},{4,5},{5,4},{6,7},{7,6},{8,9},{9,8},{10,11... | collective-permute-start | bytes 1916936 | tf_op jit(solution)/shard_map/ppermute | solution.py:549
  158.7 14.1 %collective-permute-start.51 = (bf16[320,768]{1,0:T(8,128)(2,1)S(1)}, bf16[320,768]{1,0:T(8,128)(2,1)S(1)}, u32[]{:S(2)}, u32[]{:S(2)}) collective-permute-start(bf16[320,768]{1,0:T(8,128)(2,1)S(1)} %input_pair.1.sent), channel_id=1, source_target_pairs={{0,2},{1,3},{2,0},{3,1},{4,6},{5,7},{6,4},{7,5},{8,10},{9,11},{10,... | collective-permute-start | bytes 1474568 | tf_op jit(solution)/shard_map/ppermute | solution.py:549
  168.4 8.8 %collective-permute-start.57 = (bf16[96,1536]{1,0:T(8,128)(2,1)S(1)}, bf16[96,1536]{1,0:T(8,128)(2,1)S(1)}, u32[]{:S(2)}, u32[]{:S(2)}) collective-permute-start(bf16[96,1536]{1,0:T(8,128)(2,1)S(1)} %add_convert_fusion.1), channel_id=1, source_target_pairs={{0,2},{1,3},{2,0},{3,1},{4,6},{5,7},{6,4},{7,5},{8,10},{9,11},{10,... | collective-permute-start | bytes 884744 | tf_op jit(solution)/shard_map/ppermute | solution.py:549
  173.8 11.0 %collective-permute-start.56 = (bf16[96,1408]{1,0:T(8,128)(2,1)S(1)}, bf16[96,1408]{1,0:T(8,128)(2,1)S(1)}, u32[]{:S(2)}, u32[]{:S(2)}) collective-permute-start(bf16[96,1408]{1,0:T(8,128)(2,1)S(1)} %add_convert_fusion.4), channel_id=1, source_target_pairs={{0,16},{4,20},{8,0},{12,4},{24,8},{28,12},{16,24},{20,28},{1,17},{... | collective-permute-start | bytes 811016 | tf_op jit(solution)/shard_map/ppermute | solution.py:586
  175.1 9.8 %collective-permute-start.61 = (bf16[96,1408]{1,0:T(8,128)(2,1)S(1)}, bf16[96,1408]{1,0:T(8,128)(2,1)S(1)}, u32[]{:S(2)}, u32[]{:S(2)}) collective-permute-start(bf16[96,1408]{1,0:T(8,128)(2,1)S(1)} %get-tuple-element.290), channel_id=1, source_target_pairs={{0,4},{4,0},{8,12},{12,8},{16,20},{20,16},{24,28},{28,24},{1,5},{5... | collective-permute-start | bytes 811016 | tf_op jit(solution)/shard_map/ppermute | solution.py:570
  (63 other events, 415.2 us)

commit v3 on v2

--- a/solution.py
+++ b/solution.py
@@ -363,7 +363,10 @@
     low = d.astype(bf16)
     dc = [dot_nt(low, wo[block(wo, partner(k), wide)]).astype(bf16) for k in range(RANKS)]
     d0[...] = dc[0]
-    core[2 * width :, :wide] = dc[1]
+    base = 2 * scr.shape[1]
+    mine = dc[1].shape[0]
+    core[base : base + mine] = dc[1][:, :128]
+    core[base + mine :] = jnp.concatenate([dc[1][: mine // 2, 128:], dc[1][mine // 2 :, 128:]], 1)
     d2[...] = dc[2]
     d3[...] = dc[3]
     sums = jnp.concatenate(
@@ -371,17 +374,30 @@
         + [jnp.sum(dh, axis=0, keepdims=True), two[1:2], jnp.zeros((124, width), f32)],
         0,
     )
+    half = width // 2
     for k, c in enumerate((c0, c1, c2, c3)):
         g = dot_tn(c[...], low).astype(bf16)
-        at = block(scr, partner(k), wide)
+        q = partner(k)
+        tail = pl.ds(pl.multiple_of(width + lax.rem(q, 2) * wide, 64), wide)
         for t in range(RANKS):
-            scr[t, at, :wide] = g[:, wide * t : wide * t + wide]
-    vec = sums.T.astype(bf16)
+            scr[t, block(scr, q, wide)] = g[:, wide * t : wide * t + 128]
+        for side in (0, 1):
+
+            @pl.when(lax.div(q, 2) == side)
+            def _():
+                for t in range(RANKS):
+                    rest = g[:, wide * t + 128 : wide * t + wide]
+                    scr[t, tail, 64 * side : 64 * side + 64] = rest
+
+    low_sums = sums[:8].astype(bf16)
     for t in range(RANKS):
-        scr[t, :, wide:] = vec[:, :64]
+        for j in range(width // 128):
+            at = width + half + 8 * j
+            scr[t, at : at + 8] = low_sums[:, 128 * j : 128 * j + 128]
+    rows = scr.shape[1]
     w_own[...] = scr[partner(0)]
-    core[:width] = scr[partner(3)]
-    core[width : 2 * width] = scr[partner(1)]
+    core[:rows] = scr[partner(3)]
+    core[rows : 2 * rows] = scr[partner(1)]
     w_across[...] = scr[partner(2)]
 
 
@@ -393,8 +409,13 @@
     share = (rows - words) // RANKS
     hl = HEADS // RANKS
     dh = wide // hl
-    base = core.shape[0] - d0.shape[0]
-    for k, d in enumerate((d0[...], core[base:, :wide], d2[...], d3[...])):
+    mine = d0.shape[0]
+    base = core.shape[0] - mine * 3 // 2
+    tail = core[base + mine :]
+    d1 = jnp.concatenate(
+        [core[base : base + mine], jnp.concatenate([tail[:, :64], tail[:, 64:]], 0)], 1
+    )
+    for k, d in enumerate((d0[...], d1, d2[...], d3[...])):
         to = jnp.bitwise_xor(b, k)
         dc[block(dc, to, local)] = d[:local]
         dc[pl.ds(pl.multiple_of(words + to * share, share), share)] = d[local:]
@@ -449,7 +470,17 @@
     scr[:, :half] = w[:, :half].astype(bf16)
     scr[:, half : 2 * half] = (w[:, half:] + e[:, half:]).astype(bf16)
     scr[:, 2 * half : 3 * half] = e[:, :half].astype(bf16)
-    scr[:, 3 * half :] = (o0[...].astype(f32) + o1[out_rows : 2 * out_rows].astype(f32) + o2[...].astype(f32)).astype(bf16)
+    o = o0[...].astype(f32) + o1[out_rows : 2 * out_rows].astype(f32) + o2[...].astype(f32)
+    width = scr.shape[0]
+    middle = width // 2
+    tail = o[width : width + middle]
+    scr[:, 3 * half : 3 * half + 128] = o[:width].astype(bf16)
+    scr[:middle, 3 * half + 128 : 3 * half + 192] = tail[:, :64].astype(bf16)
+    scr[middle:, 3 * half + 128 : 3 * half + 192] = tail[:, 64:].astype(bf16)
+    vec = o[width + middle :]
+    sums = jnp.concatenate([vec[8 * j : 8 * j + 8] for j in range(width // 128)], 1)
+    sums = jnp.concatenate([sums, jnp.zeros((120, width), f32)], 0).T
+    scr[:, 3 * half + 192 :] = sums[:, :64].astype(bf16)
     for j, out in enumerate(outs):
         to = ring_seat(j // 2, j % 2) if len(outs) > 1 else 0
         out[...] = scr[block(scr, to, out.shape[0])]
@@ -749,13 +780,13 @@
         [((width, width), bf16)],
         [pltpu.VMEM((RANKS, width * 3 // 2, 128), bf16)],
     )
-    (wo,) = join_out(*wos)
+    (wo,) = join_out(*(after(wos, f3) if direct else wos))
     mix = call(
         mix_body,
         "mix",
         [((mine, width), bf16), ((mine, width), f32), ((mine, 1), f32)],
     )
-    hr, n1, i1 = mix(*ctx, after(wo, f3) if direct else wo, norms, xw_own, xe)
+    hr, n1, i1 = mix(*ctx, wo, norms, xw_own, xe)
 
     def place_ff(slots, *args):
         outs = [((width, ff), bf16), ((ff, width), bf16)]
@@ -818,33 +849,32 @@
         us=3,
         vmem=16,
     )
-    ff_chunks = feed_grads(*ds, *hs, g_all, dz_near, dz_far)
-    sent = plus(across, after(core, ff_chunks)[0])
+    sent = plus(across, core[0])
+    ff_chunks = feed_grads(*ds, *hs, g_all, dz_near, after(dz_far, sent))
     dhs = [own, core, swap_ff(sent, 2, direct)]
     if direct:
         ff0, ff1, ff2, ff3, ff4, ff5, ff6, ff7 = ff_chunks
         fy, fz = swap(ff5, 2), along_ring(ff2)
-        part = plus(ff4, fy)
-        dhs[2] = after(dhs[2], part, fz)
+        part = plus(ff4, after(fy, fz))
+        dhs[2] = after(dhs[2], ff_chunks)
         fl = along_ring(part, -1)
 
+    packed = width * 3 // 2 + 8 * (width // 128)
     norm_one = call(
         norm_one_body,
         "norm_one",
         [((mine, wide), bf16)] * 3
-        + [((2 * width + mine, wide + 64), bf16), ((mine, width), f32)]
-        + [((width, wide + 64), bf16)] * 2,
-        [pltpu.VMEM((RANKS, width, wide + 64), bf16)],
+        + [((2 * packed + mine * 3 // 2, 128), bf16), ((mine, width), f32)]
+        + [((packed, 128), bf16)] * 2,
+        [pltpu.VMEM((RANKS, packed, 128), bf16)],
         vmem=12,
     )
     d0, d2, d3, core, du1, wo_own, across = norm_one(
         *dhs, du2, n1, i1, norms, sums, wo, *ctx
     )
     dcs = [d0, swap(core, 1), swap(d2, 2), swap(d3, 3)]
-    sent = plus(across, after(dcs[1], dcs[2], dcs[3])[:width])
+    sent = plus(across, after(dcs[1], dcs[2], dcs[3])[:packed])
     outs = [wo_own, dcs[1], swap(sent, 2)]
-    if direct:
-        fb, fc = along_ring(after(ff3, du1)), along_ring(after(ff7, du1), -1)
     dcs = after(dcs, sent)
     attend_back = call(
         lambda *r: attend_back_body(factor, *r),
@@ -867,7 +897,6 @@
     own, across, core = to_input(dqkv, wq, du1, ye)
     if direct:
         own = after(own, fl)
-        fl = along_ring(plus(ff6, after(fl, dqkv)), -1)
     core = swap(core, 1)
     proj_grads = call(
         proj_grads_body,
@@ -879,8 +908,9 @@
     )
     chunks = proj_grads(after(dqkv, own), xw, xe, *outs)
     if direct:
-        part = plus(chunks[2], after(over_x(chunks[3]), fl, fb, fc))
-        fy = swap(plus(ff1, fb, after(fc, part)), 2)
+        fl = along_ring(plus(ff6, after(fl, dqkv)), -1)
+        fb, fc = along_ring(after(ff3, chunks)), along_ring(after(ff7, chunks), -1)
+        part = plus(chunks[2], after(over_x(chunks[3]), fl, fb))
         cx, cz = over_x(after(chunks[5], part)), along_ring(part, -1)
         core = after(core, part)
     (sent,) = call(input_pair_body, "input_pair", [((local + ents + 2 * share, width), bf16)])(across, core)
@@ -902,9 +932,10 @@
         )
         part = plus(chunks[4], cz, cx)
         cx, cz = over_x(after(chunks[7], part)), along_ring(part, -1)
-        grad_ff_out, *back = last_ff(ff0, fz, fl, after(fy, part))
+        fy_last = swap(plus(ff1, fb, after(fc, part)), 2)
         part = plus(chunks[6], after(cz, came), cx)
         cx, cz = over_x(after(chunks[1], part)), along_ring(part, -1)
+        grad_ff_out, *back = last_ff(ff0, fz, fl, after(fy_last, part))
         back = [back[0]] + [swap_ff(back[k], k, direct) for k in (1, 2, 3)]
         spread_ff = call(
             spread_ff_body,

time: 192 us -> 191 us (level)
  waiting for transfers between devices: 89.1 us -> 84.2 us
  starting transfers between devices: 57.2 us -> 59.8 us
    ppermute x34, waiting for transfers between devices: 28.8 us -> 17.6 us  [swap(): return lax.ppermute(x, 'blk', [(i, i ^ k) for i in range(RANKS)])]
    ppermute x15, waiting for transfers between devices: 23.2 us -> 26.8 us  [along_ring(): lax.ppermute(x, 'seq', [(2 * z + i, 2 * to + i) for z, to in route for i...]
    ppermute x14, waiting for transfers between devices: 36.6 us -> 39.8 us  [over_x(): return lax.ppermute(x, 'seq', [(i, i ^ 1) for i in range(8)])]
  transfers between devices with their start and end apart: 65 -> 65, of which waited for: 33 -> 34; matrix products, arithmetic and copies ran while one was open for 1% -> 1% of each run, Pallas kernels for 12% -> 13%
where the time goes in v3:
time: 191 us; the launch traced here: 190 us
  waiting for transfers between devices  84.2 us (44%)
  starting transfers between devices  59.8 us (31%)
  Pallas kernels  34.7 us (18%)
  local copies, waits for them, and re-layouts  9.02 us (5%)
    ppermute x14, waiting for transfers between devices, over_x(): return lax.ppermute(x, 'seq', [(i, i ^ 1) for i in range(8)])  39.8 us
    pallas_call x28, Pallas kernels, run(): pl.pallas_call(body, name=name, out_shape=[jax.ShapeDtypeStruct(s, t) for...  34.7 us
    ppermute x15, waiting for transfers between devices, along_ring(): lax.ppermute(x, 'seq', [(2 * z + i, 2 * to + i) for z, to in route for i...  26.8 us
    ppermute x15, starting transfers between devices, along_ring(): lax.ppermute(x, 'seq', [(2 * z + i, 2 * to + i) for z, to in route for i...  21.7 us
    ppermute x34, starting transfers between devices, swap(): return lax.ppermute(x, 'blk', [(i, i ^ k) for i in range(RANKS)])  21.5 us
    ppermute x34, waiting for transfers between devices, swap(): return lax.ppermute(x, 'blk', [(i, i ^ k) for i in range(RANKS)])  17.6 us
    ppermute x14, starting transfers between devices, over_x(): return lax.ppermute(x, 'seq', [(i, i ^ 1) for i in range(8)])  14.9 us
    unnamed x44, local copies, waits for them, and re-layouts  7.59 us
  transfers between devices with their start and end apart: 65, of which 34 were waited for; matrix products, arithmetic and copies ran while one was open for 1% of the time, Pallas kernels for 13%

profile of v3, /device:TPU:0, one launch (start us, length us, event | category | flops | bytes accessed | tf_op | source)
XLA Modules:
  0.0 190.2 jit_solution(4134912501221137936)
XLA Ops:
  3.2 2.6 %collective-permute-start.1 = (bf16[24,1408]{1,0:T(8,128)(2,1)}, bf16[24,1408]{1,0:T(8,128)(2,1)S(1)}, u32[]{:S(2)}, u32[]{:S(2)}) collective-permute-start(bf16[24,1408]{1,0:T(8,128)(2,1)} %get-tuple-element.162), channel_id=1, source_target_pairs={{0,2},{1,3},{2,0},{3,1},{4,6},{5,7},{6,4},{7,5},{8,10},{9,11},{10,... | collective-permute-start | bytes 202760 | tf_op jit(solution)/shard_map/ppermute | solution.py:580
  14.9 3.9 %collective-permute-done.4.r_1_ = bf16[96,1408]{1,0:T(8,128)(2,1)S(1)} collective-permute-done((bf16[96,1408]{1,0:T(8,128)(2,1)S(1)}, bf16[96,1408]{1,0:T(8,128)(2,1)S(1)}, u32[]{:S(2)}, u32[]{:S(2)}) %collective-permute-start.4) | collective-permute-done | bytes 270368 | tf_op jit(solution)/shard_map/ppermute | solution.py:601
  18.8 2.1 %collective-permute-done.3.r_2_ = bf16[96,1408]{1,0:T(8,128)(2,1)S(1)} collective-permute-done((bf16[96,1408]{1,0:T(8,128)(2,1)S(1)}, bf16[96,1408]{1,0:T(8,128)(2,1)S(1)}, u32[]{:S(2)}, u32[]{:S(2)}) %collective-permute-start.3) | collective-permute-done | bytes 270368 | tf_op jit(solution)/shard_map/ppermute | solution.py:617
  26.7 2.8 %collective-permute-done.9.p2 = bf16[24,768]{1,0:T(8,128)(2,1)S(1)} collective-permute-done((bf16[24,768]{1,0:T(8,128)(2,1)S(1)}, bf16[24,768]{1,0:T(8,128)(2,1)S(1)}, u32[]{:S(2)}, u32[]{:S(2)}) %collective-permute-start.9) | collective-permute-done | bytes 36896 | tf_op jit(solution)/shard_map/ppermute | solution.py:601
  35.5 3.4 %collective-permute-done.13.r_3_ = bf16[96,1408]{1,0:T(8,128)(2,1)S(1)} collective-permute-done((bf16[96,1408]{1,0:T(8,128)(2,1)S(1)}, bf16[96,1408]{1,0:T(8,128)(2,1)S(1)}, u32[]{:S(2)}, u32[]{:S(2)}) %collective-permute-start.13) | collective-permute-done | bytes 270368 | tf_op jit(solution)/shard_map/ppermute | solution.py:601
  50.4 2.4 %collective-permute-start.24 = (bf16[96,1536]{1,0:T(8,128)(2,1)}, bf16[96,1536]{1,0:T(8,128)(2,1)}, u32[]{:S(2)}, u32[]{:S(2)}) collective-permute-start(bf16[96,1536]{1,0:T(8,128)(2,1)} %collective-permute-done.16.r_2_), channel_id=1, source_target_pairs={{0,8},{4,12},{8,24},{12,28},{24,16},{28,20},{16,0},{20,4},{1,9},{5... | collective-permute-start | bytes 884744 | tf_op jit(solution)/shard_map/ppermute | solution.py:617
  54.6 4.8 %attend.1 = (bf16[160,192]{1,0:T(8,128)(2,1)S(1)}, bf16[160,192]{1,0:T(8,128)(2,1)S(1)}, bf16[160,192]{1,0:T(8,128)(2,1)S(1)}, bf16[160,192]{1,0:T(8,128)(2,1)S(...) custom-call(bf16[512,768]{1,0:T(8,128)(2,1)S(1)} %join_rows.1.r_0_.x, ...), custom_call_target="tpu_custom_call" | custom-call | flops 7000000 | bytes 7000 | tf_op jit(solution)/shard_map/attend/pallas_call | solution.py:34
  67.1 4.6 %collective-permute-done.25.r_5_ = bf16[96,1536]{1,0:T(8,128)(2,1)S(1)} collective-permute-done((bf16[96,1536]{1,0:T(8,128)(2,1)}, bf16[96,1536]{1,0:T(8,128)(2,1)S(1)}, u32[]{:S(2)}, u32[]{:S(2)}) %collective-permute-start.25) | collective-permute-done | bytes 294944 | tf_op jit(solution)/shard_map/ppermute | solution.py:617
  78.7 2.9 %collective-permute-done.27.h2 = bf16[160,768]{1,0:T(8,128)(2,1)S(1)} collective-permute-done((bf16[160,768]{1,0:T(8,128)(2,1)S(1)}, bf16[160,768]{1,0:T(8,128)(2,1)S(1)}, u32[]{:S(2)}, u32[]{:S(2)}) %collective-permute-start.27) | collective-permute-done | bytes 245792 | tf_op jit(solution)/shard_map/ppermute | solution.py:601
  83.7 2.3 %feed.1 = (f32[160,768]{1,0:T(8,128)S(1)}, bf16[160,768]{1,0:T(8,128)(2,1)S(1)}, bf16[2,160,768]{2,1,0:T(8,128)(2,1)S(1)}, bf16[4,160,768]{2,1,0:T(8,128)(2,1)S(1)}, bf16[4,160,768]{2,1,0:T(8,128)(2,1)S(1)}) custom-call(bf16[160,768]{1,0:T(8,128)(2,1)S(1)} %get-tuple-element.210.h0, bf16[160,768]{1,0:T(8,128)(2,1)S(1)} %collective-permute-done.26.h1, ...), custom_call_target="tpu_custom_call" | custom-call | flops 3000000 | bytes 3000 | tf_op jit(solution)/shard_map/feed/pallas_call | solution.py:34
  89.1 7.0 %collective-permute-done.33.f2 = bf16[160,768]{1,0:T(8,128)(2,1)S(1)} collective-permute-done((bf16[160,768]{1,0:T(8,128)(2,1)S(1)}, bf16[160,768]{1,0:T(8,128)(2,1)S(1)}, u32[]{:S(2)}, u32[]{:S(2)}) %collective-permute-start.33) | collective-permute-done | bytes 245792 | tf_op jit(solution)/shard_map/ppermute | solution.py:601
  98.2 6.1 %collective-permute-done.35.d2 = bf16[160,768]{1,0:T(8,128)(2,1)S(1)} collective-permute-done((bf16[160,768]{1,0:T(8,128)(2,1)S(1)}, bf16[160,768]{1,0:T(8,128)(2,1)S(1)}, u32[]{:S(2)}, u32[]{:S(2)}) %collective-permute-start.35) | collective-permute-done | bytes 245792 | tf_op jit(solution)/shard_map/ppermute | solution.py:601
  110.8 2.1 %feed_grads.1 = (bf16[96,1536]{1,0:T(8,128)(2,1)S(1)}, bf16[96,1536]{1,0:T(8,128)(2,1)S(1)}, bf16[96,1536]{1,0:T(8,128)(2,1)S(1)}, bf16[96,1536]{1,0:T(8,128)(2,...) custom-call(bf16[160,768]{1,0:T(8,128)(2,1)S(1)} %get-tuple-element., ...), custom_call_target="tpu_custom_call" | custom-call | flops 3000000 | bytes 3000 | tf_op jit(solution)/shard_map/feed_grads/pallas_call | solution.py:34
  118.0 2.6 %norm_one.1 = (bf16[160,192]{1,0:T(8,128)(2,1)S(1)}, bf16[160,192]{1,0:T(8,128)(2,1)S(1)}, bf16[160,192]{1,0:T(8,128)(2,1)S(1)}, bf16[2640,128]{1,0:T(8,128)(2,1...) custom-call(f32[160,768]{1,0:T(8,128)S(1)} %get-tuple-element.227.h0, ...), custom_call_target="tpu_custom_call" | custom-call | flops 1000000 | bytes 1000 | tf_op jit(solution)/shard_map/norm_one/pallas_call | solution.py:34
  128.5 4.9 %attend_back.1.dqkv = bf16[640,768]{1,0:T(8,128)(2,1)S(1)} custom-call(bf16[160,192]{1,0:T(8,128)(2,1)S(1)} %get-tuple-element.253.r_0_, bf16[2640,128]{1,0:T(8,128)(2,1)S(1)} %collective-permute-done.39.r_1_.o1, bf16[160,192]{1,0:T(8,128)(2,1)S(1)} %collective-permute-done.40.r_2_, bf16[160,192]{1,0:T(8,128)(2,1)S(1)} %collective-permute-done.41.r_3_, ...), custom_call_target="tpu_custom_call" | custom-call | flops 7000000 | bytes 7000 | tf_op jit(solution)/shard_map/attend_back/pallas_call | solution.py:34
  137.8 2.0 %collective-permute-start.49 = (bf16[96,1536]{1,0:T(8,128)(2,1)S(1)}, bf16[96,1536]{1,0:T(8,128)(2,1)S(1)}, u32[]{:S(2)}, u32[]{:S(2)}) collective-permute-start(bf16[96,1536]{1,0:T(8,128)(2,1)S(1)} %get-tuple-element.279), channel_id=1, source_target_pairs={{0,8},{4,12},{8,24},{12,28},{24,16},{28,20},{16,0},{20,4},{1,9},{5... | collective-permute-start | bytes 884744 | tf_op jit(solution)/shard_map/ppermute | solution.py:617
  140.8 3.1 %collective-permute-done.48.a2 = bf16[96,1536]{1,0:T(8,128)(2,1)S(1)} collective-permute-done((bf16[96,1536]{1,0:T(8,128)(2,1)S(1)}, bf16[96,1536]{1,0:T(8,128)(2,1)S(1)}, u32[]{:S(2)}, u32[]{:S(2)}) %collective-permute-start.48) | collective-permute-done | bytes 294944 | tf_op jit(solution)/shard_map/ppermute | solution.py:617
  143.9 3.5 %collective-permute-done.47 = bf16[96,1408]{1,0:T(8,128)(2,1)S(1)} collective-permute-done((bf16[96,1408]{1,0:T(8,128)(2,1)S(1)}, bf16[96,1408]{1,0:T(8,128)(2,1)S(1)}, u32[]{:S(2)}, u32[]{:S(2)}) %collective-permute-start.47) | collective-permute-done | bytes 270368 | tf_op jit(solution)/shard_map/ppermute | solution.py:601
  147.4 4.8 %collective-permute-done.49 = bf16[96,1536]{1,0:T(8,128)(2,1)S(1)} collective-permute-done((bf16[96,1536]{1,0:T(8,128)(2,1)S(1)}, bf16[96,1536]{1,0:T(8,128)(2,1)S(1)}, u32[]{:S(2)}, u32[]{:S(2)}) %collective-permute-start.49) | collective-permute-done | bytes 294944 | tf_op jit(solution)/shard_map/ppermute | solution.py:617
  156.5 4.2 %collective-permute-done.52 = bf16[96,1408]{1,0:T(8,128)(2,1)S(1)} collective-permute-done((bf16[96,1408]{1,0:T(8,128)(2,1)S(1)}, bf16[96,1408]{1,0:T(8,128)(2,1)S(1)}, u32[]{:S(2)}, u32[]{:S(2)}) %collective-permute-start.52) | collective-permute-done | bytes 270368 | tf_op jit(solution)/shard_map/ppermute | solution.py:601
  165.5 3.6 %collective-permute-done.56 = bf16[96,1536]{1,0:T(8,128)(2,1)S(1)} collective-permute-done((bf16[96,1536]{1,0:T(8,128)(2,1)S(1)}, bf16[96,1536]{1,0:T(8,128)(2,1)S(1)}, u32[]{:S(2)}, u32[]{:S(2)}) %collective-permute-start.56) | collective-permute-done | bytes 294944 | tf_op jit(solution)/shard_map/ppermute | solution.py:617
  169.8 3.7 %collective-permute-done.53 = bf16[96,1408]{1,0:T(8,128)(2,1)S(1)} collective-permute-done((bf16[96,1408]{1,0:T(8,128)(2,1)S(1)}, bf16[96,1408]{1,0:T(8,128)(2,1)S(1)}, u32[]{:S(2)}, u32[]{:S(2)}) %collective-permute-start.53) | collective-permute-done | bytes 270368 | tf_op jit(solution)/shard_map/ppermute | solution.py:617
  179.8 3.0 %collective-permute-done.59.c2 = bf16[24,768]{1,0:T(8,128)(2,1)S(1)} collective-permute-done((bf16[24,768]{1,0:T(8,128)(2,1)S(1)}, bf16[24,768]{1,0:T(8,128)(2,1)S(1)}, u32[]{:S(2)}, u32[]{:S(2)}) %collective-permute-start.59) | collective-permute-done | bytes 36896 | tf_op jit(solution)/shard_map/ppermute | solution.py:601
  185.8 3.3 %collective-permute-done.63.c2 = bf16[24,1408]{1,0:T(8,128)(2,1)S(1)} collective-permute-done((bf16[24,1408]{1,0:T(8,128)(2,1)S(1)}, bf16[24,1408]{1,0:T(8,128)(2,1)S(1)}, u32[]{:S(2)}, u32[]{:S(2)}) %collective-permute-start.63) | collective-permute-done | bytes 67616 | tf_op jit(solution)/shard_map/ppermute | solution.py:580
  (193 shorter events, 102.8 us)
Async XLA Ops:
  11.8 9.1 %collective-permute-start.3 = (bf16[96,1408]{1,0:T(8,128)(2,1)S(1)}, bf16[96,1408]{1,0:T(8,128)(2,1)S(1)}, u32[]{:S(2)}, u32[]{:S(2)}) collective-permute-start(bf16[96,1408]{1,0:T(8,128)(2,1)S(1)} %arrange.1.r_0_), channel_id=1, source_target_pairs={{0,8},{4,12},{8,24},{12,28},{24,16},{28,20},{16,0},{20,4},{1,9},{5... | collective-permute-start | bytes 811016 | tf_op jit(solution)/shard_map/ppermute | solution.py:617
  13.6 16.0 %collective-permute-start.11 = (bf16[128,768]{1,0:T(8,128)(2,1)S(1)}, bf16[128,768]{1,0:T(8,128)(2,1)S(1)}, u32[]{:S(2)}, u32[]{:S(2)}) collective-permute-start(bf16[128,768]{1,0:T(8,128)(2,1)S(1)} %bitcast.46), channel_id=1, source_target_pairs={{0,2},{1,3},{2,0},{3,1},{4,6},{5,7},{6,4},{7,5},{8,10},{9,11},{10,... | collective-permute-start | bytes 589832 | tf_op jit(solution)/shard_map/ppermute | solution.py:580
  21.5 8.8 %collective-permute-start.6 = (bf16[96,1408]{1,0:T(8,128)(2,1)S(1)}, bf16[96,1408]{1,0:T(8,128)(2,1)S(1)}, u32[]{:S(2)}, u32[]{:S(2)}) collective-permute-start(bf16[96,1408]{1,0:T(8,128)(2,1)S(1)} %collective-permute-done.3.r_2_), channel_id=1, source_target_pairs={{0,8},{4,12},{8,24},{12,28},{24,16},{28,20},{16,0},{20,4},{1,9},{5... | collective-permute-start | bytes 811016 | tf_op jit(solution)/shard_map/ppermute | solution.py:617
  31.0 9.4 %collective-permute-start.12 = (bf16[96,1408]{1,0:T(8,128)(2,1)S(1)}, bf16[96,1408]{1,0:T(8,128)(2,1)S(1)}, u32[]{:S(2)}, u32[]{:S(2)}) collective-permute-start(bf16[96,1408]{1,0:T(8,128)(2,1)S(1)} %collective-permute-done.6.r_4_), channel_id=1, source_target_pairs={{0,8},{4,12},{8,24},{12,28},{24,16},{28,20},{16,0},{20,4},{1,9},{5... | collective-permute-start | bytes 811016 | tf_op jit(solution)/shard_map/ppermute | solution.py:617
  34.0 13.1 %collective-permute-start.17 = (bf16[96,1536]{1,0:T(8,128)(2,1)S(1)}, bf16[96,1536]{1,0:T(8,128)(2,1)S(1)}, u32[]{:S(2)}, u32[]{:S(2)}) collective-permute-start(bf16[96,1536]{1,0:T(8,128)(2,1)S(1)} %arrange_ff.1.r_0_), channel_id=1, source_target_pairs={{0,2},{1,3},{2,0},{3,1},{4,6},{5,7},{6,4},{7,5},{8,10},{9,11},{10,... | collective-permute-start | bytes 884744 | tf_op jit(solution)/shard_map/ppermute | solution.py:580
  40.3 9.2 %collective-permute-start.16 = (bf16[96,1536]{1,0:T(8,128)(2,1)S(1)}, bf16[96,1536]{1,0:T(8,128)(2,1)}, u32[]{:S(2)}, u32[]{:S(2)}) collective-permute-start(bf16[96,1536]{1,0:T(8,128)(2,1)S(1)} %arrange_ff.1.r_0_), channel_id=1, source_target_pairs={{0,8},{4,12},{8,24},{12,28},{24,16},{28,20},{16,0},{20,4},{1,9},{5... | collective-permute-start | bytes 884744 | tf_op jit(solution)/shard_map/ppermute | solution.py:617
  50.4 9.0 %collective-permute-start.18 = (bf16[1152,128]{1,0:T(8,128)(2,1)}, bf16[1152,128]{1,0:T(8,128)(2,1)}, u32[]{:S(2)}, u32[]{:S(2)}) collective-permute-start(bf16[1152,128]{1,0:T(8,128)(2,1)} %get-tuple-element.205.w0), channel_id=1, source_target_pairs={{0,1},{1,0},{2,3},{3,2},{4,5},{5,4},{6,7},{7,6},{8,9},{9,8},{10,11... | collective-permute-start | bytes 884744 | tf_op jit(solution)/shard_map/ppermute | solution.py:580
  50.4 10.9 %collective-permute-start.24 = (bf16[96,1536]{1,0:T(8,128)(2,1)}, bf16[96,1536]{1,0:T(8,128)(2,1)}, u32[]{:S(2)}, u32[]{:S(2)}) collective-permute-start(bf16[96,1536]{1,0:T(8,128)(2,1)} %collective-permute-done.16.r_2_), channel_id=1, source_target_pairs={{0,8},{4,12},{8,24},{12,28},{24,16},{28,20},{16,0},{20,4},{1,9},{5... | collective-permute-start | bytes 884744 | tf_op jit(solution)/shard_map/ppermute | solution.py:617
  52.8 10.4 %collective-permute-start.22 = (bf16[1152,128]{1,0:T(8,128)(2,1)}, bf16[1152,128]{1,0:T(8,128)(2,1)}, u32[]{:S(2)}, u32[]{:S(2)}) collective-permute-start(bf16[1152,128]{1,0:T(8,128)(2,1)} %get-tuple-element.205.w0), channel_id=1, source_target_pairs={{0,2},{1,3},{2,0},{3,1},{4,6},{5,7},{6,4},{7,5},{8,10},{9,11},{10,... | collective-permute-start | bytes 884744 | tf_op jit(solution)/shard_map/ppermute | solution.py:580
  61.4 10.4 %collective-permute-start.25 = (bf16[96,1536]{1,0:T(8,128)(2,1)}, bf16[96,1536]{1,0:T(8,128)(2,1)S(1)}, u32[]{:S(2)}, u32[]{:S(2)}) collective-permute-start(bf16[96,1536]{1,0:T(8,128)(2,1)} %collective-permute-done.24.r_4_), channel_id=1, source_target_pairs={{0,8},{4,12},{8,24},{12,28},{24,16},{28,20},{16,0},{20,4},{1,9},{5... | collective-permute-start | bytes 884744 | tf_op jit(solution)/shard_map/ppermute | solution.py:617
  66.2 11.3 %collective-permute-start.28 = (bf16[96,1536]{1,0:T(8,128)(2,1)}, bf16[96,1536]{1,0:T(8,128)(2,1)S(1)}, u32[]{:S(2)}, u32[]{:S(2)}) collective-permute-start(bf16[96,1536]{1,0:T(8,128)(2,1)} %collective-permute-done.16.r_2_), channel_id=1, source_target_pairs={{0,2},{1,3},{2,0},{3,1},{4,6},{5,7},{6,4},{7,5},{8,10},{9,11},{10,... | collective-permute-start | bytes 884744 | tf_op jit(solution)/shard_map/ppermute | solution.py:580
  112.9 9.9 %collective-permute-start.43 = (bf16[96,1536]{1,0:T(8,128)(2,1)S(1)}, bf16[96,1536]{1,0:T(8,128)(2,1)S(1)}, u32[]{:S(2)}, u32[]{:S(2)}) collective-permute-start(bf16[96,1536]{1,0:T(8,128)(2,1)S(1)} %get-tuple-element.237), channel_id=1, source_target_pairs={{0,8},{4,12},{8,24},{12,28},{24,16},{28,20},{16,0},{20,4},{1,9},{5... | collective-permute-start | bytes 884744 | tf_op jit(solution)/shard_map/ppermute | solution.py:617
  123.7 11.0 %collective-permute-start.44 = (bf16[96,1536]{1,0:T(8,128)(2,1)S(1)}, bf16[96,1536]{1,0:T(8,128)(2,1)S(1)}, u32[]{:S(2)}, u32[]{:S(2)}) collective-permute-start(bf16[96,1536]{1,0:T(8,128)(2,1)S(1)} %add_convert_fusion.3), channel_id=1, source_target_pairs={{0,16},{4,20},{8,0},{12,4},{24,8},{28,12},{16,24},{20,28},{1,17},{... | collective-permute-start | bytes 884744 | tf_op jit(solution)/shard_map/ppermute | solution.py:617
  127.1 9.4 %collective-permute-start.46 = (bf16[1200,128]{1,0:T(8,128)(2,1)S(1)}, bf16[1200,128]{1,0:T(8,128)(2,1)S(1)}, u32[]{:S(2)}, u32[]{:S(2)}) collective-permute-start(bf16[1200,128]{1,0:T(8,128)(2,1)S(1)} %add_convert_fusion), channel_id=1, source_target_pairs={{0,2},{1,3},{2,0},{3,1},{4,6},{5,7},{6,4},{7,5},{8,10},{9,11},{10,... | collective-permute-start | bytes 921608 | tf_op jit(solution)/shard_map/ppermute | solution.py:580
  134.8 9.1 %collective-permute-start.48 = (bf16[96,1536]{1,0:T(8,128)(2,1)S(1)}, bf16[96,1536]{1,0:T(8,128)(2,1)S(1)}, u32[]{:S(2)}, u32[]{:S(2)}) collective-permute-start(bf16[96,1536]{1,0:T(8,128)(2,1)S(1)} %add_convert_fusion.2), channel_id=1, source_target_pairs={{0,16},{4,20},{8,0},{12,4},{24,8},{28,12},{16,24},{20,28},{1,17},{... | collective-permute-start | bytes 884744 | tf_op jit(solution)/shard_map/ppermute | solution.py:617
  137.8 14.4 %collective-permute-start.49 = (bf16[96,1536]{1,0:T(8,128)(2,1)S(1)}, bf16[96,1536]{1,0:T(8,128)(2,1)S(1)}, u32[]{:S(2)}, u32[]{:S(2)}) collective-permute-start(bf16[96,1536]{1,0:T(8,128)(2,1)S(1)} %get-tuple-element.279), channel_id=1, source_target_pairs={{0,8},{4,12},{8,24},{12,28},{24,16},{28,20},{16,0},{20,4},{1,9},{5... | collective-permute-start | bytes 884744 | tf_op jit(solution)/shard_map/ppermute | solution.py:617
  140.8 14.0 %collective-permute-start.45 = (bf16[416,768]{1,0:T(8,128)(2,1)S(1)}, bf16[416,768]{1,0:T(8,128)(2,1)S(1)}, u32[]{:S(2)}, u32[]{:S(2)}) collective-permute-start(bf16[416,768]{1,0:T(8,128)(2,1)S(1)} %get-tuple-element.267), channel_id=1, source_target_pairs={{0,1},{1,0},{2,3},{3,2},{4,5},{5,4},{6,7},{7,6},{8,9},{9,8},{10,11... | collective-permute-start | bytes 1916936 | tf_op jit(solution)/shard_map/ppermute | solution.py:580
  153.3 9.4 %collective-permute-start.51 = (bf16[96,1408]{1,0:T(8,128)(2,1)S(1)}, bf16[96,1408]{1,0:T(8,128)(2,1)S(1)}, u32[]{:S(2)}, u32[]{:S(2)}) collective-permute-start(bf16[96,1408]{1,0:T(8,128)(2,1)S(1)} %add_convert_fusion.6), channel_id=1, source_target_pairs={{0,16},{4,20},{8,0},{12,4},{24,8},{28,12},{16,24},{20,28},{1,17},{... | collective-permute-start | bytes 811016 | tf_op jit(solution)/shard_map/ppermute | solution.py:617
  154.0 15.1 %collective-permute-start.56 = (bf16[96,1536]{1,0:T(8,128)(2,1)S(1)}, bf16[96,1536]{1,0:T(8,128)(2,1)S(1)}, u32[]{:S(2)}, u32[]{:S(2)}) collective-permute-start(bf16[96,1536]{1,0:T(8,128)(2,1)S(1)} %get-tuple-element.290), channel_id=1, source_target_pairs={{0,16},{4,20},{8,0},{12,4},{24,8},{28,12},{16,24},{20,28},{1,17},{... | collective-permute-start | bytes 884744 | tf_op jit(solution)/shard_map/ppermute | solution.py:617
  154.9 14.9 %collective-permute-start.50 = (bf16[320,768]{1,0:T(8,128)(2,1)S(1)}, bf16[320,768]{1,0:T(8,128)(2,1)S(1)}, u32[]{:S(2)}, u32[]{:S(2)}) collective-permute-start(bf16[320,768]{1,0:T(8,128)(2,1)S(1)} %input_pair.1.sent), channel_id=1, source_target_pairs={{0,2},{1,3},{2,0},{3,1},{4,6},{5,7},{6,4},{7,5},{8,10},{9,11},{10,... | collective-permute-start | bytes 1474568 | tf_op jit(solution)/shard_map/ppermute | solution.py:580
  162.9 10.7 %collective-permute-start.53 = (bf16[96,1408]{1,0:T(8,128)(2,1)S(1)}, bf16[96,1408]{1,0:T(8,128)(2,1)S(1)}, u32[]{:S(2)}, u32[]{:S(2)}) collective-permute-start(bf16[96,1408]{1,0:T(8,128)(2,1)S(1)} %add_convert_fusion.5), channel_id=1, source_target_pairs={{0,16},{4,20},{8,0},{12,4},{24,8},{28,12},{16,24},{20,28},{1,17},{... | collective-permute-start | bytes 811016 | tf_op jit(solution)/shard_map/ppermute | solution.py:617
  164.4 9.1 %collective-permute-start.54 = (bf16[96,1408]{1,0:T(8,128)(2,1)S(1)}, bf16[96,1408]{1,0:T(8,128)(2,1)S(1)}, u32[]{:S(2)}, u32[]{:S(2)}) collective-permute-start(bf16[96,1408]{1,0:T(8,128)(2,1)S(1)} %get-tuple-element.285), channel_id=1, source_target_pairs={{0,4},{4,0},{8,12},{12,8},{16,20},{20,16},{24,28},{28,24},{1,5},{5... | collective-permute-start | bytes 811016 | tf_op jit(solution)/shard_map/ppermute | solution.py:601
  173.7 10.0 %collective-permute-start.55 = (bf16[96,1408]{1,0:T(8,128)(2,1)S(1)}, bf16[96,1408]{1,0:T(8,128)(2,1)S(1)}, u32[]{:S(2)}, u32[]{:S(2)}) collective-permute-start(bf16[96,1408]{1,0:T(8,128)(2,1)S(1)} %add_convert_fusion.4), channel_id=1, source_target_pairs={{0,16},{4,20},{8,0},{12,4},{24,8},{28,12},{16,24},{20,28},{1,17},{... | collective-permute-start | bytes 811016 | tf_op jit(solution)/shard_map/ppermute | solution.py:617
  174.9 8.7 %collective-permute-start.61 = (bf16[96,1408]{1,0:T(8,128)(2,1)S(1)}, bf16[96,1408]{1,0:T(8,128)(2,1)S(1)}, u32[]{:S(2)}, u32[]{:S(2)}) collective-permute-start(bf16[96,1408]{1,0:T(8,128)(2,1)S(1)} %get-tuple-element.298), channel_id=1, source_target_pairs={{0,4},{4,0},{8,12},{12,8},{16,20},{20,16},{24,28},{28,24},{1,5},{5... | collective-permute-start | bytes 811016 | tf_op jit(solution)/shard_map/ppermute | solution.py:601
  (63 other events, 410.5 us)

commit v4 on v3

--- a/solution.py
+++ b/solution.py
@@ -909,8 +909,9 @@
     chunks = proj_grads(after(dqkv, own), xw, xe, *outs)
     if direct:
         fl = along_ring(plus(ff6, after(fl, dqkv)), -1)
-        fb, fc = along_ring(after(ff3, chunks)), along_ring(after(ff7, chunks), -1)
-        part = plus(chunks[2], after(over_x(chunks[3]), fl, fb))
+        fb = along_ring(after(ff3, chunks))
+        part = plus(chunks[2], after(over_x(chunks[3]), fl))
+        fc = along_ring(after(ff7, fb), -1)
         cx, cz = over_x(after(chunks[5], part)), along_ring(part, -1)
         core = after(core, part)
     (sent,) = call(input_pair_body, "input_pair", [((local + ents + 2 * share, width), bf16)])(across, core)
@@ -930,7 +931,7 @@
             [((ff_part, width), f32)] + [((part_rows, ff), bf16)] * 4,
             [pltpu.VMEM((RANKS * part_rows, ff), f32)],
         )
-        part = plus(chunks[4], cz, cx)
+        part = plus(chunks[4], cz, after(cx, fb))
         cx, cz = over_x(after(chunks[7], part)), along_ring(part, -1)
         fy_last = swap(plus(ff1, fb, after(fc, part)), 2)
         part = plus(chunks[6], after(cz, came), cx)

time: 191 us -> 195 us (1.021)
  starting transfers between devices: 59.8 us -> 79.8 us
  waiting for transfers between devices: 84.2 us -> 68.9 us
    ppermute x34, starting transfers between devices: 21.5 us -> 34.9 us  [swap(): return lax.ppermute(x, 'blk', [(i, i ^ k) for i in range(RANKS)])]
    ppermute x15, waiting for transfers between devices: 26.8 us -> 14.1 us  [along_ring(): lax.ppermute(x, 'seq', [(2 * z + i, 2 * to + i) for z, to in route for i...]
    ppermute x15, starting transfers between devices: 21.7 us -> 28.1 us  [along_ring(): lax.ppermute(x, 'seq', [(2 * z + i, 2 * to + i) for z, to in route for i...]
    ppermute x14, waiting for transfers between devices: 39.8 us -> 35.2 us  [over_x(): return lax.ppermute(x, 'seq', [(i, i ^ 1) for i in range(8)])]
    ppermute x34, waiting for transfers between devices: 17.6 us -> 19.6 us  [swap(): return lax.ppermute(x, 'blk', [(i, i ^ k) for i in range(RANKS)])]
  transfers between devices with their start and end apart: 65 -> 65, of which waited for: 34 -> 31; matrix products, arithmetic and copies ran while one was open for 1% -> 1% of each run, Pallas kernels for 13% -> 13%
where the time goes in v4:
time: 195 us
  starting transfers between devices  79.8 us (41%)
  waiting for transfers between devices  68.9 us (35%)
  Pallas kernels  34.7 us (18%)
  local copies, waits for them, and re-layouts  9.02 us (5%)
    ppermute x14, waiting for transfers between devices, over_x(): return lax.ppermute(x, 'seq', [(i, i ^ 1) for i in range(8)])  35.2 us
    ppermute x34, starting transfers between devices, swap(): return lax.ppermute(x, 'blk', [(i, i ^ k) for i in range(RANKS)])  34.9 us
    pallas_call x28, Pallas kernels, run(): pl.pallas_call(body, name=name, out_shape=[jax.ShapeDtypeStruct(s, t) for...  34.7 us
    ppermute x15, starting transfers between devices, along_ring(): lax.ppermute(x, 'seq', [(2 * z + i, 2 * to + i) for z, to in route for i...  28.1 us
    ppermute x34, waiting for transfers between devices, swap(): return lax.ppermute(x, 'blk', [(i, i ^ k) for i in range(RANKS)])  19.6 us
    ppermute x14, starting transfers between devices, over_x(): return lax.ppermute(x, 'seq', [(i, i ^ 1) for i in range(8)])  15 us
    ppermute x15, waiting for transfers between devices, along_ring(): lax.ppermute(x, 'seq', [(2 * z + i, 2 * to + i) for z, to in route for i...  14.1 us
    unnamed x44, local copies, waits for them, and re-layouts  7.59 us
  transfers between devices with their start and end apart: 65, of which 31 were waited for; matrix products, arithmetic and copies ran while one was open for 1% of the time, Pallas kernels for 13%

profile of v4, /device:TPU:0, one launch (start us, length us, event | category | flops | bytes accessed | tf_op | source)
XLA Modules:
  0.0 195.0 jit_solution(13821542522189729681)
XLA Ops:
  3.2 2.6 %collective-permute-start.1 = (bf16[24,1408]{1,0:T(8,128)(2,1)}, bf16[24,1408]{1,0:T(8,128)(2,1)S(1)}, u32[]{:S(2)}, u32[]{:S(2)}) collective-permute-start(bf16[24,1408]{1,0:T(8,128)(2,1)} %get-tuple-element.163), channel_id=1, source_target_pairs={{0,2},{1,3},{2,0},{3,1},{4,6},{5,7},{6,4},{7,5},{8,10},{9,11},{10,... | collective-permute-start | bytes 202760 | tf_op jit(solution)/shard_map/ppermute | solution.py:580
  14.9 3.9 %collective-permute-done.4.r_1_ = bf16[96,1408]{1,0:T(8,128)(2,1)S(1)} collective-permute-done((bf16[96,1408]{1,0:T(8,128)(2,1)S(1)}, bf16[96,1408]{1,0:T(8,128)(2,1)S(1)}, u32[]{:S(2)}, u32[]{:S(2)}) %collective-permute-start.4) | collective-permute-done | bytes 270368 | tf_op jit(solution)/shard_map/ppermute | solution.py:601
  18.8 2.1 %collective-permute-done.3.r_2_ = bf16[96,1408]{1,0:T(8,128)(2,1)S(1)} collective-permute-done((bf16[96,1408]{1,0:T(8,128)(2,1)S(1)}, bf16[96,1408]{1,0:T(8,128)(2,1)S(1)}, u32[]{:S(2)}, u32[]{:S(2)}) %collective-permute-start.3) | collective-permute-done | bytes 270368 | tf_op jit(solution)/shard_map/ppermute | solution.py:617
  26.7 2.8 %collective-permute-done.9.p2 = bf16[24,768]{1,0:T(8,128)(2,1)S(1)} collective-permute-done((bf16[24,768]{1,0:T(8,128)(2,1)S(1)}, bf16[24,768]{1,0:T(8,128)(2,1)S(1)}, u32[]{:S(2)}, u32[]{:S(2)}) %collective-permute-start.9) | collective-permute-done | bytes 36896 | tf_op jit(solution)/shard_map/ppermute | solution.py:601
  35.5 3.4 %collective-permute-done.13.r_3_ = bf16[96,1408]{1,0:T(8,128)(2,1)S(1)} collective-permute-done((bf16[96,1408]{1,0:T(8,128)(2,1)S(1)}, bf16[96,1408]{1,0:T(8,128)(2,1)S(1)}, u32[]{:S(2)}, u32[]{:S(2)}) %collective-permute-start.13) | collective-permute-done | bytes 270368 | tf_op jit(solution)/shard_map/ppermute | solution.py:601
  50.4 2.4 %collective-permute-start.24 = (bf16[96,1536]{1,0:T(8,128)(2,1)}, bf16[96,1536]{1,0:T(8,128)(2,1)}, u32[]{:S(2)}, u32[]{:S(2)}) collective-permute-start(bf16[96,1536]{1,0:T(8,128)(2,1)} %collective-permute-done.16.r_2_), channel_id=1, source_target_pairs={{0,8},{4,12},{8,24},{12,28},{24,16},{28,20},{16,0},{20,4},{1,9},{5... | collective-permute-start | bytes 884744 | tf_op jit(solution)/shard_map/ppermute | solution.py:617
  54.6 4.8 %attend.1 = (bf16[160,192]{1,0:T(8,128)(2,1)S(1)}, bf16[160,192]{1,0:T(8,128)(2,1)S(1)}, bf16[160,192]{1,0:T(8,128)(2,1)S(1)}, bf16[160,192]{1,0:T(8,128)(2,1)S(...) custom-call(bf16[512,768]{1,0:T(8,128)(2,1)S(1)} %join_rows.1.r_0_.x, ...), custom_call_target="tpu_custom_call" | custom-call | flops 7000000 | bytes 7000 | tf_op jit(solution)/shard_map/attend/pallas_call | solution.py:34
  67.1 4.6 %collective-permute-done.25.r_5_ = bf16[96,1536]{1,0:T(8,128)(2,1)S(1)} collective-permute-done((bf16[96,1536]{1,0:T(8,128)(2,1)}, bf16[96,1536]{1,0:T(8,128)(2,1)S(1)}, u32[]{:S(2)}, u32[]{:S(2)}) %collective-permute-start.25) | collective-permute-done | bytes 294944 | tf_op jit(solution)/shard_map/ppermute | solution.py:617
  78.7 2.9 %collective-permute-done.27.h2 = bf16[160,768]{1,0:T(8,128)(2,1)S(1)} collective-permute-done((bf16[160,768]{1,0:T(8,128)(2,1)S(1)}, bf16[160,768]{1,0:T(8,128)(2,1)S(1)}, u32[]{:S(2)}, u32[]{:S(2)}) %collective-permute-start.27) | collective-permute-done | bytes 245792 | tf_op jit(solution)/shard_map/ppermute | solution.py:601
  83.7 2.3 %feed.1 = (f32[160,768]{1,0:T(8,128)S(1)}, bf16[160,768]{1,0:T(8,128)(2,1)S(1)}, bf16[2,160,768]{2,1,0:T(8,128)(2,1)S(1)}, bf16[4,160,768]{2,1,0:T(8,128)(2,1)S(1)}, bf16[4,160,768]{2,1,0:T(8,128)(2,1)S(1)}) custom-call(bf16[160,768]{1,0:T(8,128)(2,1)S(1)} %get-tuple-element.211.h0, bf16[160,768]{1,0:T(8,128)(2,1)S(1)} %collective-permute-done.26.h1, ...), custom_call_target="tpu_custom_call" | custom-call | flops 3000000 | bytes 3000 | tf_op jit(solution)/shard_map/feed/pallas_call | solution.py:34
  89.1 7.0 %collective-permute-done.33.f2 = bf16[160,768]{1,0:T(8,128)(2,1)S(1)} collective-permute-done((bf16[160,768]{1,0:T(8,128)(2,1)S(1)}, bf16[160,768]{1,0:T(8,128)(2,1)S(1)}, u32[]{:S(2)}, u32[]{:S(2)}) %collective-permute-start.33) | collective-permute-done | bytes 245792 | tf_op jit(solution)/shard_map/ppermute | solution.py:601
  98.2 6.1 %collective-permute-done.35.d2 = bf16[160,768]{1,0:T(8,128)(2,1)S(1)} collective-permute-done((bf16[160,768]{1,0:T(8,128)(2,1)S(1)}, bf16[160,768]{1,0:T(8,128)(2,1)S(1)}, u32[]{:S(2)}, u32[]{:S(2)}) %collective-permute-start.35) | collective-permute-done | bytes 245792 | tf_op jit(solution)/shard_map/ppermute | solution.py:601
  110.8 2.1 %feed_grads.1 = (bf16[96,1536]{1,0:T(8,128)(2,1)S(1)}, bf16[96,1536]{1,0:T(8,128)(2,1)S(1)}, bf16[96,1536]{1,0:T(8,128)(2,1)S(1)}, bf16[96,1536]{1,0:T(8,128)(2,...) custom-call(bf16[160,768]{1,0:T(8,128)(2,1)S(1)} %get-tuple-element., ...), custom_call_target="tpu_custom_call" | custom-call | flops 3000000 | bytes 3000 | tf_op jit(solution)/shard_map/feed_grads/pallas_call | solution.py:34
  118.0 2.6 %norm_one.1 = (bf16[160,192]{1,0:T(8,128)(2,1)S(1)}, bf16[160,192]{1,0:T(8,128)(2,1)S(1)}, bf16[160,192]{1,0:T(8,128)(2,1)S(1)}, bf16[2640,128]{1,0:T(8,128)(2,1...) custom-call(f32[160,768]{1,0:T(8,128)S(1)} %get-tuple-element.228.h0, ...), custom_call_target="tpu_custom_call" | custom-call | flops 1000000 | bytes 1000 | tf_op jit(solution)/shard_map/norm_one/pallas_call | solution.py:34
  128.5 4.9 %attend_back.1.dqkv = bf16[640,768]{1,0:T(8,128)(2,1)S(1)} custom-call(bf16[160,192]{1,0:T(8,128)(2,1)S(1)} %get-tuple-element.254.r_0_, bf16[2640,128]{1,0:T(8,128)(2,1)S(1)} %collective-permute-done.39.r_1_.o1, bf16[160,192]{1,0:T(8,128)(2,1)S(1)} %collective-permute-done.40.r_2_, bf16[160,192]{1,0:T(8,128)(2,1)S(1)} %collective-permute-done.41.r_3_, ...), custom_call_target="tpu_custom_call" | custom-call | flops 7000000 | bytes 7000 | tf_op jit(solution)/shard_map/attend_back/pallas_call | solution.py:34
  142.5 3.3 %collective-permute-done.47 = bf16[96,1408]{1,0:T(8,128)(2,1)S(1)} collective-permute-done((bf16[96,1408]{1,0:T(8,128)(2,1)S(1)}, bf16[96,1408]{1,0:T(8,128)(2,1)S(1)}, u32[]{:S(2)}, u32[]{:S(2)}) %collective-permute-start.47) | collective-permute-done | bytes 270368 | tf_op jit(solution)/shard_map/ppermute | solution.py:601
  147.0 2.2 %collective-permute-start.50 = (bf16[96,1408]{1,0:T(8,128)(2,1)S(1)}, bf16[96,1408]{1,0:T(8,128)(2,1)S(1)}, u32[]{:S(2)}, u32[]{:S(2)}) collective-permute-start(bf16[96,1408]{1,0:T(8,128)(2,1)S(1)} %add_convert_fusion.6), channel_id=1, source_target_pairs={{0,16},{4,20},{8,0},{12,4},{24,8},{28,12},{16,24},{20,28},{1,17},{... | collective-permute-start | bytes 811016 | tf_op jit(solution)/shard_map/ppermute | solution.py:617
  149.2 2.5 %collective-permute-done.52 = bf16[96,1536]{1,0:T(8,128)(2,1)S(1)} collective-permute-done((bf16[96,1536]{1,0:T(8,128)(2,1)S(1)}, bf16[96,1536]{1,0:T(8,128)(2,1)S(1)}, u32[]{:S(2)}, u32[]{:S(2)}) %collective-permute-start.52) | collective-permute-done | bytes 294944 | tf_op jit(solution)/shard_map/ppermute | solution.py:617
  152.3 11.8 %collective-permute-start.49 = (bf16[320,768]{1,0:T(8,128)(2,1)S(1)}, bf16[320,768]{1,0:T(8,128)(2,1)S(1)}, u32[]{:S(2)}, u32[]{:S(2)}) collective-permute-start(bf16[320,768]{1,0:T(8,128)(2,1)S(1)} %input_pair.1.sent), channel_id=1, source_target_pairs={{0,2},{1,3},{2,0},{3,1},{4,6},{5,7},{6,4},{7,5},{8,10},{9,11},{10,... | collective-permute-start | bytes 1474568 | tf_op jit(solution)/shard_map/ppermute | solution.py:580
  166.8 3.9 %collective-permute-start.57 = (bf16[96,1536]{1,0:T(8,128)(2,1)S(1)}, bf16[96,1536]{1,0:T(8,128)(2,1)S(1)}, u32[]{:S(2)}, u32[]{:S(2)}) collective-permute-start(bf16[96,1536]{1,0:T(8,128)(2,1)S(1)} %add_convert_fusion.1), channel_id=1, source_target_pairs={{0,2},{1,3},{2,0},{3,1},{4,6},{5,7},{6,4},{7,5},{8,10},{9,11},{10,... | collective-permute-start | bytes 884744 | tf_op jit(solution)/shard_map/ppermute | solution.py:580
  171.1 2.2 %collective-permute-done.49.came = bf16[320,768]{1,0:T(8,128)(2,1)S(1)} collective-permute-done((bf16[320,768]{1,0:T(8,128)(2,1)S(1)}, bf16[320,768]{1,0:T(8,128)(2,1)S(1)}, u32[]{:S(2)}, u32[]{:S(2)}) %collective-permute-start.49) | collective-permute-done | bytes 491552 | tf_op jit(solution)/shard_map/ppermute | solution.py:580
  173.4 6.4 %collective-permute-start.55 = (bf16[96,1408]{1,0:T(8,128)(2,1)S(1)}, bf16[96,1408]{1,0:T(8,128)(2,1)S(1)}, u32[]{:S(2)}, u32[]{:S(2)}) collective-permute-start(bf16[96,1408]{1,0:T(8,128)(2,1)S(1)} %add_convert_fusion.4), channel_id=1, source_target_pairs={{0,16},{4,20},{8,0},{12,4},{24,8},{28,12},{16,24},{20,28},{1,17},{... | collective-permute-start | bytes 811016 | tf_op jit(solution)/shard_map/ppermute | solution.py:617
  184.7 2.8 %collective-permute-done.59.c2 = bf16[24,768]{1,0:T(8,128)(2,1)S(1)} collective-permute-done((bf16[24,768]{1,0:T(8,128)(2,1)S(1)}, bf16[24,768]{1,0:T(8,128)(2,1)S(1)}, u32[]{:S(2)}, u32[]{:S(2)}) %collective-permute-start.59) | collective-permute-done | bytes 36896 | tf_op jit(solution)/shard_map/ppermute | solution.py:601
  190.5 3.3 %collective-permute-done.63.c2 = bf16[24,1408]{1,0:T(8,128)(2,1)S(1)} collective-permute-done((bf16[24,1408]{1,0:T(8,128)(2,1)S(1)}, bf16[24,1408]{1,0:T(8,128)(2,1)S(1)}, u32[]{:S(2)}, u32[]{:S(2)}) %collective-permute-start.63) | collective-permute-done | bytes 67616 | tf_op jit(solution)/shard_map/ppermute | solution.py:580
  (193 shorter events, 100.3 us)
Async XLA Ops:
  11.8 9.1 %collective-permute-start.3 = (bf16[96,1408]{1,0:T(8,128)(2,1)S(1)}, bf16[96,1408]{1,0:T(8,128)(2,1)S(1)}, u32[]{:S(2)}, u32[]{:S(2)}) collective-permute-start(bf16[96,1408]{1,0:T(8,128)(2,1)S(1)} %arrange.1.r_0_), channel_id=1, source_target_pairs={{0,8},{4,12},{8,24},{12,28},{24,16},{28,20},{16,0},{20,4},{1,9},{5... | collective-permute-start | bytes 811016 | tf_op jit(solution)/shard_map/ppermute | solution.py:617
  13.6 16.0 %collective-permute-start.11 = (bf16[128,768]{1,0:T(8,128)(2,1)S(1)}, bf16[128,768]{1,0:T(8,128)(2,1)S(1)}, u32[]{:S(2)}, u32[]{:S(2)}) collective-permute-start(bf16[128,768]{1,0:T(8,128)(2,1)S(1)} %bitcast.46), channel_id=1, source_target_pairs={{0,2},{1,3},{2,0},{3,1},{4,6},{5,7},{6,4},{7,5},{8,10},{9,11},{10,... | collective-permute-start | bytes 589832 | tf_op jit(solution)/shard_map/ppermute | solution.py:580
  21.5 8.8 %collective-permute-start.6 = (bf16[96,1408]{1,0:T(8,128)(2,1)S(1)}, bf16[96,1408]{1,0:T(8,128)(2,1)S(1)}, u32[]{:S(2)}, u32[]{:S(2)}) collective-permute-start(bf16[96,1408]{1,0:T(8,128)(2,1)S(1)} %collective-permute-done.3.r_2_), channel_id=1, source_target_pairs={{0,8},{4,12},{8,24},{12,28},{24,16},{28,20},{16,0},{20,4},{1,9},{5... | collective-permute-start | bytes 811016 | tf_op jit(solution)/shard_map/ppermute | solution.py:617
  31.0 9.4 %collective-permute-start.12 = (bf16[96,1408]{1,0:T(8,128)(2,1)S(1)}, bf16[96,1408]{1,0:T(8,128)(2,1)S(1)}, u32[]{:S(2)}, u32[]{:S(2)}) collective-permute-start(bf16[96,1408]{1,0:T(8,128)(2,1)S(1)} %collective-permute-done.6.r_4_), channel_id=1, source_target_pairs={{0,8},{4,12},{8,24},{12,28},{24,16},{28,20},{16,0},{20,4},{1,9},{5... | collective-permute-start | bytes 811016 | tf_op jit(solution)/shard_map/ppermute | solution.py:617
  34.0 13.1 %collective-permute-start.17 = (bf16[96,1536]{1,0:T(8,128)(2,1)S(1)}, bf16[96,1536]{1,0:T(8,128)(2,1)S(1)}, u32[]{:S(2)}, u32[]{:S(2)}) collective-permute-start(bf16[96,1536]{1,0:T(8,128)(2,1)S(1)} %arrange_ff.1.r_0_), channel_id=1, source_target_pairs={{0,2},{1,3},{2,0},{3,1},{4,6},{5,7},{6,4},{7,5},{8,10},{9,11},{10,... | collective-permute-start | bytes 884744 | tf_op jit(solution)/shard_map/ppermute | solution.py:580
  40.3 9.2 %collective-permute-start.16 = (bf16[96,1536]{1,0:T(8,128)(2,1)S(1)}, bf16[96,1536]{1,0:T(8,128)(2,1)}, u32[]{:S(2)}, u32[]{:S(2)}) collective-permute-start(bf16[96,1536]{1,0:T(8,128)(2,1)S(1)} %arrange_ff.1.r_0_), channel_id=1, source_target_pairs={{0,8},{4,12},{8,24},{12,28},{24,16},{28,20},{16,0},{20,4},{1,9},{5... | collective-permute-start | bytes 884744 | tf_op jit(solution)/shard_map/ppermute | solution.py:617
  50.4 9.0 %collective-permute-start.18 = (bf16[1152,128]{1,0:T(8,128)(2,1)}, bf16[1152,128]{1,0:T(8,128)(2,1)}, u32[]{:S(2)}, u32[]{:S(2)}) collective-permute-start(bf16[1152,128]{1,0:T(8,128)(2,1)} %get-tuple-element.206.w0), channel_id=1, source_target_pairs={{0,1},{1,0},{2,3},{3,2},{4,5},{5,4},{6,7},{7,6},{8,9},{9,8},{10,11... | collective-permute-start | bytes 884744 | tf_op jit(solution)/shard_map/ppermute | solution.py:580
  50.4 10.9 %collective-permute-start.24 = (bf16[96,1536]{1,0:T(8,128)(2,1)}, bf16[96,1536]{1,0:T(8,128)(2,1)}, u32[]{:S(2)}, u32[]{:S(2)}) collective-permute-start(bf16[96,1536]{1,0:T(8,128)(2,1)} %collective-permute-done.16.r_2_), channel_id=1, source_target_pairs={{0,8},{4,12},{8,24},{12,28},{24,16},{28,20},{16,0},{20,4},{1,9},{5... | collective-permute-start | bytes 884744 | tf_op jit(solution)/shard_map/ppermute | solution.py:617
  52.8 10.4 %collective-permute-start.22 = (bf16[1152,128]{1,0:T(8,128)(2,1)}, bf16[1152,128]{1,0:T(8,128)(2,1)}, u32[]{:S(2)}, u32[]{:S(2)}) collective-permute-start(bf16[1152,128]{1,0:T(8,128)(2,1)} %get-tuple-element.206.w0), channel_id=1, source_target_pairs={{0,2},{1,3},{2,0},{3,1},{4,6},{5,7},{6,4},{7,5},{8,10},{9,11},{10,... | collective-permute-start | bytes 884744 | tf_op jit(solution)/shard_map/ppermute | solution.py:580
  61.4 10.4 %collective-permute-start.25 = (bf16[96,1536]{1,0:T(8,128)(2,1)}, bf16[96,1536]{1,0:T(8,128)(2,1)S(1)}, u32[]{:S(2)}, u32[]{:S(2)}) collective-permute-start(bf16[96,1536]{1,0:T(8,128)(2,1)} %collective-permute-done.24.r_4_), channel_id=1, source_target_pairs={{0,8},{4,12},{8,24},{12,28},{24,16},{28,20},{16,0},{20,4},{1,9},{5... | collective-permute-start | bytes 884744 | tf_op jit(solution)/shard_map/ppermute | solution.py:617
  66.2 11.3 %collective-permute-start.28 = (bf16[96,1536]{1,0:T(8,128)(2,1)}, bf16[96,1536]{1,0:T(8,128)(2,1)S(1)}, u32[]{:S(2)}, u32[]{:S(2)}) collective-permute-start(bf16[96,1536]{1,0:T(8,128)(2,1)} %collective-permute-done.16.r_2_), channel_id=1, source_target_pairs={{0,2},{1,3},{2,0},{3,1},{4,6},{5,7},{6,4},{7,5},{8,10},{9,11},{10,... | collective-permute-start | bytes 884744 | tf_op jit(solution)/shard_map/ppermute | solution.py:580
  112.9 9.9 %collective-permute-start.43 = (bf16[96,1536]{1,0:T(8,128)(2,1)S(1)}, bf16[96,1536]{1,0:T(8,128)(2,1)S(1)}, u32[]{:S(2)}, u32[]{:S(2)}) collective-permute-start(bf16[96,1536]{1,0:T(8,128)(2,1)S(1)} %get-tuple-element.238), channel_id=1, source_target_pairs={{0,8},{4,12},{8,24},{12,28},{24,16},{28,20},{16,0},{20,4},{1,9},{5... | collective-permute-start | bytes 884744 | tf_op jit(solution)/shard_map/ppermute | solution.py:617
  114.9 8.7 %collective-permute-start.42 = (bf16[96,1536]{1,0:T(8,128)(2,1)S(1)}, bf16[96,1536]{1,0:T(8,128)(2,1)S(1)}, u32[]{:S(2)}, u32[]{:S(2)}) collective-permute-start(bf16[96,1536]{1,0:T(8,128)(2,1)S(1)} %get-tuple-element.241), channel_id=1, source_target_pairs={{0,2},{1,3},{2,0},{3,1},{4,6},{5,7},{6,4},{7,5},{8,10},{9,11},{10,... | collective-permute-start | bytes 884744 | tf_op jit(solution)/shard_map/ppermute | solution.py:580
  123.7 9.7 %collective-permute-start.44 = (bf16[96,1536]{1,0:T(8,128)(2,1)S(1)}, bf16[96,1536]{1,0:T(8,128)(2,1)S(1)}, u32[]{:S(2)}, u32[]{:S(2)}) collective-permute-start(bf16[96,1536]{1,0:T(8,128)(2,1)S(1)} %add_convert_fusion.3), channel_id=1, source_target_pairs={{0,16},{4,20},{8,0},{12,4},{24,8},{28,12},{16,24},{20,28},{1,17},{... | collective-permute-start | bytes 884744 | tf_op jit(solution)/shard_map/ppermute | solution.py:617
  127.1 9.6 %collective-permute-start.46 = (bf16[1200,128]{1,0:T(8,128)(2,1)S(1)}, bf16[1200,128]{1,0:T(8,128)(2,1)S(1)}, u32[]{:S(2)}, u32[]{:S(2)}) collective-permute-start(bf16[1200,128]{1,0:T(8,128)(2,1)S(1)} %add_convert_fusion), channel_id=1, source_target_pairs={{0,2},{1,3},{2,0},{3,1},{4,6},{5,7},{6,4},{7,5},{8,10},{9,11},{10,... | collective-permute-start | bytes 921608 | tf_op jit(solution)/shard_map/ppermute | solution.py:580
  133.5 9.0 %collective-permute-start.48 = (bf16[96,1536]{1,0:T(8,128)(2,1)S(1)}, bf16[96,1536]{1,0:T(8,128)(2,1)S(1)}, u32[]{:S(2)}, u32[]{:S(2)}) collective-permute-start(bf16[96,1536]{1,0:T(8,128)(2,1)S(1)} %add_convert_fusion.2), channel_id=1, source_target_pairs={{0,16},{4,20},{8,0},{12,4},{24,8},{28,12},{16,24},{20,28},{1,17},{... | collective-permute-start | bytes 884744 | tf_op jit(solution)/shard_map/ppermute | solution.py:617
  139.2 13.0 %collective-permute-start.45 = (bf16[416,768]{1,0:T(8,128)(2,1)S(1)}, bf16[416,768]{1,0:T(8,128)(2,1)S(1)}, u32[]{:S(2)}, u32[]{:S(2)}) collective-permute-start(bf16[416,768]{1,0:T(8,128)(2,1)S(1)} %get-tuple-element.268), channel_id=1, source_target_pairs={{0,1},{1,0},{2,3},{3,2},{4,5},{5,4},{6,7},{7,6},{8,9},{9,8},{10,11... | collective-permute-start | bytes 1916936 | tf_op jit(solution)/shard_map/ppermute | solution.py:580
  139.2 12.5 %collective-permute-start.52 = (bf16[96,1536]{1,0:T(8,128)(2,1)S(1)}, bf16[96,1536]{1,0:T(8,128)(2,1)S(1)}, u32[]{:S(2)}, u32[]{:S(2)}) collective-permute-start(bf16[96,1536]{1,0:T(8,128)(2,1)S(1)} %get-tuple-element.284), channel_id=1, source_target_pairs={{0,8},{4,12},{8,24},{12,28},{24,16},{28,20},{16,0},{20,4},{1,9},{5... | collective-permute-start | bytes 884744 | tf_op jit(solution)/shard_map/ppermute | solution.py:617
  145.9 18.2 %collective-permute-start.51 = (bf16[96,1408]{1,0:T(8,128)(2,1)S(1)}, bf16[96,1408]{1,0:T(8,128)(2,1)S(1)}, u32[]{:S(2)}, u32[]{:S(2)}) collective-permute-start(bf16[96,1408]{1,0:T(8,128)(2,1)S(1)} %get-tuple-element.280), channel_id=1, source_target_pairs={{0,4},{4,0},{8,12},{12,8},{16,20},{20,16},{24,28},{28,24},{1,5},{5... | collective-permute-start | bytes 811016 | tf_op jit(solution)/shard_map/ppermute | solution.py:601
  147.0 17.1 %collective-permute-start.50 = (bf16[96,1408]{1,0:T(8,128)(2,1)S(1)}, bf16[96,1408]{1,0:T(8,128)(2,1)S(1)}, u32[]{:S(2)}, u32[]{:S(2)}) collective-permute-start(bf16[96,1408]{1,0:T(8,128)(2,1)S(1)} %add_convert_fusion.6), channel_id=1, source_target_pairs={{0,16},{4,20},{8,0},{12,4},{24,8},{28,12},{16,24},{20,28},{1,17},{... | collective-permute-start | bytes 811016 | tf_op jit(solution)/shard_map/ppermute | solution.py:617
  151.7 15.0 %collective-permute-start.56 = (bf16[96,1536]{1,0:T(8,128)(2,1)S(1)}, bf16[96,1536]{1,0:T(8,128)(2,1)S(1)}, u32[]{:S(2)}, u32[]{:S(2)}) collective-permute-start(bf16[96,1536]{1,0:T(8,128)(2,1)S(1)} %get-tuple-element.292), channel_id=1, source_target_pairs={{0,16},{4,20},{8,0},{12,4},{24,8},{28,12},{16,24},{20,28},{1,17},{... | collective-permute-start | bytes 884744 | tf_op jit(solution)/shard_map/ppermute | solution.py:617
  152.3 21.0 %collective-permute-start.49 = (bf16[320,768]{1,0:T(8,128)(2,1)S(1)}, bf16[320,768]{1,0:T(8,128)(2,1)S(1)}, u32[]{:S(2)}, u32[]{:S(2)}) collective-permute-start(bf16[320,768]{1,0:T(8,128)(2,1)S(1)} %input_pair.1.sent), channel_id=1, source_target_pairs={{0,2},{1,3},{2,0},{3,1},{4,6},{5,7},{6,4},{7,5},{8,10},{9,11},{10,... | collective-permute-start | bytes 1474568 | tf_op jit(solution)/shard_map/ppermute | solution.py:580
  166.8 14.0 %collective-permute-start.57 = (bf16[96,1536]{1,0:T(8,128)(2,1)S(1)}, bf16[96,1536]{1,0:T(8,128)(2,1)S(1)}, u32[]{:S(2)}, u32[]{:S(2)}) collective-permute-start(bf16[96,1536]{1,0:T(8,128)(2,1)S(1)} %add_convert_fusion.1), channel_id=1, source_target_pairs={{0,2},{1,3},{2,0},{3,1},{4,6},{5,7},{6,4},{7,5},{8,10},{9,11},{10,... | collective-permute-start | bytes 884744 | tf_op jit(solution)/shard_map/ppermute | solution.py:580
  173.4 15.0 %collective-permute-start.55 = (bf16[96,1408]{1,0:T(8,128)(2,1)S(1)}, bf16[96,1408]{1,0:T(8,128)(2,1)S(1)}, u32[]{:S(2)}, u32[]{:S(2)}) collective-permute-start(bf16[96,1408]{1,0:T(8,128)(2,1)S(1)} %add_convert_fusion.4), channel_id=1, source_target_pairs={{0,16},{4,20},{8,0},{12,4},{24,8},{28,12},{16,24},{20,28},{1,17},{... | collective-permute-start | bytes 811016 | tf_op jit(solution)/shard_map/ppermute | solution.py:617
  (63 other events, 410.0 us)

commit v5 on v3

--- a/solution.py
+++ b/solution.py
@@ -909,7 +909,7 @@
     chunks = proj_grads(after(dqkv, own), xw, xe, *outs)
     if direct:
         fl = along_ring(plus(ff6, after(fl, dqkv)), -1)
-        fb, fc = along_ring(after(ff3, chunks)), along_ring(after(ff7, chunks), -1)
+        fb, fc = along_ring(after(ff3, dqkv)), along_ring(after(ff7, chunks), -1)
         part = plus(chunks[2], after(over_x(chunks[3]), fl, fb))
         cx, cz = over_x(after(chunks[5], part)), along_ring(part, -1)
         core = after(core, part)

time: 191 us -> 189 us (0.990)
    ppermute x14, waiting for transfers between devices: 39.8 us -> 36 us  [over_x(): return lax.ppermute(x, 'seq', [(i, i ^ 1) for i in range(8)])]
    ppermute x15, waiting for transfers between devices: 26.8 us -> 30.2 us  [along_ring(): lax.ppermute(x, 'seq', [(2 * z + i, 2 * to + i) for z, to in route for i...]
  transfers between devices with their start and end apart: 65 -> 65, of which waited for: 34 -> 33; matrix products, arithmetic and copies ran while one was open for 1% -> 1% of each run, Pallas kernels for 13% -> 14%
where the time goes in v5:
time: 189 us
  waiting for transfers between devices  83.8 us (44%)
  starting transfers between devices  58.8 us (31%)
  Pallas kernels  34.7 us (18%)
  local copies, waits for them, and re-layouts  9.02 us (5%)
    ppermute x14, waiting for transfers between devices, over_x(): return lax.ppermute(x, 'seq', [(i, i ^ 1) for i in range(8)])  36 us
    pallas_call x28, Pallas kernels, run(): pl.pallas_call(body, name=name, out_shape=[jax.ShapeDtypeStruct(s, t) for...  34.7 us
    ppermute x15, waiting for transfers between devices, along_ring(): lax.ppermute(x, 'seq', [(2 * z + i, 2 * to + i) for z, to in route for i...  30.2 us
    ppermute x34, starting transfers between devices, swap(): return lax.ppermute(x, 'blk', [(i, i ^ k) for i in range(RANKS)])  21.4 us
    ppermute x15, starting transfers between devices, along_ring(): lax.ppermute(x, 'seq', [(2 * z + i, 2 * to + i) for z, to in route for i...  20.6 us
    ppermute x34, waiting for transfers between devices, swap(): return lax.ppermute(x, 'blk', [(i, i ^ k) for i in range(RANKS)])  17.6 us
    ppermute x14, starting transfers between devices, over_x(): return lax.ppermute(x, 'seq', [(i, i ^ 1) for i in range(8)])  15 us
    unnamed x44, local copies, waits for them, and re-layouts  7.59 us
  transfers between devices with their start and end apart: 65, of which 33 were waited for; matrix products, arithmetic and copies ran while one was open for 1% of the time, Pallas kernels for 14%

profile of v5, /device:TPU:0, one launch (start us, length us, event | category | flops | bytes accessed | tf_op | source)
XLA Modules:
  0.0 188.9 jit_solution(9635937056891799515)
XLA Ops:
  3.2 2.6 %collective-permute-start.1 = (bf16[24,1408]{1,0:T(8,128)(2,1)}, bf16[24,1408]{1,0:T(8,128)(2,1)S(1)}, u32[]{:S(2)}, u32[]{:S(2)}) collective-permute-start(bf16[24,1408]{1,0:T(8,128)(2,1)} %get-tuple-element.162), channel_id=1, source_target_pairs={{0,2},{1,3},{2,0},{3,1},{4,6},{5,7},{6,4},{7,5},{8,10},{9,11},{10,... | collective-permute-start | bytes 202760 | tf_op jit(solution)/shard_map/ppermute | solution.py:580
  14.9 3.9 %collective-permute-done.4.r_1_ = bf16[96,1408]{1,0:T(8,128)(2,1)S(1)} collective-permute-done((bf16[96,1408]{1,0:T(8,128)(2,1)S(1)}, bf16[96,1408]{1,0:T(8,128)(2,1)S(1)}, u32[]{:S(2)}, u32[]{:S(2)}) %collective-permute-start.4) | collective-permute-done | bytes 270368 | tf_op jit(solution)/shard_map/ppermute | solution.py:601
  18.8 2.1 %collective-permute-done.3.r_2_ = bf16[96,1408]{1,0:T(8,128)(2,1)S(1)} collective-permute-done((bf16[96,1408]{1,0:T(8,128)(2,1)S(1)}, bf16[96,1408]{1,0:T(8,128)(2,1)S(1)}, u32[]{:S(2)}, u32[]{:S(2)}) %collective-permute-start.3) | collective-permute-done | bytes 270368 | tf_op jit(solution)/shard_map/ppermute | solution.py:617
  26.7 2.8 %collective-permute-done.9.p2 = bf16[24,768]{1,0:T(8,128)(2,1)S(1)} collective-permute-done((bf16[24,768]{1,0:T(8,128)(2,1)S(1)}, bf16[24,768]{1,0:T(8,128)(2,1)S(1)}, u32[]{:S(2)}, u32[]{:S(2)}) %collective-permute-start.9) | collective-permute-done | bytes 36896 | tf_op jit(solution)/shard_map/ppermute | solution.py:601
  35.5 3.4 %collective-permute-done.13.r_3_ = bf16[96,1408]{1,0:T(8,128)(2,1)S(1)} collective-permute-done((bf16[96,1408]{1,0:T(8,128)(2,1)S(1)}, bf16[96,1408]{1,0:T(8,128)(2,1)S(1)}, u32[]{:S(2)}, u32[]{:S(2)}) %collective-permute-start.13) | collective-permute-done | bytes 270368 | tf_op jit(solution)/shard_map/ppermute | solution.py:601
  50.4 2.4 %collective-permute-start.24 = (bf16[96,1536]{1,0:T(8,128)(2,1)}, bf16[96,1536]{1,0:T(8,128)(2,1)}, u32[]{:S(2)}, u32[]{:S(2)}) collective-permute-start(bf16[96,1536]{1,0:T(8,128)(2,1)} %collective-permute-done.16.r_2_), channel_id=1, source_target_pairs={{0,8},{4,12},{8,24},{12,28},{24,16},{28,20},{16,0},{20,4},{1,9},{5... | collective-permute-start | bytes 884744 | tf_op jit(solution)/shard_map/ppermute | solution.py:617
  54.6 4.8 %attend.1 = (bf16[160,192]{1,0:T(8,128)(2,1)S(1)}, bf16[160,192]{1,0:T(8,128)(2,1)S(1)}, bf16[160,192]{1,0:T(8,128)(2,1)S(1)}, bf16[160,192]{1,0:T(8,128)(2,1)S(...) custom-call(bf16[512,768]{1,0:T(8,128)(2,1)S(1)} %join_rows.1.r_0_.x, ...), custom_call_target="tpu_custom_call" | custom-call | flops 7000000 | bytes 7000 | tf_op jit(solution)/shard_map/attend/pallas_call | solution.py:34
  67.1 4.6 %collective-permute-done.25.r_5_ = bf16[96,1536]{1,0:T(8,128)(2,1)S(1)} collective-permute-done((bf16[96,1536]{1,0:T(8,128)(2,1)}, bf16[96,1536]{1,0:T(8,128)(2,1)S(1)}, u32[]{:S(2)}, u32[]{:S(2)}) %collective-permute-start.25) | collective-permute-done | bytes 294944 | tf_op jit(solution)/shard_map/ppermute | solution.py:617
  78.7 2.9 %collective-permute-done.27.h2 = bf16[160,768]{1,0:T(8,128)(2,1)S(1)} collective-permute-done((bf16[160,768]{1,0:T(8,128)(2,1)S(1)}, bf16[160,768]{1,0:T(8,128)(2,1)S(1)}, u32[]{:S(2)}, u32[]{:S(2)}) %collective-permute-start.27) | collective-permute-done | bytes 245792 | tf_op jit(solution)/shard_map/ppermute | solution.py:601
  83.7 2.3 %feed.1 = (f32[160,768]{1,0:T(8,128)S(1)}, bf16[160,768]{1,0:T(8,128)(2,1)S(1)}, bf16[2,160,768]{2,1,0:T(8,128)(2,1)S(1)}, bf16[4,160,768]{2,1,0:T(8,128)(2,1)S(1)}, bf16[4,160,768]{2,1,0:T(8,128)(2,1)S(1)}) custom-call(bf16[160,768]{1,0:T(8,128)(2,1)S(1)} %get-tuple-element.210.h0, bf16[160,768]{1,0:T(8,128)(2,1)S(1)} %collective-permute-done.26.h1, ...), custom_call_target="tpu_custom_call" | custom-call | flops 3000000 | bytes 3000 | tf_op jit(solution)/shard_map/feed/pallas_call | solution.py:34
  89.1 7.0 %collective-permute-done.33.f2 = bf16[160,768]{1,0:T(8,128)(2,1)S(1)} collective-permute-done((bf16[160,768]{1,0:T(8,128)(2,1)S(1)}, bf16[160,768]{1,0:T(8,128)(2,1)S(1)}, u32[]{:S(2)}, u32[]{:S(2)}) %collective-permute-start.33) | collective-permute-done | bytes 245792 | tf_op jit(solution)/shard_map/ppermute | solution.py:601
  98.2 6.1 %collective-permute-done.35.d2 = bf16[160,768]{1,0:T(8,128)(2,1)S(1)} collective-permute-done((bf16[160,768]{1,0:T(8,128)(2,1)S(1)}, bf16[160,768]{1,0:T(8,128)(2,1)S(1)}, u32[]{:S(2)}, u32[]{:S(2)}) %collective-permute-start.35) | collective-permute-done | bytes 245792 | tf_op jit(solution)/shard_map/ppermute | solution.py:601
  110.8 2.1 %feed_grads.1 = (bf16[96,1536]{1,0:T(8,128)(2,1)S(1)}, bf16[96,1536]{1,0:T(8,128)(2,1)S(1)}, bf16[96,1536]{1,0:T(8,128)(2,1)S(1)}, bf16[96,1536]{1,0:T(8,128)(2,...) custom-call(bf16[160,768]{1,0:T(8,128)(2,1)S(1)} %get-tuple-element., ...), custom_call_target="tpu_custom_call" | custom-call | flops 3000000 | bytes 3000 | tf_op jit(solution)/shard_map/feed_grads/pallas_call | solution.py:34
  112.9 2.0 %collective-permute-start.43 = (bf16[96,1536]{1,0:T(8,128)(2,1)S(1)}, bf16[96,1536]{1,0:T(8,128)(2,1)S(1)}, u32[]{:S(2)}, u32[]{:S(2)}) collective-permute-start(bf16[96,1536]{1,0:T(8,128)(2,1)S(1)} %get-tuple-element.237), channel_id=1, source_target_pairs={{0,8},{4,12},{8,24},{12,28},{24,16},{28,20},{16,0},{20,4},{1,9},{5... | collective-permute-start | bytes 884744 | tf_op jit(solution)/shard_map/ppermute | solution.py:617
  118.0 2.6 %norm_one.1 = (bf16[160,192]{1,0:T(8,128)(2,1)S(1)}, bf16[160,192]{1,0:T(8,128)(2,1)S(1)}, bf16[160,192]{1,0:T(8,128)(2,1)S(1)}, bf16[2640,128]{1,0:T(8,128)(2,1...) custom-call(f32[160,768]{1,0:T(8,128)S(1)} %get-tuple-element.227.h0, ...), custom_call_target="tpu_custom_call" | custom-call | flops 1000000 | bytes 1000 | tf_op jit(solution)/shard_map/norm_one/pallas_call | solution.py:34
  128.5 4.9 %attend_back.1.dqkv = bf16[640,768]{1,0:T(8,128)(2,1)S(1)} custom-call(bf16[160,192]{1,0:T(8,128)(2,1)S(1)} %get-tuple-element.253.r_0_, bf16[2640,128]{1,0:T(8,128)(2,1)S(1)} %collective-permute-done.39.r_1_.o1, bf16[160,192]{1,0:T(8,128)(2,1)S(1)} %collective-permute-done.40.r_2_, bf16[160,192]{1,0:T(8,128)(2,1)S(1)} %collective-permute-done.41.r_3_, ...), custom_call_target="tpu_custom_call" | custom-call | flops 7000000 | bytes 7000 | tf_op jit(solution)/shard_map/attend_back/pallas_call | solution.py:34
  139.3 3.6 %collective-permute-done.48.a2 = bf16[96,1536]{1,0:T(8,128)(2,1)S(1)} collective-permute-done((bf16[96,1536]{1,0:T(8,128)(2,1)S(1)}, bf16[96,1536]{1,0:T(8,128)(2,1)S(1)}, u32[]{:S(2)}, u32[]{:S(2)}) %collective-permute-start.48) | collective-permute-done | bytes 294944 | tf_op jit(solution)/shard_map/ppermute | solution.py:617
  142.9 7.9 %collective-permute-done.49 = bf16[96,1536]{1,0:T(8,128)(2,1)S(1)} collective-permute-done((bf16[96,1536]{1,0:T(8,128)(2,1)S(1)}, bf16[96,1536]{1,0:T(8,128)(2,1)S(1)}, u32[]{:S(2)}, u32[]{:S(2)}) %collective-permute-start.49) | collective-permute-done | bytes 294944 | tf_op jit(solution)/shard_map/ppermute | solution.py:617
  155.2 4.1 %collective-permute-done.52 = bf16[96,1408]{1,0:T(8,128)(2,1)S(1)} collective-permute-done((bf16[96,1408]{1,0:T(8,128)(2,1)S(1)}, bf16[96,1408]{1,0:T(8,128)(2,1)S(1)}, u32[]{:S(2)}, u32[]{:S(2)}) %collective-permute-start.52) | collective-permute-done | bytes 270368 | tf_op jit(solution)/shard_map/ppermute | solution.py:601
  159.3 2.1 %collective-permute-done.51 = bf16[96,1408]{1,0:T(8,128)(2,1)S(1)} collective-permute-done((bf16[96,1408]{1,0:T(8,128)(2,1)S(1)}, bf16[96,1408]{1,0:T(8,128)(2,1)S(1)}, u32[]{:S(2)}, u32[]{:S(2)}) %collective-permute-start.51) | collective-permute-done | bytes 270368 | tf_op jit(solution)/shard_map/ppermute | solution.py:617
  164.2 3.5 %collective-permute-done.56 = bf16[96,1536]{1,0:T(8,128)(2,1)S(1)} collective-permute-done((bf16[96,1536]{1,0:T(8,128)(2,1)S(1)}, bf16[96,1536]{1,0:T(8,128)(2,1)S(1)}, u32[]{:S(2)}, u32[]{:S(2)}) %collective-permute-start.56) | collective-permute-done | bytes 294944 | tf_op jit(solution)/shard_map/ppermute | solution.py:617
  168.7 3.5 %collective-permute-done.53 = bf16[96,1408]{1,0:T(8,128)(2,1)S(1)} collective-permute-done((bf16[96,1408]{1,0:T(8,128)(2,1)S(1)}, bf16[96,1408]{1,0:T(8,128)(2,1)S(1)}, u32[]{:S(2)}, u32[]{:S(2)}) %collective-permute-start.53) | collective-permute-done | bytes 270368 | tf_op jit(solution)/shard_map/ppermute | solution.py:617
  178.4 2.8 %collective-permute-done.59.c2 = bf16[24,768]{1,0:T(8,128)(2,1)S(1)} collective-permute-done((bf16[24,768]{1,0:T(8,128)(2,1)S(1)}, bf16[24,768]{1,0:T(8,128)(2,1)S(1)}, u32[]{:S(2)}, u32[]{:S(2)}) %collective-permute-start.59) | collective-permute-done | bytes 36896 | tf_op jit(solution)/shard_map/ppermute | solution.py:601
  184.2 3.1 %collective-permute-done.63.c2 = bf16[24,1408]{1,0:T(8,128)(2,1)S(1)} collective-permute-done((bf16[24,1408]{1,0:T(8,128)(2,1)S(1)}, bf16[24,1408]{1,0:T(8,128)(2,1)S(1)}, u32[]{:S(2)}, u32[]{:S(2)}) %collective-permute-start.63) | collective-permute-done | bytes 67616 | tf_op jit(solution)/shard_map/ppermute | solution.py:580
  (193 shorter events, 100.0 us)
Async XLA Ops:
  11.8 9.1 %collective-permute-start.3 = (bf16[96,1408]{1,0:T(8,128)(2,1)S(1)}, bf16[96,1408]{1,0:T(8,128)(2,1)S(1)}, u32[]{:S(2)}, u32[]{:S(2)}) collective-permute-start(bf16[96,1408]{1,0:T(8,128)(2,1)S(1)} %arrange.1.r_0_), channel_id=1, source_target_pairs={{0,8},{4,12},{8,24},{12,28},{24,16},{28,20},{16,0},{20,4},{1,9},{5... | collective-permute-start | bytes 811016 | tf_op jit(solution)/shard_map/ppermute | solution.py:617
  13.6 16.0 %collective-permute-start.11 = (bf16[128,768]{1,0:T(8,128)(2,1)S(1)}, bf16[128,768]{1,0:T(8,128)(2,1)S(1)}, u32[]{:S(2)}, u32[]{:S(2)}) collective-permute-start(bf16[128,768]{1,0:T(8,128)(2,1)S(1)} %bitcast.46), channel_id=1, source_target_pairs={{0,2},{1,3},{2,0},{3,1},{4,6},{5,7},{6,4},{7,5},{8,10},{9,11},{10,... | collective-permute-start | bytes 589832 | tf_op jit(solution)/shard_map/ppermute | solution.py:580
  21.5 8.8 %collective-permute-start.6 = (bf16[96,1408]{1,0:T(8,128)(2,1)S(1)}, bf16[96,1408]{1,0:T(8,128)(2,1)S(1)}, u32[]{:S(2)}, u32[]{:S(2)}) collective-permute-start(bf16[96,1408]{1,0:T(8,128)(2,1)S(1)} %collective-permute-done.3.r_2_), channel_id=1, source_target_pairs={{0,8},{4,12},{8,24},{12,28},{24,16},{28,20},{16,0},{20,4},{1,9},{5... | collective-permute-start | bytes 811016 | tf_op jit(solution)/shard_map/ppermute | solution.py:617
  31.0 9.4 %collective-permute-start.12 = (bf16[96,1408]{1,0:T(8,128)(2,1)S(1)}, bf16[96,1408]{1,0:T(8,128)(2,1)S(1)}, u32[]{:S(2)}, u32[]{:S(2)}) collective-permute-start(bf16[96,1408]{1,0:T(8,128)(2,1)S(1)} %collective-permute-done.6.r_4_), channel_id=1, source_target_pairs={{0,8},{4,12},{8,24},{12,28},{24,16},{28,20},{16,0},{20,4},{1,9},{5... | collective-permute-start | bytes 811016 | tf_op jit(solution)/shard_map/ppermute | solution.py:617
  34.0 13.1 %collective-permute-start.17 = (bf16[96,1536]{1,0:T(8,128)(2,1)S(1)}, bf16[96,1536]{1,0:T(8,128)(2,1)S(1)}, u32[]{:S(2)}, u32[]{:S(2)}) collective-permute-start(bf16[96,1536]{1,0:T(8,128)(2,1)S(1)} %arrange_ff.1.r_0_), channel_id=1, source_target_pairs={{0,2},{1,3},{2,0},{3,1},{4,6},{5,7},{6,4},{7,5},{8,10},{9,11},{10,... | collective-permute-start | bytes 884744 | tf_op jit(solution)/shard_map/ppermute | solution.py:580
  40.3 9.2 %collective-permute-start.16 = (bf16[96,1536]{1,0:T(8,128)(2,1)S(1)}, bf16[96,1536]{1,0:T(8,128)(2,1)}, u32[]{:S(2)}, u32[]{:S(2)}) collective-permute-start(bf16[96,1536]{1,0:T(8,128)(2,1)S(1)} %arrange_ff.1.r_0_), channel_id=1, source_target_pairs={{0,8},{4,12},{8,24},{12,28},{24,16},{28,20},{16,0},{20,4},{1,9},{5... | collective-permute-start | bytes 884744 | tf_op jit(solution)/shard_map/ppermute | solution.py:617
  50.4 9.0 %collective-permute-start.18 = (bf16[1152,128]{1,0:T(8,128)(2,1)}, bf16[1152,128]{1,0:T(8,128)(2,1)}, u32[]{:S(2)}, u32[]{:S(2)}) collective-permute-start(bf16[1152,128]{1,0:T(8,128)(2,1)} %get-tuple-element.205.w0), channel_id=1, source_target_pairs={{0,1},{1,0},{2,3},{3,2},{4,5},{5,4},{6,7},{7,6},{8,9},{9,8},{10,11... | collective-permute-start | bytes 884744 | tf_op jit(solution)/shard_map/ppermute | solution.py:580
  50.4 10.9 %collective-permute-start.24 = (bf16[96,1536]{1,0:T(8,128)(2,1)}, bf16[96,1536]{1,0:T(8,128)(2,1)}, u32[]{:S(2)}, u32[]{:S(2)}) collective-permute-start(bf16[96,1536]{1,0:T(8,128)(2,1)} %collective-permute-done.16.r_2_), channel_id=1, source_target_pairs={{0,8},{4,12},{8,24},{12,28},{24,16},{28,20},{16,0},{20,4},{1,9},{5... | collective-permute-start | bytes 884744 | tf_op jit(solution)/shard_map/ppermute | solution.py:617
  52.8 10.4 %collective-permute-start.22 = (bf16[1152,128]{1,0:T(8,128)(2,1)}, bf16[1152,128]{1,0:T(8,128)(2,1)}, u32[]{:S(2)}, u32[]{:S(2)}) collective-permute-start(bf16[1152,128]{1,0:T(8,128)(2,1)} %get-tuple-element.205.w0), channel_id=1, source_target_pairs={{0,2},{1,3},{2,0},{3,1},{4,6},{5,7},{6,4},{7,5},{8,10},{9,11},{10,... | collective-permute-start | bytes 884744 | tf_op jit(solution)/shard_map/ppermute | solution.py:580
  61.4 10.4 %collective-permute-start.25 = (bf16[96,1536]{1,0:T(8,128)(2,1)}, bf16[96,1536]{1,0:T(8,128)(2,1)S(1)}, u32[]{:S(2)}, u32[]{:S(2)}) collective-permute-start(bf16[96,1536]{1,0:T(8,128)(2,1)} %collective-permute-done.24.r_4_), channel_id=1, source_target_pairs={{0,8},{4,12},{8,24},{12,28},{24,16},{28,20},{16,0},{20,4},{1,9},{5... | collective-permute-start | bytes 884744 | tf_op jit(solution)/shard_map/ppermute | solution.py:617
  66.2 11.3 %collective-permute-start.28 = (bf16[96,1536]{1,0:T(8,128)(2,1)}, bf16[96,1536]{1,0:T(8,128)(2,1)S(1)}, u32[]{:S(2)}, u32[]{:S(2)}) collective-permute-start(bf16[96,1536]{1,0:T(8,128)(2,1)} %collective-permute-done.16.r_2_), channel_id=1, source_target_pairs={{0,2},{1,3},{2,0},{3,1},{4,6},{5,7},{6,4},{7,5},{8,10},{9,11},{10,... | collective-permute-start | bytes 884744 | tf_op jit(solution)/shard_map/ppermute | solution.py:580
  112.9 9.9 %collective-permute-start.43 = (bf16[96,1536]{1,0:T(8,128)(2,1)S(1)}, bf16[96,1536]{1,0:T(8,128)(2,1)S(1)}, u32[]{:S(2)}, u32[]{:S(2)}) collective-permute-start(bf16[96,1536]{1,0:T(8,128)(2,1)S(1)} %get-tuple-element.237), channel_id=1, source_target_pairs={{0,8},{4,12},{8,24},{12,28},{24,16},{28,20},{16,0},{20,4},{1,9},{5... | collective-permute-start | bytes 884744 | tf_op jit(solution)/shard_map/ppermute | solution.py:617
  123.7 9.7 %collective-permute-start.44 = (bf16[96,1536]{1,0:T(8,128)(2,1)S(1)}, bf16[96,1536]{1,0:T(8,128)(2,1)S(1)}, u32[]{:S(2)}, u32[]{:S(2)}) collective-permute-start(bf16[96,1536]{1,0:T(8,128)(2,1)S(1)} %add_convert_fusion.3), channel_id=1, source_target_pairs={{0,16},{4,20},{8,0},{12,4},{24,8},{28,12},{16,24},{20,28},{1,17},{... | collective-permute-start | bytes 884744 | tf_op jit(solution)/shard_map/ppermute | solution.py:617
  127.1 9.7 %collective-permute-start.46 = (bf16[1200,128]{1,0:T(8,128)(2,1)S(1)}, bf16[1200,128]{1,0:T(8,128)(2,1)S(1)}, u32[]{:S(2)}, u32[]{:S(2)}) collective-permute-start(bf16[1200,128]{1,0:T(8,128)(2,1)S(1)} %add_convert_fusion), channel_id=1, source_target_pairs={{0,2},{1,3},{2,0},{3,1},{4,6},{5,7},{6,4},{7,5},{8,10},{9,11},{10,... | collective-permute-start | bytes 921608 | tf_op jit(solution)/shard_map/ppermute | solution.py:580
  133.5 9.5 %collective-permute-start.48 = (bf16[96,1536]{1,0:T(8,128)(2,1)S(1)}, bf16[96,1536]{1,0:T(8,128)(2,1)S(1)}, u32[]{:S(2)}, u32[]{:S(2)}) collective-permute-start(bf16[96,1536]{1,0:T(8,128)(2,1)S(1)} %add_convert_fusion.2), channel_id=1, source_target_pairs={{0,16},{4,20},{8,0},{12,4},{24,8},{28,12},{16,24},{20,28},{1,17},{... | collective-permute-start | bytes 884744 | tf_op jit(solution)/shard_map/ppermute | solution.py:617
  135.5 15.4 %collective-permute-start.49 = (bf16[96,1536]{1,0:T(8,128)(2,1)S(1)}, bf16[96,1536]{1,0:T(8,128)(2,1)S(1)}, u32[]{:S(2)}, u32[]{:S(2)}) collective-permute-start(bf16[96,1536]{1,0:T(8,128)(2,1)S(1)} %get-tuple-element.273), channel_id=1, source_target_pairs={{0,8},{4,12},{8,24},{12,28},{24,16},{28,20},{16,0},{20,4},{1,9},{5... | collective-permute-start | bytes 884744 | tf_op jit(solution)/shard_map/ppermute | solution.py:617
  138.2 12.6 %collective-permute-start.47 = (bf16[96,1408]{1,0:T(8,128)(2,1)S(1)}, bf16[96,1408]{1,0:T(8,128)(2,1)S(1)}, u32[]{:S(2)}, u32[]{:S(2)}) collective-permute-start(bf16[96,1408]{1,0:T(8,128)(2,1)S(1)} %get-tuple-element.271), channel_id=1, source_target_pairs={{0,4},{4,0},{8,12},{12,8},{16,20},{20,16},{24,28},{28,24},{1,5},{5... | collective-permute-start | bytes 811016 | tf_op jit(solution)/shard_map/ppermute | solution.py:601
  139.3 14.4 %collective-permute-start.45 = (bf16[416,768]{1,0:T(8,128)(2,1)S(1)}, bf16[416,768]{1,0:T(8,128)(2,1)S(1)}, u32[]{:S(2)}, u32[]{:S(2)}) collective-permute-start(bf16[416,768]{1,0:T(8,128)(2,1)S(1)} %get-tuple-element.267), channel_id=1, source_target_pairs={{0,1},{1,0},{2,3},{3,2},{4,5},{5,4},{6,7},{7,6},{8,9},{9,8},{10,11... | collective-permute-start | bytes 1916936 | tf_op jit(solution)/shard_map/ppermute | solution.py:580
  152.0 9.4 %collective-permute-start.51 = (bf16[96,1408]{1,0:T(8,128)(2,1)S(1)}, bf16[96,1408]{1,0:T(8,128)(2,1)S(1)}, u32[]{:S(2)}, u32[]{:S(2)}) collective-permute-start(bf16[96,1408]{1,0:T(8,128)(2,1)S(1)} %add_convert_fusion.6), channel_id=1, source_target_pairs={{0,16},{4,20},{8,0},{12,4},{24,8},{28,12},{16,24},{20,28},{1,17},{... | collective-permute-start | bytes 811016 | tf_op jit(solution)/shard_map/ppermute | solution.py:617
  152.7 15.0 %collective-permute-start.56 = (bf16[96,1536]{1,0:T(8,128)(2,1)S(1)}, bf16[96,1536]{1,0:T(8,128)(2,1)S(1)}, u32[]{:S(2)}, u32[]{:S(2)}) collective-permute-start(bf16[96,1536]{1,0:T(8,128)(2,1)S(1)} %get-tuple-element.290), channel_id=1, source_target_pairs={{0,16},{4,20},{8,0},{12,4},{24,8},{28,12},{16,24},{20,28},{1,17},{... | collective-permute-start | bytes 884744 | tf_op jit(solution)/shard_map/ppermute | solution.py:617
  153.9 18.3 %collective-permute-start.50 = (bf16[320,768]{1,0:T(8,128)(2,1)S(1)}, bf16[320,768]{1,0:T(8,128)(2,1)S(1)}, u32[]{:S(2)}, u32[]{:S(2)}) collective-permute-start(bf16[320,768]{1,0:T(8,128)(2,1)S(1)} %input_pair.1.sent), channel_id=1, source_target_pairs={{0,2},{1,3},{2,0},{3,1},{4,6},{5,7},{6,4},{7,5},{8,10},{9,11},{10,... | collective-permute-start | bytes 1474568 | tf_op jit(solution)/shard_map/ppermute | solution.py:580
  161.5 10.7 %collective-permute-start.53 = (bf16[96,1408]{1,0:T(8,128)(2,1)S(1)}, bf16[96,1408]{1,0:T(8,128)(2,1)S(1)}, u32[]{:S(2)}, u32[]{:S(2)}) collective-permute-start(bf16[96,1408]{1,0:T(8,128)(2,1)S(1)} %add_convert_fusion.5), channel_id=1, source_target_pairs={{0,16},{4,20},{8,0},{12,4},{24,8},{28,12},{16,24},{20,28},{1,17},{... | collective-permute-start | bytes 811016 | tf_op jit(solution)/shard_map/ppermute | solution.py:617
  163.2 9.0 %collective-permute-start.54 = (bf16[96,1408]{1,0:T(8,128)(2,1)S(1)}, bf16[96,1408]{1,0:T(8,128)(2,1)S(1)}, u32[]{:S(2)}, u32[]{:S(2)}) collective-permute-start(bf16[96,1408]{1,0:T(8,128)(2,1)S(1)} %get-tuple-element.283), channel_id=1, source_target_pairs={{0,4},{4,0},{8,12},{12,8},{16,20},{20,16},{24,28},{28,24},{1,5},{5... | collective-permute-start | bytes 811016 | tf_op jit(solution)/shard_map/ppermute | solution.py:601
  172.3 9.8 %collective-permute-start.55 = (bf16[96,1408]{1,0:T(8,128)(2,1)S(1)}, bf16[96,1408]{1,0:T(8,128)(2,1)S(1)}, u32[]{:S(2)}, u32[]{:S(2)}) collective-permute-start(bf16[96,1408]{1,0:T(8,128)(2,1)S(1)} %add_convert_fusion.4), channel_id=1, source_target_pairs={{0,16},{4,20},{8,0},{12,4},{24,8},{28,12},{16,24},{20,28},{1,17},{... | collective-permute-start | bytes 811016 | tf_op jit(solution)/shard_map/ppermute | solution.py:617
  (63 other events, 410.7 us)

commit v6 on v5

--- a/solution.py
+++ b/solution.py
@@ -353,7 +353,7 @@
 
 
 def norm_one_body(h0, h1, h2, du2, n1, i1, norms, two, wo, c0, c1, c2, c3, *refs):
-    d0, d2, d3, core, du1, w_own, w_across, scr = refs
+    d0, d2, d3, core, du1, w_own, w_across, scr, whole = refs
     wide = d0.shape[1]
     dh = du2[...] + (h0[...] + h1[1].astype(f32) + h2[...].astype(f32))
     width = dh.shape[1]
@@ -376,18 +376,12 @@
     )
     half = width // 2
     for k, c in enumerate((c0, c1, c2, c3)):
-        g = dot_tn(c[...], low).astype(bf16)
-        q = partner(k)
-        tail = pl.ds(pl.multiple_of(width + lax.rem(q, 2) * wide, 64), wide)
-        for t in range(RANKS):
-            scr[t, block(scr, q, wide)] = g[:, wide * t : wide * t + 128]
-        for side in (0, 1):
-
-            @pl.when(lax.div(q, 2) == side)
-            def _():
-                for t in range(RANKS):
-                    rest = g[:, wide * t + 128 : wide * t + wide]
-                    scr[t, tail, 64 * side : 64 * side + 64] = rest
+        whole[block(whole, partner(k), wide)] = dot_tn(c[...], low).astype(bf16)
+    for t in range(RANKS):
+        at = wide * t
+        scr[t, :width] = whole[:, at : at + 128]
+        rest = slice(at + 128, at + wide)
+        scr[t, width : width + half] = jnp.concatenate([whole[:half, rest], whole[half:, rest]], 1)
 
     low_sums = sums[:8].astype(bf16)
     for t in range(RANKS):
@@ -719,8 +713,8 @@
         g3, x2, xc, segq, segk = fence(g3, x2, xc, segq, segk)
         f1, x3 = along_ring(after(ff_slab, g3)), over_x(g3)
         (xw,) = join_rows(xw_own, xb, xa, xc)
-        x3, f1, y0, xw = fence(x3, f1, y0, xw)
-        f2 = along_ring(f1)
+        x3, y0 = after((x3, y0), xw)
+        f2 = along_ring(after(f1, y0, x3))
         slabs = [slab, x0, g1, x1, g2, x2, g3, x3]
     else:
         vec = jnp.concatenate([norm_gain[0], norm_bias[0]], 0).T
@@ -866,7 +860,7 @@
         [((mine, wide), bf16)] * 3
         + [((2 * packed + mine * 3 // 2, 128), bf16), ((mine, width), f32)]
         + [((packed, 128), bf16)] * 2,
-        [pltpu.VMEM((RANKS, packed, 128), bf16)],
+        [pltpu.VMEM((RANKS, packed, 128), bf16), pltpu.VMEM((width, width), bf16)],
         vmem=12,
     )
     d0, d2, d3, core, du1, wo_own, across = norm_one(

time: 189 us -> 188 us (level)
  no operation moved by 1% of the time
where the time goes in v6:
time: 188 us; the launch traced here: 187 us
  waiting for transfers between devices  84.4 us (45%)
  starting transfers between devices  57.4 us (31%)
  Pallas kernels  33.7 us (18%)
  local copies, waits for them, and re-layouts  9.02 us (5%)
    ppermute x14, waiting for transfers between devices, over_x(): return lax.ppermute(x, 'seq', [(i, i ^ 1) for i in range(8)])  36.2 us
    pallas_call x28, Pallas kernels, run(): pl.pallas_call(body, name=name, out_shape=[jax.ShapeDtypeStruct(s, t) for...  33.7 us
    ppermute x15, waiting for transfers between devices, along_ring(): lax.ppermute(x, 'seq', [(2 * z + i, 2 * to + i) for z, to in route for i...  30.8 us
    ppermute x34, starting transfers between devices, swap(): return lax.ppermute(x, 'blk', [(i, i ^ k) for i in range(RANKS)])  20.5 us
    ppermute x15, starting transfers between devices, along_ring(): lax.ppermute(x, 'seq', [(2 * z + i, 2 * to + i) for z, to in route for i...  20.4 us
    ppermute x34, waiting for transfers between devices, swap(): return lax.ppermute(x, 'blk', [(i, i ^ k) for i in range(RANKS)])  17.4 us
    ppermute x14, starting transfers between devices, over_x(): return lax.ppermute(x, 'seq', [(i, i ^ 1) for i in range(8)])  14.8 us
    unnamed x44, local copies, waits for them, and re-layouts  7.59 us
  transfers between devices with their start and end apart: 65, of which 33 were waited for; matrix products, arithmetic and copies ran while one was open for 1% of the time, Pallas kernels for 14%

profile of v6, /device:TPU:0, one launch (start us, length us, event | category | flops | bytes accessed | tf_op | source)
XLA Modules:
  0.0 187.1 jit_solution(18164551917290729452)
XLA Ops:
  3.2 2.6 %collective-permute-start.1 = (bf16[24,1408]{1,0:T(8,128)(2,1)}, bf16[24,1408]{1,0:T(8,128)(2,1)S(1)}, u32[]{:S(2)}, u32[]{:S(2)}) collective-permute-start(bf16[24,1408]{1,0:T(8,128)(2,1)} %get-tuple-element.161), channel_id=1, source_target_pairs={{0,2},{1,3},{2,0},{3,1},{4,6},{5,7},{6,4},{7,5},{8,10},{9,11},{10,... | collective-permute-start | bytes 202760 | tf_op jit(solution)/shard_map/ppermute | solution.py:574
  14.9 3.9 %collective-permute-done.4.r_1_ = bf16[96,1408]{1,0:T(8,128)(2,1)S(1)} collective-permute-done((bf16[96,1408]{1,0:T(8,128)(2,1)S(1)}, bf16[96,1408]{1,0:T(8,128)(2,1)S(1)}, u32[]{:S(2)}, u32[]{:S(2)}) %collective-permute-start.4) | collective-permute-done | bytes 270368 | tf_op jit(solution)/shard_map/ppermute | solution.py:595
  18.8 2.1 %collective-permute-done.3.r_2_ = bf16[96,1408]{1,0:T(8,128)(2,1)S(1)} collective-permute-done((bf16[96,1408]{1,0:T(8,128)(2,1)S(1)}, bf16[96,1408]{1,0:T(8,128)(2,1)S(1)}, u32[]{:S(2)}, u32[]{:S(2)}) %collective-permute-start.3) | collective-permute-done | bytes 270368 | tf_op jit(solution)/shard_map/ppermute | solution.py:611
  26.7 2.8 %collective-permute-done.9.p2 = bf16[24,768]{1,0:T(8,128)(2,1)S(1)} collective-permute-done((bf16[24,768]{1,0:T(8,128)(2,1)S(1)}, bf16[24,768]{1,0:T(8,128)(2,1)S(1)}, u32[]{:S(2)}, u32[]{:S(2)}) %collective-permute-start.9) | collective-permute-done | bytes 36896 | tf_op jit(solution)/shard_map/ppermute | solution.py:595
  35.5 3.4 %collective-permute-done.13.r_3_ = bf16[96,1408]{1,0:T(8,128)(2,1)S(1)} collective-permute-done((bf16[96,1408]{1,0:T(8,128)(2,1)S(1)}, bf16[96,1408]{1,0:T(8,128)(2,1)S(1)}, u32[]{:S(2)}, u32[]{:S(2)}) %collective-permute-start.13) | collective-permute-done | bytes 270368 | tf_op jit(solution)/shard_map/ppermute | solution.py:595
  53.3 4.8 %attend.1 = (bf16[160,192]{1,0:T(8,128)(2,1)S(1)}, bf16[160,192]{1,0:T(8,128)(2,1)S(1)}, bf16[160,192]{1,0:T(8,128)(2,1)S(1)}, bf16[160,192]{1,0:T(8,128)(2,1)S(...) custom-call(bf16[512,768]{1,0:T(8,128)(2,1)S(1)} %join_rows.1.r_0_.x, ...), custom_call_target="tpu_custom_call" | custom-call | flops 7000000 | bytes 7000 | tf_op jit(solution)/shard_map/attend/pallas_call | solution.py:34
  60.1 2.9 %collective-permute-start.25 = (bf16[96,1536]{1,0:T(8,128)(2,1)}, bf16[96,1536]{1,0:T(8,128)(2,1)S(1)}, u32[]{:S(2)}, u32[]{:S(2)}) collective-permute-start(bf16[96,1536]{1,0:T(8,128)(2,1)} %collective-permute-done.24.r_4_), channel_id=1, source_target_pairs={{0,8},{4,12},{8,24},{12,28},{24,16},{28,20},{16,0},{20,4},{1,9},{5... | collective-permute-start | bytes 884744 | tf_op jit(solution)/shard_map/ppermute | solution.py:611
  66.1 4.4 %collective-permute-done.25.r_5_ = bf16[96,1536]{1,0:T(8,128)(2,1)S(1)} collective-permute-done((bf16[96,1536]{1,0:T(8,128)(2,1)}, bf16[96,1536]{1,0:T(8,128)(2,1)S(1)}, u32[]{:S(2)}, u32[]{:S(2)}) %collective-permute-start.25) | collective-permute-done | bytes 294944 | tf_op jit(solution)/shard_map/ppermute | solution.py:611
  76.3 4.0 %collective-permute-done.27.h2 = bf16[160,768]{1,0:T(8,128)(2,1)S(1)} collective-permute-done((bf16[160,768]{1,0:T(8,128)(2,1)S(1)}, bf16[160,768]{1,0:T(8,128)(2,1)S(1)}, u32[]{:S(2)}, u32[]{:S(2)}) %collective-permute-start.27) | collective-permute-done | bytes 245792 | tf_op jit(solution)/shard_map/ppermute | solution.py:595
  82.6 2.3 %feed.1 = (f32[160,768]{1,0:T(8,128)S(1)}, bf16[160,768]{1,0:T(8,128)(2,1)S(1)}, bf16[2,160,768]{2,1,0:T(8,128)(2,1)S(1)}, bf16[4,160,768]{2,1,0:T(8,128)(2,1)S(1)}, bf16[4,160,768]{2,1,0:T(8,128)(2,1)S(1)}) custom-call(bf16[160,768]{1,0:T(8,128)(2,1)S(1)} %get-tuple-element.209.h0, bf16[160,768]{1,0:T(8,128)(2,1)S(1)} %collective-permute-done.26.h1, ...), custom_call_target="tpu_custom_call" | custom-call | flops 3000000 | bytes 3000 | tf_op jit(solution)/shard_map/feed/pallas_call | solution.py:34
  88.0 7.0 %collective-permute-done.33.f2 = bf16[160,768]{1,0:T(8,128)(2,1)S(1)} collective-permute-done((bf16[160,768]{1,0:T(8,128)(2,1)S(1)}, bf16[160,768]{1,0:T(8,128)(2,1)S(1)}, u32[]{:S(2)}, u32[]{:S(2)}) %collective-permute-start.33) | collective-permute-done | bytes 245792 | tf_op jit(solution)/shard_map/ppermute | solution.py:595
  97.1 6.2 %collective-permute-done.35.d2 = bf16[160,768]{1,0:T(8,128)(2,1)S(1)} collective-permute-done((bf16[160,768]{1,0:T(8,128)(2,1)S(1)}, bf16[160,768]{1,0:T(8,128)(2,1)S(1)}, u32[]{:S(2)}, u32[]{:S(2)}) %collective-permute-start.35) | collective-permute-done | bytes 245792 | tf_op jit(solution)/shard_map/ppermute | solution.py:595
  109.6 2.1 %feed_grads.1 = (bf16[96,1536]{1,0:T(8,128)(2,1)S(1)}, bf16[96,1536]{1,0:T(8,128)(2,1)S(1)}, bf16[96,1536]{1,0:T(8,128)(2,1)S(1)}, bf16[96,1536]{1,0:T(8,128)(2,...) custom-call(bf16[160,768]{1,0:T(8,128)(2,1)S(1)} %get-tuple-element., ...), custom_call_target="tpu_custom_call" | custom-call | flops 3000000 | bytes 3000 | tf_op jit(solution)/shard_map/feed_grads/pallas_call | solution.py:34
  111.8 2.7 %collective-permute-start.43 = (bf16[96,1536]{1,0:T(8,128)(2,1)S(1)}, bf16[96,1536]{1,0:T(8,128)(2,1)S(1)}, u32[]{:S(2)}, u32[]{:S(2)}) collective-permute-start(bf16[96,1536]{1,0:T(8,128)(2,1)S(1)} %get-tuple-element.235), channel_id=1, source_target_pairs={{0,8},{4,12},{8,24},{12,28},{24,16},{28,20},{16,0},{20,4},{1,9},{5... | collective-permute-start | bytes 884744 | tf_op jit(solution)/shard_map/ppermute | solution.py:611
  121.7 2.7 %collective-permute-done.42 = bf16[96,1536]{1,0:T(8,128)(2,1)S(1)} collective-permute-done((bf16[96,1536]{1,0:T(8,128)(2,1)S(1)}, bf16[96,1536]{1,0:T(8,128)(2,1)S(1)}, u32[]{:S(2)}, u32[]{:S(2)}) %collective-permute-start.42) | collective-permute-done | bytes 294944 | tf_op jit(solution)/shard_map/ppermute | solution.py:574
  127.6 4.8 %attend_back.1.dqkv = bf16[640,768]{1,0:T(8,128)(2,1)S(1)} custom-call(bf16[160,192]{1,0:T(8,128)(2,1)S(1)} %get-tuple-element.251.r_0_, bf16[2640,128]{1,0:T(8,128)(2,1)S(1)} %collective-permute-done.39.r_1_.o1, bf16[160,192]{1,0:T(8,128)(2,1)S(1)} %collective-permute-done.40.r_2_, bf16[160,192]{1,0:T(8,128)(2,1)S(1)} %collective-permute-done.41.r_3_, ...), custom_call_target="tpu_custom_call" | custom-call | flops 7000000 | bytes 7000 | tf_op jit(solution)/shard_map/attend_back/pallas_call | solution.py:34
  138.4 4.2 %collective-permute-done.48.a2 = bf16[96,1536]{1,0:T(8,128)(2,1)S(1)} collective-permute-done((bf16[96,1536]{1,0:T(8,128)(2,1)S(1)}, bf16[96,1536]{1,0:T(8,128)(2,1)S(1)}, u32[]{:S(2)}, u32[]{:S(2)}) %collective-permute-start.48) | collective-permute-done | bytes 294944 | tf_op jit(solution)/shard_map/ppermute | solution.py:611
  142.6 6.7 %collective-permute-done.49 = bf16[96,1536]{1,0:T(8,128)(2,1)S(1)} collective-permute-done((bf16[96,1536]{1,0:T(8,128)(2,1)S(1)}, bf16[96,1536]{1,0:T(8,128)(2,1)S(1)}, u32[]{:S(2)}, u32[]{:S(2)}) %collective-permute-start.49) | collective-permute-done | bytes 294944 | tf_op jit(solution)/shard_map/ppermute | solution.py:611
  152.7 4.6 %collective-permute-done.52 = bf16[96,1408]{1,0:T(8,128)(2,1)S(1)} collective-permute-done((bf16[96,1408]{1,0:T(8,128)(2,1)S(1)}, bf16[96,1408]{1,0:T(8,128)(2,1)S(1)}, u32[]{:S(2)}, u32[]{:S(2)}) %collective-permute-start.52) | collective-permute-done | bytes 270368 | tf_op jit(solution)/shard_map/ppermute | solution.py:595
  157.3 2.5 %collective-permute-done.51 = bf16[96,1408]{1,0:T(8,128)(2,1)S(1)} collective-permute-done((bf16[96,1408]{1,0:T(8,128)(2,1)S(1)}, bf16[96,1408]{1,0:T(8,128)(2,1)S(1)}, u32[]{:S(2)}, u32[]{:S(2)}) %collective-permute-start.51) | collective-permute-done | bytes 270368 | tf_op jit(solution)/shard_map/ppermute | solution.py:611
  163.0 3.1 %collective-permute-done.56 = bf16[96,1536]{1,0:T(8,128)(2,1)S(1)} collective-permute-done((bf16[96,1536]{1,0:T(8,128)(2,1)S(1)}, bf16[96,1536]{1,0:T(8,128)(2,1)S(1)}, u32[]{:S(2)}, u32[]{:S(2)}) %collective-permute-start.56) | collective-permute-done | bytes 294944 | tf_op jit(solution)/shard_map/ppermute | solution.py:611
  166.7 3.4 %collective-permute-done.53 = bf16[96,1408]{1,0:T(8,128)(2,1)S(1)} collective-permute-done((bf16[96,1408]{1,0:T(8,128)(2,1)S(1)}, bf16[96,1408]{1,0:T(8,128)(2,1)S(1)}, u32[]{:S(2)}, u32[]{:S(2)}) %collective-permute-start.53) | collective-permute-done | bytes 270368 | tf_op jit(solution)/shard_map/ppermute | solution.py:611
  176.9 2.8 %collective-permute-done.59.c2 = bf16[24,768]{1,0:T(8,128)(2,1)S(1)} collective-permute-done((bf16[24,768]{1,0:T(8,128)(2,1)S(1)}, bf16[24,768]{1,0:T(8,128)(2,1)S(1)}, u32[]{:S(2)}, u32[]{:S(2)}) %collective-permute-start.59) | collective-permute-done | bytes 36896 | tf_op jit(solution)/shard_map/ppermute | solution.py:595
  182.7 3.3 %collective-permute-done.63.c2 = bf16[24,1408]{1,0:T(8,128)(2,1)S(1)} collective-permute-done((bf16[24,1408]{1,0:T(8,128)(2,1)S(1)}, bf16[24,1408]{1,0:T(8,128)(2,1)S(1)}, u32[]{:S(2)}, u32[]{:S(2)}) %collective-permute-start.63) | collective-permute-done | bytes 67616 | tf_op jit(solution)/shard_map/ppermute | solution.py:574
  (193 shorter events, 96.1 us)
Async XLA Ops:
  11.8 9.1 %collective-permute-start.3 = (bf16[96,1408]{1,0:T(8,128)(2,1)S(1)}, bf16[96,1408]{1,0:T(8,128)(2,1)S(1)}, u32[]{:S(2)}, u32[]{:S(2)}) collective-permute-start(bf16[96,1408]{1,0:T(8,128)(2,1)S(1)} %arrange.1.r_0_), channel_id=1, source_target_pairs={{0,8},{4,12},{8,24},{12,28},{24,16},{28,20},{16,0},{20,4},{1,9},{5... | collective-permute-start | bytes 811016 | tf_op jit(solution)/shard_map/ppermute | solution.py:611
  13.6 16.0 %collective-permute-start.11 = (bf16[128,768]{1,0:T(8,128)(2,1)S(1)}, bf16[128,768]{1,0:T(8,128)(2,1)S(1)}, u32[]{:S(2)}, u32[]{:S(2)}) collective-permute-start(bf16[128,768]{1,0:T(8,128)(2,1)S(1)} %bitcast.46), channel_id=1, source_target_pairs={{0,2},{1,3},{2,0},{3,1},{4,6},{5,7},{6,4},{7,5},{8,10},{9,11},{10,... | collective-permute-start | bytes 589832 | tf_op jit(solution)/shard_map/ppermute | solution.py:574
  20.9 8.6 %collective-permute-start.7 = (bf16[96,1408]{1,0:T(8,128)(2,1)S(1)}, bf16[96,1408]{1,0:T(8,128)(2,1)S(1)}, u32[]{:S(2)}, u32[]{:S(2)}) collective-permute-start(bf16[96,1408]{1,0:T(8,128)(2,1)S(1)} %collective-permute-done.3.r_2_), channel_id=1, source_target_pairs={{0,4},{4,0},{8,12},{12,8},{16,20},{20,16},{24,28},{28,24},{1,5},{5... | collective-permute-start | bytes 811016 | tf_op jit(solution)/shard_map/ppermute | solution.py:595
  21.5 8.8 %collective-permute-start.6 = (bf16[96,1408]{1,0:T(8,128)(2,1)S(1)}, bf16[96,1408]{1,0:T(8,128)(2,1)S(1)}, u32[]{:S(2)}, u32[]{:S(2)}) collective-permute-start(bf16[96,1408]{1,0:T(8,128)(2,1)S(1)} %collective-permute-done.3.r_2_), channel_id=1, source_target_pairs={{0,8},{4,12},{8,24},{12,28},{24,16},{28,20},{16,0},{20,4},{1,9},{5... | collective-permute-start | bytes 811016 | tf_op jit(solution)/shard_map/ppermute | solution.py:611
  31.0 9.4 %collective-permute-start.12 = (bf16[96,1408]{1,0:T(8,128)(2,1)S(1)}, bf16[96,1408]{1,0:T(8,128)(2,1)S(1)}, u32[]{:S(2)}, u32[]{:S(2)}) collective-permute-start(bf16[96,1408]{1,0:T(8,128)(2,1)S(1)} %collective-permute-done.6.r_4_), channel_id=1, source_target_pairs={{0,8},{4,12},{8,24},{12,28},{24,16},{28,20},{16,0},{20,4},{1,9},{5... | collective-permute-start | bytes 811016 | tf_op jit(solution)/shard_map/ppermute | solution.py:611
  34.0 13.1 %collective-permute-start.16 = (bf16[96,1536]{1,0:T(8,128)(2,1)S(1)}, bf16[96,1536]{1,0:T(8,128)(2,1)S(1)}, u32[]{:S(2)}, u32[]{:S(2)}) collective-permute-start(bf16[96,1536]{1,0:T(8,128)(2,1)S(1)} %arrange_ff.1.r_0_), channel_id=1, source_target_pairs={{0,2},{1,3},{2,0},{3,1},{4,6},{5,7},{6,4},{7,5},{8,10},{9,11},{10,... | collective-permute-start | bytes 884744 | tf_op jit(solution)/shard_map/ppermute | solution.py:574
  41.5 8.7 %collective-permute-start.23 = (bf16[96,1536]{1,0:T(8,128)(2,1)S(1)}, bf16[96,1536]{1,0:T(8,128)(2,1)}, u32[]{:S(2)}, u32[]{:S(2)}) collective-permute-start(bf16[96,1536]{1,0:T(8,128)(2,1)S(1)} %arrange_ff.1.r_0_), channel_id=1, source_target_pairs={{0,8},{4,12},{8,24},{12,28},{24,16},{28,20},{16,0},{20,4},{1,9},{5... | collective-permute-start | bytes 884744 | tf_op jit(solution)/shard_map/ppermute | solution.py:611
  48.9 9.2 %collective-permute-start.17 = (bf16[1152,128]{1,0:T(8,128)(2,1)}, bf16[1152,128]{1,0:T(8,128)(2,1)}, u32[]{:S(2)}, u32[]{:S(2)}) collective-permute-start(bf16[1152,128]{1,0:T(8,128)(2,1)} %get-tuple-element.204.w0), channel_id=1, source_target_pairs={{0,1},{1,0},{2,3},{3,2},{4,5},{5,4},{6,7},{7,6},{8,9},{9,8},{10,11... | collective-permute-start | bytes 884744 | tf_op jit(solution)/shard_map/ppermute | solution.py:574
  50.2 9.8 %collective-permute-start.24 = (bf16[96,1536]{1,0:T(8,128)(2,1)}, bf16[96,1536]{1,0:T(8,128)(2,1)}, u32[]{:S(2)}, u32[]{:S(2)}) collective-permute-start(bf16[96,1536]{1,0:T(8,128)(2,1)} %collective-permute-done.23.r_2_), channel_id=1, source_target_pairs={{0,8},{4,12},{8,24},{12,28},{24,16},{28,20},{16,0},{20,4},{1,9},{5... | collective-permute-start | bytes 884744 | tf_op jit(solution)/shard_map/ppermute | solution.py:611
  51.5 11.5 %collective-permute-start.21 = (bf16[1152,128]{1,0:T(8,128)(2,1)}, bf16[1152,128]{1,0:T(8,128)(2,1)}, u32[]{:S(2)}, u32[]{:S(2)}) collective-permute-start(bf16[1152,128]{1,0:T(8,128)(2,1)} %get-tuple-element.204.w0), channel_id=1, source_target_pairs={{0,2},{1,3},{2,0},{3,1},{4,6},{5,7},{6,4},{7,5},{8,10},{9,11},{10,... | collective-permute-start | bytes 884744 | tf_op jit(solution)/shard_map/ppermute | solution.py:574
  60.1 10.4 %collective-permute-start.25 = (bf16[96,1536]{1,0:T(8,128)(2,1)}, bf16[96,1536]{1,0:T(8,128)(2,1)S(1)}, u32[]{:S(2)}, u32[]{:S(2)}) collective-permute-start(bf16[96,1536]{1,0:T(8,128)(2,1)} %collective-permute-done.24.r_4_), channel_id=1, source_target_pairs={{0,8},{4,12},{8,24},{12,28},{24,16},{28,20},{16,0},{20,4},{1,9},{5... | collective-permute-start | bytes 884744 | tf_op jit(solution)/shard_map/ppermute | solution.py:611
  64.9 10.1 %collective-permute-start.28 = (bf16[96,1536]{1,0:T(8,128)(2,1)}, bf16[96,1536]{1,0:T(8,128)(2,1)S(1)}, u32[]{:S(2)}, u32[]{:S(2)}) collective-permute-start(bf16[96,1536]{1,0:T(8,128)(2,1)} %collective-permute-done.23.r_2_), channel_id=1, source_target_pairs={{0,2},{1,3},{2,0},{3,1},{4,6},{5,7},{6,4},{7,5},{8,10},{9,11},{10,... | collective-permute-start | bytes 884744 | tf_op jit(solution)/shard_map/ppermute | solution.py:574
  111.8 9.9 %collective-permute-start.43 = (bf16[96,1536]{1,0:T(8,128)(2,1)S(1)}, bf16[96,1536]{1,0:T(8,128)(2,1)S(1)}, u32[]{:S(2)}, u32[]{:S(2)}) collective-permute-start(bf16[96,1536]{1,0:T(8,128)(2,1)S(1)} %get-tuple-element.235), channel_id=1, source_target_pairs={{0,8},{4,12},{8,24},{12,28},{24,16},{28,20},{16,0},{20,4},{1,9},{5... | collective-permute-start | bytes 884744 | tf_op jit(solution)/shard_map/ppermute | solution.py:611
  114.5 9.9 %collective-permute-start.42 = (bf16[96,1536]{1,0:T(8,128)(2,1)S(1)}, bf16[96,1536]{1,0:T(8,128)(2,1)S(1)}, u32[]{:S(2)}, u32[]{:S(2)}) collective-permute-start(bf16[96,1536]{1,0:T(8,128)(2,1)S(1)} %get-tuple-element.238), channel_id=1, source_target_pairs={{0,2},{1,3},{2,0},{3,1},{4,6},{5,7},{6,4},{7,5},{8,10},{9,11},{10,... | collective-permute-start | bytes 884744 | tf_op jit(solution)/shard_map/ppermute | solution.py:574
  126.0 10.0 %collective-permute-start.46 = (bf16[1200,128]{1,0:T(8,128)(2,1)S(1)}, bf16[1200,128]{1,0:T(8,128)(2,1)S(1)}, u32[]{:S(2)}, u32[]{:S(2)}) collective-permute-start(bf16[1200,128]{1,0:T(8,128)(2,1)S(1)} %add_convert_fusion), channel_id=1, source_target_pairs={{0,2},{1,3},{2,0},{3,1},{4,6},{5,7},{6,4},{7,5},{8,10},{9,11},{10,... | collective-permute-start | bytes 921608 | tf_op jit(solution)/shard_map/ppermute | solution.py:574
  132.6 10.0 %collective-permute-start.48 = (bf16[96,1536]{1,0:T(8,128)(2,1)S(1)}, bf16[96,1536]{1,0:T(8,128)(2,1)S(1)}, u32[]{:S(2)}, u32[]{:S(2)}) collective-permute-start(bf16[96,1536]{1,0:T(8,128)(2,1)S(1)} %add_convert_fusion.2), channel_id=1, source_target_pairs={{0,16},{4,20},{8,0},{12,4},{24,8},{28,12},{16,24},{20,28},{1,17},{... | collective-permute-start | bytes 884744 | tf_op jit(solution)/shard_map/ppermute | solution.py:611
  133.5 15.8 %collective-permute-start.49 = (bf16[96,1536]{1,0:T(8,128)(2,1)S(1)}, bf16[96,1536]{1,0:T(8,128)(2,1)S(1)}, u32[]{:S(2)}, u32[]{:S(2)}) collective-permute-start(bf16[96,1536]{1,0:T(8,128)(2,1)S(1)} %get-tuple-element.271), channel_id=1, source_target_pairs={{0,8},{4,12},{8,24},{12,28},{24,16},{28,20},{16,0},{20,4},{1,9},{5... | collective-permute-start | bytes 884744 | tf_op jit(solution)/shard_map/ppermute | solution.py:611
  137.3 11.9 %collective-permute-start.47 = (bf16[96,1408]{1,0:T(8,128)(2,1)S(1)}, bf16[96,1408]{1,0:T(8,128)(2,1)S(1)}, u32[]{:S(2)}, u32[]{:S(2)}) collective-permute-start(bf16[96,1408]{1,0:T(8,128)(2,1)S(1)} %get-tuple-element.269), channel_id=1, source_target_pairs={{0,4},{4,0},{8,12},{12,8},{16,20},{20,16},{24,28},{28,24},{1,5},{5... | collective-permute-start | bytes 811016 | tf_op jit(solution)/shard_map/ppermute | solution.py:595
  138.4 13.7 %collective-permute-start.45 = (bf16[416,768]{1,0:T(8,128)(2,1)S(1)}, bf16[416,768]{1,0:T(8,128)(2,1)S(1)}, u32[]{:S(2)}, u32[]{:S(2)}) collective-permute-start(bf16[416,768]{1,0:T(8,128)(2,1)S(1)} %get-tuple-element.265), channel_id=1, source_target_pairs={{0,1},{1,0},{2,3},{3,2},{4,5},{5,4},{6,7},{7,6},{8,9},{9,8},{10,11... | collective-permute-start | bytes 1916936 | tf_op jit(solution)/shard_map/ppermute | solution.py:574
  150.4 9.4 %collective-permute-start.51 = (bf16[96,1408]{1,0:T(8,128)(2,1)S(1)}, bf16[96,1408]{1,0:T(8,128)(2,1)S(1)}, u32[]{:S(2)}, u32[]{:S(2)}) collective-permute-start(bf16[96,1408]{1,0:T(8,128)(2,1)S(1)} %add_convert_fusion.6), channel_id=1, source_target_pairs={{0,16},{4,20},{8,0},{12,4},{24,8},{28,12},{16,24},{20,28},{1,17},{... | collective-permute-start | bytes 811016 | tf_op jit(solution)/shard_map/ppermute | solution.py:611
  151.5 14.6 %collective-permute-start.56 = (bf16[96,1536]{1,0:T(8,128)(2,1)S(1)}, bf16[96,1536]{1,0:T(8,128)(2,1)S(1)}, u32[]{:S(2)}, u32[]{:S(2)}) collective-permute-start(bf16[96,1536]{1,0:T(8,128)(2,1)S(1)} %get-tuple-element.288), channel_id=1, source_target_pairs={{0,16},{4,20},{8,0},{12,4},{24,8},{28,12},{16,24},{20,28},{1,17},{... | collective-permute-start | bytes 884744 | tf_op jit(solution)/shard_map/ppermute | solution.py:611
  152.2 17.9 %collective-permute-start.50 = (bf16[320,768]{1,0:T(8,128)(2,1)S(1)}, bf16[320,768]{1,0:T(8,128)(2,1)S(1)}, u32[]{:S(2)}, u32[]{:S(2)}) collective-permute-start(bf16[320,768]{1,0:T(8,128)(2,1)S(1)} %input_pair.1.sent), channel_id=1, source_target_pairs={{0,2},{1,3},{2,0},{3,1},{4,6},{5,7},{6,4},{7,5},{8,10},{9,11},{10,... | collective-permute-start | bytes 1474568 | tf_op jit(solution)/shard_map/ppermute | solution.py:574
  160.0 10.2 %collective-permute-start.53 = (bf16[96,1408]{1,0:T(8,128)(2,1)S(1)}, bf16[96,1408]{1,0:T(8,128)(2,1)S(1)}, u32[]{:S(2)}, u32[]{:S(2)}) collective-permute-start(bf16[96,1408]{1,0:T(8,128)(2,1)S(1)} %add_convert_fusion.5), channel_id=1, source_target_pairs={{0,16},{4,20},{8,0},{12,4},{24,8},{28,12},{16,24},{20,28},{1,17},{... | collective-permute-start | bytes 811016 | tf_op jit(solution)/shard_map/ppermute | solution.py:611
  170.2 10.3 %collective-permute-start.55 = (bf16[96,1408]{1,0:T(8,128)(2,1)S(1)}, bf16[96,1408]{1,0:T(8,128)(2,1)S(1)}, u32[]{:S(2)}, u32[]{:S(2)}) collective-permute-start(bf16[96,1408]{1,0:T(8,128)(2,1)S(1)} %add_convert_fusion.4), channel_id=1, source_target_pairs={{0,16},{4,20},{8,0},{12,4},{24,8},{28,12},{16,24},{20,28},{1,17},{... | collective-permute-start | bytes 811016 | tf_op jit(solution)/shard_map/ppermute | solution.py:611
  (63 other events, 415.6 us)

commit v7 on v6

--- a/solution.py
+++ b/solution.py
@@ -904,8 +904,8 @@
     if direct:
         fl = along_ring(plus(ff6, after(fl, dqkv)), -1)
         fb, fc = along_ring(after(ff3, dqkv)), along_ring(after(ff7, chunks), -1)
-        part = plus(chunks[2], after(over_x(chunks[3]), fl, fb))
-        cx, cz = over_x(after(chunks[5], part)), along_ring(part, -1)
+        part = plus(chunks[2], after(over_x(chunks[3]), fl))
+        cx, cz = over_x(after(chunks[5], part, fb)), along_ring(part, -1)
         core = after(core, part)
     (sent,) = call(input_pair_body, "input_pair", [((local + ents + 2 * share, width), bf16)])(across, core)
     came = swap(sent, 2)

time: 188 us -> 188 us (level)
    ppermute x14, waiting for transfers between devices: 36.2 us -> 40.7 us  [over_x(): return lax.ppermute(x, 'seq', [(i, i ^ 1) for i in range(8)])]
    ppermute x15, waiting for transfers between devices: 30.8 us -> 26.7 us  [along_ring(): lax.ppermute(x, 'seq', [(2 * z + i, 2 * to + i) for z, to in route for i...]
  transfers between devices with their start and end apart: 65 -> 65, of which waited for: 33 -> 35; matrix products, arithmetic and copies ran while one was open for 1% -> 1% of each run, Pallas kernels for 14% -> 14%
where the time goes in v7:
time: 188 us
  waiting for transfers between devices  85.9 us (46%)
  starting transfers between devices  56.4 us (30%)
  Pallas kernels  33.7 us (18%)
  local copies, waits for them, and re-layouts  9.02 us (5%)
    ppermute x14, waiting for transfers between devices, over_x(): return lax.ppermute(x, 'seq', [(i, i ^ 1) for i in range(8)])  40.7 us
    pallas_call x28, Pallas kernels, run(): pl.pallas_call(body, name=name, out_shape=[jax.ShapeDtypeStruct(s, t) for...  33.7 us
    ppermute x15, waiting for transfers between devices, along_ring(): lax.ppermute(x, 'seq', [(2 * z + i, 2 * to + i) for z, to in route for i...  26.7 us
    ppermute x34, starting transfers between devices, swap(): return lax.ppermute(x, 'blk', [(i, i ^ k) for i in range(RANKS)])  20.9 us
    ppermute x15, starting transfers between devices, along_ring(): lax.ppermute(x, 'seq', [(2 * z + i, 2 * to + i) for z, to in route for i...  19 us
    ppermute x34, waiting for transfers between devices, swap(): return lax.ppermute(x, 'blk', [(i, i ^ k) for i in range(RANKS)])  18.5 us
    ppermute x14, starting transfers between devices, over_x(): return lax.ppermute(x, 'seq', [(i, i ^ 1) for i in range(8)])  14.7 us
    unnamed x44, local copies, waits for them, and re-layouts  7.59 us
  transfers between devices with their start and end apart: 65, of which 35 were waited for; matrix products, arithmetic and copies ran while one was open for 1% of the time, Pallas kernels for 14%

profile of v7, /device:TPU:0, one launch (start us, length us, event | category | flops | bytes accessed | tf_op | source)
XLA Modules:
  0.0 187.6 jit_solution(2570751605041327831)
XLA Ops:
  3.2 2.6 %collective-permute-start.1 = (bf16[24,1408]{1,0:T(8,128)(2,1)}, bf16[24,1408]{1,0:T(8,128)(2,1)S(1)}, u32[]{:S(2)}, u32[]{:S(2)}) collective-permute-start(bf16[24,1408]{1,0:T(8,128)(2,1)} %get-tuple-element.161), channel_id=1, source_target_pairs={{0,2},{1,3},{2,0},{3,1},{4,6},{5,7},{6,4},{7,5},{8,10},{9,11},{10,... | collective-permute-start | bytes 202760 | tf_op jit(solution)/shard_map/ppermute | solution.py:574
  14.9 3.9 %collective-permute-done.4.r_1_ = bf16[96,1408]{1,0:T(8,128)(2,1)S(1)} collective-permute-done((bf16[96,1408]{1,0:T(8,128)(2,1)S(1)}, bf16[96,1408]{1,0:T(8,128)(2,1)S(1)}, u32[]{:S(2)}, u32[]{:S(2)}) %collective-permute-start.4) | collective-permute-done | bytes 270368 | tf_op jit(solution)/shard_map/ppermute | solution.py:595
  18.8 2.1 %collective-permute-done.3.r_2_ = bf16[96,1408]{1,0:T(8,128)(2,1)S(1)} collective-permute-done((bf16[96,1408]{1,0:T(8,128)(2,1)S(1)}, bf16[96,1408]{1,0:T(8,128)(2,1)S(1)}, u32[]{:S(2)}, u32[]{:S(2)}) %collective-permute-start.3) | collective-permute-done | bytes 270368 | tf_op jit(solution)/shard_map/ppermute | solution.py:611
  26.7 2.8 %collective-permute-done.9.p2 = bf16[24,768]{1,0:T(8,128)(2,1)S(1)} collective-permute-done((bf16[24,768]{1,0:T(8,128)(2,1)S(1)}, bf16[24,768]{1,0:T(8,128)(2,1)S(1)}, u32[]{:S(2)}, u32[]{:S(2)}) %collective-permute-start.9) | collective-permute-done | bytes 36896 | tf_op jit(solution)/shard_map/ppermute | solution.py:595
  35.5 3.4 %collective-permute-done.13.r_3_ = bf16[96,1408]{1,0:T(8,128)(2,1)S(1)} collective-permute-done((bf16[96,1408]{1,0:T(8,128)(2,1)S(1)}, bf16[96,1408]{1,0:T(8,128)(2,1)S(1)}, u32[]{:S(2)}, u32[]{:S(2)}) %collective-permute-start.13) | collective-permute-done | bytes 270368 | tf_op jit(solution)/shard_map/ppermute | solution.py:595
  53.3 4.8 %attend.1 = (bf16[160,192]{1,0:T(8,128)(2,1)S(1)}, bf16[160,192]{1,0:T(8,128)(2,1)S(1)}, bf16[160,192]{1,0:T(8,128)(2,1)S(1)}, bf16[160,192]{1,0:T(8,128)(2,1)S(...) custom-call(bf16[512,768]{1,0:T(8,128)(2,1)S(1)} %join_rows.1.r_0_.x, ...), custom_call_target="tpu_custom_call" | custom-call | flops 7000000 | bytes 7000 | tf_op jit(solution)/shard_map/attend/pallas_call | solution.py:34
  60.1 2.9 %collective-permute-start.25 = (bf16[96,1536]{1,0:T(8,128)(2,1)}, bf16[96,1536]{1,0:T(8,128)(2,1)S(1)}, u32[]{:S(2)}, u32[]{:S(2)}) collective-permute-start(bf16[96,1536]{1,0:T(8,128)(2,1)} %collective-permute-done.24.r_4_), channel_id=1, source_target_pairs={{0,8},{4,12},{8,24},{12,28},{24,16},{28,20},{16,0},{20,4},{1,9},{5... | collective-permute-start | bytes 884744 | tf_op jit(solution)/shard_map/ppermute | solution.py:611
  66.1 4.4 %collective-permute-done.25.r_5_ = bf16[96,1536]{1,0:T(8,128)(2,1)S(1)} collective-permute-done((bf16[96,1536]{1,0:T(8,128)(2,1)}, bf16[96,1536]{1,0:T(8,128)(2,1)S(1)}, u32[]{:S(2)}, u32[]{:S(2)}) %collective-permute-start.25) | collective-permute-done | bytes 294944 | tf_op jit(solution)/shard_map/ppermute | solution.py:611
  76.3 4.0 %collective-permute-done.27.h2 = bf16[160,768]{1,0:T(8,128)(2,1)S(1)} collective-permute-done((bf16[160,768]{1,0:T(8,128)(2,1)S(1)}, bf16[160,768]{1,0:T(8,128)(2,1)S(1)}, u32[]{:S(2)}, u32[]{:S(2)}) %collective-permute-start.27) | collective-permute-done | bytes 245792 | tf_op jit(solution)/shard_map/ppermute | solution.py:595
  82.6 2.3 %feed.1 = (f32[160,768]{1,0:T(8,128)S(1)}, bf16[160,768]{1,0:T(8,128)(2,1)S(1)}, bf16[2,160,768]{2,1,0:T(8,128)(2,1)S(1)}, bf16[4,160,768]{2,1,0:T(8,128)(2,1)S(1)}, bf16[4,160,768]{2,1,0:T(8,128)(2,1)S(1)}) custom-call(bf16[160,768]{1,0:T(8,128)(2,1)S(1)} %get-tuple-element.209.h0, bf16[160,768]{1,0:T(8,128)(2,1)S(1)} %collective-permute-done.26.h1, ...), custom_call_target="tpu_custom_call" | custom-call | flops 3000000 | bytes 3000 | tf_op jit(solution)/shard_map/feed/pallas_call | solution.py:34
  88.0 7.0 %collective-permute-done.33.f2 = bf16[160,768]{1,0:T(8,128)(2,1)S(1)} collective-permute-done((bf16[160,768]{1,0:T(8,128)(2,1)S(1)}, bf16[160,768]{1,0:T(8,128)(2,1)S(1)}, u32[]{:S(2)}, u32[]{:S(2)}) %collective-permute-start.33) | collective-permute-done | bytes 245792 | tf_op jit(solution)/shard_map/ppermute | solution.py:595
  97.1 6.2 %collective-permute-done.35.d2 = bf16[160,768]{1,0:T(8,128)(2,1)S(1)} collective-permute-done((bf16[160,768]{1,0:T(8,128)(2,1)S(1)}, bf16[160,768]{1,0:T(8,128)(2,1)S(1)}, u32[]{:S(2)}, u32[]{:S(2)}) %collective-permute-start.35) | collective-permute-done | bytes 245792 | tf_op jit(solution)/shard_map/ppermute | solution.py:595
  109.6 2.1 %feed_grads.1 = (bf16[96,1536]{1,0:T(8,128)(2,1)S(1)}, bf16[96,1536]{1,0:T(8,128)(2,1)S(1)}, bf16[96,1536]{1,0:T(8,128)(2,1)S(1)}, bf16[96,1536]{1,0:T(8,128)(2,...) custom-call(bf16[160,768]{1,0:T(8,128)(2,1)S(1)} %get-tuple-element., ...), custom_call_target="tpu_custom_call" | custom-call | flops 3000000 | bytes 3000 | tf_op jit(solution)/shard_map/feed_grads/pallas_call | solution.py:34
  111.8 2.7 %collective-permute-start.43 = (bf16[96,1536]{1,0:T(8,128)(2,1)S(1)}, bf16[96,1536]{1,0:T(8,128)(2,1)S(1)}, u32[]{:S(2)}, u32[]{:S(2)}) collective-permute-start(bf16[96,1536]{1,0:T(8,128)(2,1)S(1)} %get-tuple-element.235), channel_id=1, source_target_pairs={{0,8},{4,12},{8,24},{12,28},{24,16},{28,20},{16,0},{20,4},{1,9},{5... | collective-permute-start | bytes 884744 | tf_op jit(solution)/shard_map/ppermute | solution.py:611
  121.7 2.7 %collective-permute-done.42 = bf16[96,1536]{1,0:T(8,128)(2,1)S(1)} collective-permute-done((bf16[96,1536]{1,0:T(8,128)(2,1)S(1)}, bf16[96,1536]{1,0:T(8,128)(2,1)S(1)}, u32[]{:S(2)}, u32[]{:S(2)}) %collective-permute-start.42) | collective-permute-done | bytes 294944 | tf_op jit(solution)/shard_map/ppermute | solution.py:574
  127.6 4.8 %attend_back.1.dqkv = bf16[640,768]{1,0:T(8,128)(2,1)S(1)} custom-call(bf16[160,192]{1,0:T(8,128)(2,1)S(1)} %get-tuple-element.251.r_0_, bf16[2640,128]{1,0:T(8,128)(2,1)S(1)} %collective-permute-done.39.r_1_.o1, bf16[160,192]{1,0:T(8,128)(2,1)S(1)} %collective-permute-done.40.r_2_, bf16[160,192]{1,0:T(8,128)(2,1)S(1)} %collective-permute-done.41.r_3_, ...), custom_call_target="tpu_custom_call" | custom-call | flops 7000000 | bytes 7000 | tf_op jit(solution)/shard_map/attend_back/pallas_call | solution.py:34
  139.5 2.5 %collective-permute-done.48.a2 = bf16[96,1536]{1,0:T(8,128)(2,1)S(1)} collective-permute-done((bf16[96,1536]{1,0:T(8,128)(2,1)S(1)}, bf16[96,1536]{1,0:T(8,128)(2,1)S(1)}, u32[]{:S(2)}, u32[]{:S(2)}) %collective-permute-start.48) | collective-permute-done | bytes 294944 | tf_op jit(solution)/shard_map/ppermute | solution.py:611
  142.1 3.4 %collective-permute-done.47 = bf16[96,1408]{1,0:T(8,128)(2,1)S(1)} collective-permute-done((bf16[96,1408]{1,0:T(8,128)(2,1)S(1)}, bf16[96,1408]{1,0:T(8,128)(2,1)S(1)}, u32[]{:S(2)}, u32[]{:S(2)}) %collective-permute-start.47) | collective-permute-done | bytes 270368 | tf_op jit(solution)/shard_map/ppermute | solution.py:595
  145.6 4.2 %collective-permute-done.51 = bf16[96,1536]{1,0:T(8,128)(2,1)S(1)} collective-permute-done((bf16[96,1536]{1,0:T(8,128)(2,1)S(1)}, bf16[96,1536]{1,0:T(8,128)(2,1)S(1)}, u32[]{:S(2)}, u32[]{:S(2)}) %collective-permute-start.51) | collective-permute-done | bytes 294944 | tf_op jit(solution)/shard_map/ppermute | solution.py:611
  152.5 5.6 %collective-permute-done.52 = bf16[96,1408]{1,0:T(8,128)(2,1)S(1)} collective-permute-done((bf16[96,1408]{1,0:T(8,128)(2,1)S(1)}, bf16[96,1408]{1,0:T(8,128)(2,1)S(1)}, u32[]{:S(2)}, u32[]{:S(2)}) %collective-permute-start.52) | collective-permute-done | bytes 270368 | tf_op jit(solution)/shard_map/ppermute | solution.py:595
  162.8 3.6 %collective-permute-done.56 = bf16[96,1536]{1,0:T(8,128)(2,1)S(1)} collective-permute-done((bf16[96,1536]{1,0:T(8,128)(2,1)S(1)}, bf16[96,1536]{1,0:T(8,128)(2,1)S(1)}, u32[]{:S(2)}, u32[]{:S(2)}) %collective-permute-start.56) | collective-permute-done | bytes 294944 | tf_op jit(solution)/shard_map/ppermute | solution.py:611
  167.6 3.4 %collective-permute-done.53 = bf16[96,1408]{1,0:T(8,128)(2,1)S(1)} collective-permute-done((bf16[96,1408]{1,0:T(8,128)(2,1)S(1)}, bf16[96,1408]{1,0:T(8,128)(2,1)S(1)}, u32[]{:S(2)}, u32[]{:S(2)}) %collective-permute-start.53) | collective-permute-done | bytes 270368 | tf_op jit(solution)/shard_map/ppermute | solution.py:611
  177.2 2.9 %collective-permute-done.59.c2 = bf16[24,768]{1,0:T(8,128)(2,1)S(1)} collective-permute-done((bf16[24,768]{1,0:T(8,128)(2,1)S(1)}, bf16[24,768]{1,0:T(8,128)(2,1)S(1)}, u32[]{:S(2)}, u32[]{:S(2)}) %collective-permute-start.59) | collective-permute-done | bytes 36896 | tf_op jit(solution)/shard_map/ppermute | solution.py:595
  183.1 3.3 %collective-permute-done.63.c2 = bf16[24,1408]{1,0:T(8,128)(2,1)S(1)} collective-permute-done((bf16[24,1408]{1,0:T(8,128)(2,1)S(1)}, bf16[24,1408]{1,0:T(8,128)(2,1)S(1)}, u32[]{:S(2)}, u32[]{:S(2)}) %collective-permute-start.63) | collective-permute-done | bytes 67616 | tf_op jit(solution)/shard_map/ppermute | solution.py:574
  (193 shorter events, 98.2 us)
Async XLA Ops:
  11.8 9.1 %collective-permute-start.3 = (bf16[96,1408]{1,0:T(8,128)(2,1)S(1)}, bf16[96,1408]{1,0:T(8,128)(2,1)S(1)}, u32[]{:S(2)}, u32[]{:S(2)}) collective-permute-start(bf16[96,1408]{1,0:T(8,128)(2,1)S(1)} %arrange.1.r_0_), channel_id=1, source_target_pairs={{0,8},{4,12},{8,24},{12,28},{24,16},{28,20},{16,0},{20,4},{1,9},{5... | collective-permute-start | bytes 811016 | tf_op jit(solution)/shard_map/ppermute | solution.py:611
  13.6 16.0 %collective-permute-start.11 = (bf16[128,768]{1,0:T(8,128)(2,1)S(1)}, bf16[128,768]{1,0:T(8,128)(2,1)S(1)}, u32[]{:S(2)}, u32[]{:S(2)}) collective-permute-start(bf16[128,768]{1,0:T(8,128)(2,1)S(1)} %bitcast.46), channel_id=1, source_target_pairs={{0,2},{1,3},{2,0},{3,1},{4,6},{5,7},{6,4},{7,5},{8,10},{9,11},{10,... | collective-permute-start | bytes 589832 | tf_op jit(solution)/shard_map/ppermute | solution.py:574
  21.5 8.8 %collective-permute-start.6 = (bf16[96,1408]{1,0:T(8,128)(2,1)S(1)}, bf16[96,1408]{1,0:T(8,128)(2,1)S(1)}, u32[]{:S(2)}, u32[]{:S(2)}) collective-permute-start(bf16[96,1408]{1,0:T(8,128)(2,1)S(1)} %collective-permute-done.3.r_2_), channel_id=1, source_target_pairs={{0,8},{4,12},{8,24},{12,28},{24,16},{28,20},{16,0},{20,4},{1,9},{5... | collective-permute-start | bytes 811016 | tf_op jit(solution)/shard_map/ppermute | solution.py:611
  31.0 9.4 %collective-permute-start.12 = (bf16[96,1408]{1,0:T(8,128)(2,1)S(1)}, bf16[96,1408]{1,0:T(8,128)(2,1)S(1)}, u32[]{:S(2)}, u32[]{:S(2)}) collective-permute-start(bf16[96,1408]{1,0:T(8,128)(2,1)S(1)} %collective-permute-done.6.r_4_), channel_id=1, source_target_pairs={{0,8},{4,12},{8,24},{12,28},{24,16},{28,20},{16,0},{20,4},{1,9},{5... | collective-permute-start | bytes 811016 | tf_op jit(solution)/shard_map/ppermute | solution.py:611
  34.0 13.1 %collective-permute-start.16 = (bf16[96,1536]{1,0:T(8,128)(2,1)S(1)}, bf16[96,1536]{1,0:T(8,128)(2,1)S(1)}, u32[]{:S(2)}, u32[]{:S(2)}) collective-permute-start(bf16[96,1536]{1,0:T(8,128)(2,1)S(1)} %arrange_ff.1.r_0_), channel_id=1, source_target_pairs={{0,2},{1,3},{2,0},{3,1},{4,6},{5,7},{6,4},{7,5},{8,10},{9,11},{10,... | collective-permute-start | bytes 884744 | tf_op jit(solution)/shard_map/ppermute | solution.py:574
  41.5 8.7 %collective-permute-start.23 = (bf16[96,1536]{1,0:T(8,128)(2,1)S(1)}, bf16[96,1536]{1,0:T(8,128)(2,1)}, u32[]{:S(2)}, u32[]{:S(2)}) collective-permute-start(bf16[96,1536]{1,0:T(8,128)(2,1)S(1)} %arrange_ff.1.r_0_), channel_id=1, source_target_pairs={{0,8},{4,12},{8,24},{12,28},{24,16},{28,20},{16,0},{20,4},{1,9},{5... | collective-permute-start | bytes 884744 | tf_op jit(solution)/shard_map/ppermute | solution.py:611
  48.9 9.2 %collective-permute-start.17 = (bf16[1152,128]{1,0:T(8,128)(2,1)}, bf16[1152,128]{1,0:T(8,128)(2,1)}, u32[]{:S(2)}, u32[]{:S(2)}) collective-permute-start(bf16[1152,128]{1,0:T(8,128)(2,1)} %get-tuple-element.204.w0), channel_id=1, source_target_pairs={{0,1},{1,0},{2,3},{3,2},{4,5},{5,4},{6,7},{7,6},{8,9},{9,8},{10,11... | collective-permute-start | bytes 884744 | tf_op jit(solution)/shard_map/ppermute | solution.py:574
  50.2 9.8 %collective-permute-start.24 = (bf16[96,1536]{1,0:T(8,128)(2,1)}, bf16[96,1536]{1,0:T(8,128)(2,1)}, u32[]{:S(2)}, u32[]{:S(2)}) collective-permute-start(bf16[96,1536]{1,0:T(8,128)(2,1)} %collective-permute-done.23.r_2_), channel_id=1, source_target_pairs={{0,8},{4,12},{8,24},{12,28},{24,16},{28,20},{16,0},{20,4},{1,9},{5... | collective-permute-start | bytes 884744 | tf_op jit(solution)/shard_map/ppermute | solution.py:611
  51.5 11.5 %collective-permute-start.21 = (bf16[1152,128]{1,0:T(8,128)(2,1)}, bf16[1152,128]{1,0:T(8,128)(2,1)}, u32[]{:S(2)}, u32[]{:S(2)}) collective-permute-start(bf16[1152,128]{1,0:T(8,128)(2,1)} %get-tuple-element.204.w0), channel_id=1, source_target_pairs={{0,2},{1,3},{2,0},{3,1},{4,6},{5,7},{6,4},{7,5},{8,10},{9,11},{10,... | collective-permute-start | bytes 884744 | tf_op jit(solution)/shard_map/ppermute | solution.py:574
  60.1 10.4 %collective-permute-start.25 = (bf16[96,1536]{1,0:T(8,128)(2,1)}, bf16[96,1536]{1,0:T(8,128)(2,1)S(1)}, u32[]{:S(2)}, u32[]{:S(2)}) collective-permute-start(bf16[96,1536]{1,0:T(8,128)(2,1)} %collective-permute-done.24.r_4_), channel_id=1, source_target_pairs={{0,8},{4,12},{8,24},{12,28},{24,16},{28,20},{16,0},{20,4},{1,9},{5... | collective-permute-start | bytes 884744 | tf_op jit(solution)/shard_map/ppermute | solution.py:611
  64.9 10.1 %collective-permute-start.28 = (bf16[96,1536]{1,0:T(8,128)(2,1)}, bf16[96,1536]{1,0:T(8,128)(2,1)S(1)}, u32[]{:S(2)}, u32[]{:S(2)}) collective-permute-start(bf16[96,1536]{1,0:T(8,128)(2,1)} %collective-permute-done.23.r_2_), channel_id=1, source_target_pairs={{0,2},{1,3},{2,0},{3,1},{4,6},{5,7},{6,4},{7,5},{8,10},{9,11},{10,... | collective-permute-start | bytes 884744 | tf_op jit(solution)/shard_map/ppermute | solution.py:574
  111.8 9.9 %collective-permute-start.43 = (bf16[96,1536]{1,0:T(8,128)(2,1)S(1)}, bf16[96,1536]{1,0:T(8,128)(2,1)S(1)}, u32[]{:S(2)}, u32[]{:S(2)}) collective-permute-start(bf16[96,1536]{1,0:T(8,128)(2,1)S(1)} %get-tuple-element.235), channel_id=1, source_target_pairs={{0,8},{4,12},{8,24},{12,28},{24,16},{28,20},{16,0},{20,4},{1,9},{5... | collective-permute-start | bytes 884744 | tf_op jit(solution)/shard_map/ppermute | solution.py:611
  114.5 9.9 %collective-permute-start.42 = (bf16[96,1536]{1,0:T(8,128)(2,1)S(1)}, bf16[96,1536]{1,0:T(8,128)(2,1)S(1)}, u32[]{:S(2)}, u32[]{:S(2)}) collective-permute-start(bf16[96,1536]{1,0:T(8,128)(2,1)S(1)} %get-tuple-element.238), channel_id=1, source_target_pairs={{0,2},{1,3},{2,0},{3,1},{4,6},{5,7},{6,4},{7,5},{8,10},{9,11},{10,... | collective-permute-start | bytes 884744 | tf_op jit(solution)/shard_map/ppermute | solution.py:574
  126.0 9.9 %collective-permute-start.46 = (bf16[1200,128]{1,0:T(8,128)(2,1)S(1)}, bf16[1200,128]{1,0:T(8,128)(2,1)S(1)}, u32[]{:S(2)}, u32[]{:S(2)}) collective-permute-start(bf16[1200,128]{1,0:T(8,128)(2,1)S(1)} %add_convert_fusion), channel_id=1, source_target_pairs={{0,2},{1,3},{2,0},{3,1},{4,6},{5,7},{6,4},{7,5},{8,10},{9,11},{10,... | collective-permute-start | bytes 921608 | tf_op jit(solution)/shard_map/ppermute | solution.py:574
  132.6 9.5 %collective-permute-start.48 = (bf16[96,1536]{1,0:T(8,128)(2,1)S(1)}, bf16[96,1536]{1,0:T(8,128)(2,1)S(1)}, u32[]{:S(2)}, u32[]{:S(2)}) collective-permute-start(bf16[96,1536]{1,0:T(8,128)(2,1)S(1)} %add_convert_fusion.2), channel_id=1, source_target_pairs={{0,16},{4,20},{8,0},{12,4},{24,8},{28,12},{16,24},{20,28},{1,17},{... | collective-permute-start | bytes 884744 | tf_op jit(solution)/shard_map/ppermute | solution.py:611
  138.3 11.4 %collective-permute-start.51 = (bf16[96,1536]{1,0:T(8,128)(2,1)S(1)}, bf16[96,1536]{1,0:T(8,128)(2,1)S(1)}, u32[]{:S(2)}, u32[]{:S(2)}) collective-permute-start(bf16[96,1536]{1,0:T(8,128)(2,1)S(1)} %get-tuple-element.277), channel_id=1, source_target_pairs={{0,8},{4,12},{8,24},{12,28},{24,16},{28,20},{16,0},{20,4},{1,9},{5... | collective-permute-start | bytes 884744 | tf_op jit(solution)/shard_map/ppermute | solution.py:611
  139.5 12.5 %collective-permute-start.45 = (bf16[416,768]{1,0:T(8,128)(2,1)S(1)}, bf16[416,768]{1,0:T(8,128)(2,1)S(1)}, u32[]{:S(2)}, u32[]{:S(2)}) collective-permute-start(bf16[416,768]{1,0:T(8,128)(2,1)S(1)} %get-tuple-element.265), channel_id=1, source_target_pairs={{0,1},{1,0},{2,3},{3,2},{4,5},{5,4},{6,7},{7,6},{8,9},{9,8},{10,11... | collective-permute-start | bytes 1916936 | tf_op jit(solution)/shard_map/ppermute | solution.py:574
  150.8 9.4 %collective-permute-start.50 = (bf16[96,1408]{1,0:T(8,128)(2,1)S(1)}, bf16[96,1408]{1,0:T(8,128)(2,1)S(1)}, u32[]{:S(2)}, u32[]{:S(2)}) collective-permute-start(bf16[96,1408]{1,0:T(8,128)(2,1)S(1)} %add_convert_fusion.6), channel_id=1, source_target_pairs={{0,16},{4,20},{8,0},{12,4},{24,8},{28,12},{16,24},{20,28},{1,17},{... | collective-permute-start | bytes 811016 | tf_op jit(solution)/shard_map/ppermute | solution.py:611
  151.3 15.1 %collective-permute-start.56 = (bf16[96,1536]{1,0:T(8,128)(2,1)S(1)}, bf16[96,1536]{1,0:T(8,128)(2,1)S(1)}, u32[]{:S(2)}, u32[]{:S(2)}) collective-permute-start(bf16[96,1536]{1,0:T(8,128)(2,1)S(1)} %get-tuple-element.288), channel_id=1, source_target_pairs={{0,16},{4,20},{8,0},{12,4},{24,8},{28,12},{16,24},{20,28},{1,17},{... | collective-permute-start | bytes 884744 | tf_op jit(solution)/shard_map/ppermute | solution.py:611
  152.2 18.8 %collective-permute-start.49 = (bf16[320,768]{1,0:T(8,128)(2,1)S(1)}, bf16[320,768]{1,0:T(8,128)(2,1)S(1)}, u32[]{:S(2)}, u32[]{:S(2)}) collective-permute-start(bf16[320,768]{1,0:T(8,128)(2,1)S(1)} %input_pair.1.sent), channel_id=1, source_target_pairs={{0,2},{1,3},{2,0},{3,1},{4,6},{5,7},{6,4},{7,5},{8,10},{9,11},{10,... | collective-permute-start | bytes 1474568 | tf_op jit(solution)/shard_map/ppermute | solution.py:574
  160.3 10.7 %collective-permute-start.53 = (bf16[96,1408]{1,0:T(8,128)(2,1)S(1)}, bf16[96,1408]{1,0:T(8,128)(2,1)S(1)}, u32[]{:S(2)}, u32[]{:S(2)}) collective-permute-start(bf16[96,1408]{1,0:T(8,128)(2,1)S(1)} %add_convert_fusion.5), channel_id=1, source_target_pairs={{0,16},{4,20},{8,0},{12,4},{24,8},{28,12},{16,24},{20,28},{1,17},{... | collective-permute-start | bytes 811016 | tf_op jit(solution)/shard_map/ppermute | solution.py:611
  161.8 9.1 %collective-permute-start.54 = (bf16[96,1408]{1,0:T(8,128)(2,1)S(1)}, bf16[96,1408]{1,0:T(8,128)(2,1)S(1)}, u32[]{:S(2)}, u32[]{:S(2)}) collective-permute-start(bf16[96,1408]{1,0:T(8,128)(2,1)S(1)} %get-tuple-element.281), channel_id=1, source_target_pairs={{0,4},{4,0},{8,12},{12,8},{16,20},{20,16},{24,28},{28,24},{1,5},{5... | collective-permute-start | bytes 811016 | tf_op jit(solution)/shard_map/ppermute | solution.py:595
  171.1 9.9 %collective-permute-start.55 = (bf16[96,1408]{1,0:T(8,128)(2,1)S(1)}, bf16[96,1408]{1,0:T(8,128)(2,1)S(1)}, u32[]{:S(2)}, u32[]{:S(2)}) collective-permute-start(bf16[96,1408]{1,0:T(8,128)(2,1)S(1)} %add_convert_fusion.4), channel_id=1, source_target_pairs={{0,16},{4,20},{8,0},{12,4},{24,8},{28,12},{16,24},{20,28},{1,17},{... | collective-permute-start | bytes 811016 | tf_op jit(solution)/shard_map/ppermute | solution.py:611
  172.3 8.7 %collective-permute-start.61 = (bf16[96,1408]{1,0:T(8,128)(2,1)S(1)}, bf16[96,1408]{1,0:T(8,128)(2,1)S(1)}, u32[]{:S(2)}, u32[]{:S(2)}) collective-permute-start(bf16[96,1408]{1,0:T(8,128)(2,1)S(1)} %get-tuple-element.296), channel_id=1, source_target_pairs={{0,4},{4,0},{8,12},{12,8},{16,20},{20,16},{24,28},{28,24},{1,5},{5... | collective-permute-start | bytes 811016 | tf_op jit(solution)/shard_map/ppermute | solution.py:595
  (63 other events, 416.3 us)

commit v8 on v6

--- a/solution.py
+++ b/solution.py
@@ -745,8 +745,8 @@
         return call(lambda *r: body(slots, *r), name, outs, same=same)(*args)
 
     if direct:
-        ready = place((0, 1, 2, 3, 4), False, *slabs[:5])
-        wq, _, _, wo_col, norms = place((5, 6, 7), True, *ready, *slabs[5:])
+        ready = place((0, 1, 2, 3, 4, 5, 6), False, *slabs[:7])
+        wq, _, _, wo_col, norms = place((7,), True, *ready, slabs[7])
     else:
         blank = [jnp.zeros((width, n), bf16) for n in (6 * wide, 128, wide - 64)]
         wq, _, _, wo_col, norms = place((0,), True, *blank, slabs[0])

time: 188 us -> 187 us (level)
  waiting for transfers between devices: 84.4 us -> 88.5 us
  local copies, waits for them, and re-layouts: 9.02 us -> 5.45 us
    ppermute x14, waiting for transfers between devices: 36.2 us -> 40 us  [over_x(): return lax.ppermute(x, 'seq', [(i, i ^ 1) for i in range(8)])]
    unnamed x44 -> x40, local copies, waits for them, and re-layouts: 7.59 us -> 4.02 us
  transfers between devices with their start and end apart: 65 -> 65, of which waited for: 33 -> 32; matrix products, arithmetic and copies ran while one was open for 1% -> 1% of each run, Pallas kernels for 14% -> 14%
where the time goes in v8:
time: 187 us
  waiting for transfers between devices  88.5 us (47%)
  starting transfers between devices  56.9 us (30%)
  Pallas kernels  33.7 us (18%)
  local copies, waits for them, and re-layouts  5.45 us (3%)
    ppermute x14, waiting for transfers between devices, over_x(): return lax.ppermute(x, 'seq', [(i, i ^ 1) for i in range(8)])  40 us
    pallas_call x28, Pallas kernels, run(): pl.pallas_call(body, name=name, out_shape=[jax.ShapeDtypeStruct(s, t) for...  33.7 us
    ppermute x15, waiting for transfers between devices, along_ring(): lax.ppermute(x, 'seq', [(2 * z + i, 2 * to + i) for z, to in route for i...  31.5 us
    ppermute x15, starting transfers between devices, along_ring(): lax.ppermute(x, 'seq', [(2 * z + i, 2 * to + i) for z, to in route for i...  20.9 us
    ppermute x34, starting transfers between devices, swap(): return lax.ppermute(x, 'blk', [(i, i ^ k) for i in range(RANKS)])  19.6 us
    ppermute x34, waiting for transfers between devices, swap(): return lax.ppermute(x, 'blk', [(i, i ^ k) for i in range(RANKS)])  16.9 us
    ppermute x14, starting transfers between devices, over_x(): return lax.ppermute(x, 'seq', [(i, i ^ 1) for i in range(8)])  14.6 us
    unnamed x40, local copies, waits for them, and re-layouts  4.02 us
  transfers between devices with their start and end apart: 65, of which 32 were waited for; matrix products, arithmetic and copies ran while one was open for 1% of the time, Pallas kernels for 14%

profile of v8, /device:TPU:0, one launch (start us, length us, event | category | flops | bytes accessed | tf_op | source)
XLA Modules:
  0.0 187.1 jit_solution(5696360100502950435)
XLA Ops:
  3.2 2.6 %collective-permute-start.1 = (bf16[24,1408]{1,0:T(8,128)(2,1)}, bf16[24,1408]{1,0:T(8,128)(2,1)S(1)}, u32[]{:S(2)}, u32[]{:S(2)}) collective-permute-start(bf16[24,1408]{1,0:T(8,128)(2,1)} %get-tuple-element.161), channel_id=1, source_target_pairs={{0,2},{1,3},{2,0},{3,1},{4,6},{5,7},{6,4},{7,5},{8,10},{9,11},{10,... | collective-permute-start | bytes 202760 | tf_op jit(solution)/shard_map/ppermute | solution.py:574
  14.9 3.9 %collective-permute-done.4.r_1_ = bf16[96,1408]{1,0:T(8,128)(2,1)S(1)} collective-permute-done((bf16[96,1408]{1,0:T(8,128)(2,1)S(1)}, bf16[96,1408]{1,0:T(8,128)(2,1)S(1)}, u32[]{:S(2)}, u32[]{:S(2)}) %collective-permute-start.4) | collective-permute-done | bytes 270368 | tf_op jit(solution)/shard_map/ppermute | solution.py:595
  26.7 2.8 %collective-permute-done.9.p2 = bf16[24,768]{1,0:T(8,128)(2,1)S(1)} collective-permute-done((bf16[24,768]{1,0:T(8,128)(2,1)S(1)}, bf16[24,768]{1,0:T(8,128)(2,1)S(1)}, u32[]{:S(2)}, u32[]{:S(2)}) %collective-permute-start.9) | collective-permute-done | bytes 36896 | tf_op jit(solution)/shard_map/ppermute | solution.py:595
  34.8 4.0 %collective-permute-done.13.r_5_ = bf16[96,1408]{1,0:T(8,128)(2,1)S(1)} collective-permute-done((bf16[96,1408]{1,0:T(8,128)(2,1)S(1)}, bf16[96,1408]{1,0:T(8,128)(2,1)S(1)}, u32[]{:S(2)}, u32[]{:S(2)}) %collective-permute-start.13) | collective-permute-done | bytes 270368 | tf_op jit(solution)/shard_map/ppermute | solution.py:595
  43.6 4.4 %collective-permute-done.15.r_3_ = bf16[96,1408]{1,0:T(8,128)(2,1)S(1)} collective-permute-done((bf16[96,1408]{1,0:T(8,128)(2,1)S(1)}, bf16[96,1408]{1,0:T(8,128)(2,1)S(1)}, u32[]{:S(2)}, u32[]{:S(2)}) %collective-permute-start.15) | collective-permute-done | bytes 270368 | tf_op jit(solution)/shard_map/ppermute | solution.py:595
  52.7 4.8 %attend.1 = (bf16[160,192]{1,0:T(8,128)(2,1)S(1)}, bf16[160,192]{1,0:T(8,128)(2,1)S(1)}, bf16[160,192]{1,0:T(8,128)(2,1)S(1)}, bf16[160,192]{1,0:T(8,128)(2,1)S(...) custom-call(bf16[512,768]{1,0:T(8,128)(2,1)S(1)} %join_rows.1.r_0_.x, ...), custom_call_target="tpu_custom_call" | custom-call | flops 7000000 | bytes 7000 | tf_op jit(solution)/shard_map/attend/pallas_call | solution.py:34
  59.5 3.5 %collective-permute-start.25 = (bf16[96,1536]{1,0:T(8,128)(2,1)}, bf16[96,1536]{1,0:T(8,128)(2,1)S(1)}, u32[]{:S(2)}, u32[]{:S(2)}) collective-permute-start(bf16[96,1536]{1,0:T(8,128)(2,1)} %collective-permute-done.24.r_4_), channel_id=1, source_target_pairs={{0,8},{4,12},{8,24},{12,28},{24,16},{28,20},{16,0},{20,4},{1,9},{5... | collective-permute-start | bytes 884744 | tf_op jit(solution)/shard_map/ppermute | solution.py:611
  64.6 5.5 %collective-permute-done.25.r_5_ = bf16[96,1536]{1,0:T(8,128)(2,1)S(1)} collective-permute-done((bf16[96,1536]{1,0:T(8,128)(2,1)}, bf16[96,1536]{1,0:T(8,128)(2,1)S(1)}, u32[]{:S(2)}, u32[]{:S(2)}) %collective-permute-start.25) | collective-permute-done | bytes 294944 | tf_op jit(solution)/shard_map/ppermute | solution.py:611
  76.3 3.7 %collective-permute-done.27.h2 = bf16[160,768]{1,0:T(8,128)(2,1)S(1)} collective-permute-done((bf16[160,768]{1,0:T(8,128)(2,1)S(1)}, bf16[160,768]{1,0:T(8,128)(2,1)S(1)}, u32[]{:S(2)}, u32[]{:S(2)}) %collective-permute-start.27) | collective-permute-done | bytes 245792 | tf_op jit(solution)/shard_map/ppermute | solution.py:595
  82.6 2.3 %feed.1 = (f32[160,768]{1,0:T(8,128)S(1)}, bf16[160,768]{1,0:T(8,128)(2,1)S(1)}, bf16[2,160,768]{2,1,0:T(8,128)(2,1)S(1)}, bf16[4,160,768]{2,1,0:T(8,128)(2,1)S(1)}, bf16[4,160,768]{2,1,0:T(8,128)(2,1)S(1)}) custom-call(bf16[160,768]{1,0:T(8,128)(2,1)S(1)} %get-tuple-element.209.h0, bf16[160,768]{1,0:T(8,128)(2,1)S(1)} %collective-permute-done.26.h1, ...), custom_call_target="tpu_custom_call" | custom-call | flops 3000000 | bytes 3000 | tf_op jit(solution)/shard_map/feed/pallas_call | solution.py:34
  88.0 7.0 %collective-permute-done.33.f2 = bf16[160,768]{1,0:T(8,128)(2,1)S(1)} collective-permute-done((bf16[160,768]{1,0:T(8,128)(2,1)S(1)}, bf16[160,768]{1,0:T(8,128)(2,1)S(1)}, u32[]{:S(2)}, u32[]{:S(2)}) %collective-permute-start.33) | collective-permute-done | bytes 245792 | tf_op jit(solution)/shard_map/ppermute | solution.py:595
  97.1 6.2 %collective-permute-done.35.d2 = bf16[160,768]{1,0:T(8,128)(2,1)S(1)} collective-permute-done((bf16[160,768]{1,0:T(8,128)(2,1)S(1)}, bf16[160,768]{1,0:T(8,128)(2,1)S(1)}, u32[]{:S(2)}, u32[]{:S(2)}) %collective-permute-start.35) | collective-permute-done | bytes 245792 | tf_op jit(solution)/shard_map/ppermute | solution.py:595
  109.7 2.1 %feed_grads.1 = (bf16[96,1536]{1,0:T(8,128)(2,1)S(1)}, bf16[96,1536]{1,0:T(8,128)(2,1)S(1)}, bf16[96,1536]{1,0:T(8,128)(2,1)S(1)}, bf16[96,1536]{1,0:T(8,128)(2,...) custom-call(bf16[160,768]{1,0:T(8,128)(2,1)S(1)} %get-tuple-element., ...), custom_call_target="tpu_custom_call" | custom-call | flops 3000000 | bytes 3000 | tf_op jit(solution)/shard_map/feed_grads/pallas_call | solution.py:34
  111.8 2.7 %collective-permute-start.43 = (bf16[96,1536]{1,0:T(8,128)(2,1)S(1)}, bf16[96,1536]{1,0:T(8,128)(2,1)S(1)}, u32[]{:S(2)}, u32[]{:S(2)}) collective-permute-start(bf16[96,1536]{1,0:T(8,128)(2,1)S(1)} %get-tuple-element.235), channel_id=1, source_target_pairs={{0,8},{4,12},{8,24},{12,28},{24,16},{28,20},{16,0},{20,4},{1,9},{5... | collective-permute-start | bytes 884744 | tf_op jit(solution)/shard_map/ppermute | solution.py:611
  121.7 2.7 %collective-permute-done.42 = bf16[96,1536]{1,0:T(8,128)(2,1)S(1)} collective-permute-done((bf16[96,1536]{1,0:T(8,128)(2,1)S(1)}, bf16[96,1536]{1,0:T(8,128)(2,1)S(1)}, u32[]{:S(2)}, u32[]{:S(2)}) %collective-permute-start.42) | collective-permute-done | bytes 294944 | tf_op jit(solution)/shard_map/ppermute | solution.py:574
  127.6 4.8 %attend_back.1.dqkv = bf16[640,768]{1,0:T(8,128)(2,1)S(1)} custom-call(bf16[160,192]{1,0:T(8,128)(2,1)S(1)} %get-tuple-element.251.r_0_, bf16[2640,128]{1,0:T(8,128)(2,1)S(1)} %collective-permute-done.39.r_1_.o1, bf16[160,192]{1,0:T(8,128)(2,1)S(1)} %collective-permute-done.40.r_2_, bf16[160,192]{1,0:T(8,128)(2,1)S(1)} %collective-permute-done.41.r_3_, ...), custom_call_target="tpu_custom_call" | custom-call | flops 7000000 | bytes 7000 | tf_op jit(solution)/shard_map/attend_back/pallas_call | solution.py:34
  138.4 4.2 %collective-permute-done.48.a2 = bf16[96,1536]{1,0:T(8,128)(2,1)S(1)} collective-permute-done((bf16[96,1536]{1,0:T(8,128)(2,1)S(1)}, bf16[96,1536]{1,0:T(8,128)(2,1)S(1)}, u32[]{:S(2)}, u32[]{:S(2)}) %collective-permute-start.48) | collective-permute-done | bytes 294944 | tf_op jit(solution)/shard_map/ppermute | solution.py:611
  142.6 6.7 %collective-permute-done.49 = bf16[96,1536]{1,0:T(8,128)(2,1)S(1)} collective-permute-done((bf16[96,1536]{1,0:T(8,128)(2,1)S(1)}, bf16[96,1536]{1,0:T(8,128)(2,1)S(1)}, u32[]{:S(2)}, u32[]{:S(2)}) %collective-permute-start.49) | collective-permute-done | bytes 294944 | tf_op jit(solution)/shard_map/ppermute | solution.py:611
  152.7 4.6 %collective-permute-done.52 = bf16[96,1408]{1,0:T(8,128)(2,1)S(1)} collective-permute-done((bf16[96,1408]{1,0:T(8,128)(2,1)S(1)}, bf16[96,1408]{1,0:T(8,128)(2,1)S(1)}, u32[]{:S(2)}, u32[]{:S(2)}) %collective-permute-start.52) | collective-permute-done | bytes 270368 | tf_op jit(solution)/shard_map/ppermute | solution.py:595
  157.3 2.6 %collective-permute-done.51 = bf16[96,1408]{1,0:T(8,128)(2,1)S(1)} collective-permute-done((bf16[96,1408]{1,0:T(8,128)(2,1)S(1)}, bf16[96,1408]{1,0:T(8,128)(2,1)S(1)}, u32[]{:S(2)}, u32[]{:S(2)}) %collective-permute-start.51) | collective-permute-done | bytes 270368 | tf_op jit(solution)/shard_map/ppermute | solution.py:611
  163.0 3.1 %collective-permute-done.56 = bf16[96,1536]{1,0:T(8,128)(2,1)S(1)} collective-permute-done((bf16[96,1536]{1,0:T(8,128)(2,1)S(1)}, bf16[96,1536]{1,0:T(8,128)(2,1)S(1)}, u32[]{:S(2)}, u32[]{:S(2)}) %collective-permute-start.56) | collective-permute-done | bytes 294944 | tf_op jit(solution)/shard_map/ppermute | solution.py:611
  166.7 3.4 %collective-permute-done.53 = bf16[96,1408]{1,0:T(8,128)(2,1)S(1)} collective-permute-done((bf16[96,1408]{1,0:T(8,128)(2,1)S(1)}, bf16[96,1408]{1,0:T(8,128)(2,1)S(1)}, u32[]{:S(2)}, u32[]{:S(2)}) %collective-permute-start.53) | collective-permute-done | bytes 270368 | tf_op jit(solution)/shard_map/ppermute | solution.py:611
  176.9 2.8 %collective-permute-done.59.c2 = bf16[24,768]{1,0:T(8,128)(2,1)S(1)} collective-permute-done((bf16[24,768]{1,0:T(8,128)(2,1)S(1)}, bf16[24,768]{1,0:T(8,128)(2,1)S(1)}, u32[]{:S(2)}, u32[]{:S(2)}) %collective-permute-start.59) | collective-permute-done | bytes 36896 | tf_op jit(solution)/shard_map/ppermute | solution.py:595
  182.7 3.3 %collective-permute-done.63.c2 = bf16[24,1408]{1,0:T(8,128)(2,1)S(1)} collective-permute-done((bf16[24,1408]{1,0:T(8,128)(2,1)S(1)}, bf16[24,1408]{1,0:T(8,128)(2,1)S(1)}, u32[]{:S(2)}, u32[]{:S(2)}) %collective-permute-start.63) | collective-permute-done | bytes 67616 | tf_op jit(solution)/shard_map/ppermute | solution.py:574
  (189 shorter events, 91.8 us)
Async XLA Ops:
  11.8 9.1 %collective-permute-start.3 = (bf16[96,1408]{1,0:T(8,128)(2,1)S(1)}, bf16[96,1408]{1,0:T(8,128)(2,1)S(1)}, u32[]{:S(2)}, u32[]{:S(2)}) collective-permute-start(bf16[96,1408]{1,0:T(8,128)(2,1)S(1)} %arrange.1.r_0_), channel_id=1, source_target_pairs={{0,8},{4,12},{8,24},{12,28},{24,16},{28,20},{16,0},{20,4},{1,9},{5... | collective-permute-start | bytes 811016 | tf_op jit(solution)/shard_map/ppermute | solution.py:611
  13.6 16.0 %collective-permute-start.11 = (bf16[128,768]{1,0:T(8,128)(2,1)S(1)}, bf16[128,768]{1,0:T(8,128)(2,1)S(1)}, u32[]{:S(2)}, u32[]{:S(2)}) collective-permute-start(bf16[128,768]{1,0:T(8,128)(2,1)S(1)} %bitcast.46), channel_id=1, source_target_pairs={{0,2},{1,3},{2,0},{3,1},{4,6},{5,7},{6,4},{7,5},{8,10},{9,11},{10,... | collective-permute-start | bytes 589832 | tf_op jit(solution)/shard_map/ppermute | solution.py:574
  20.9 8.6 %collective-permute-start.7 = (bf16[96,1408]{1,0:T(8,128)(2,1)S(1)}, bf16[96,1408]{1,0:T(8,128)(2,1)S(1)}, u32[]{:S(2)}, u32[]{:S(2)}) collective-permute-start(bf16[96,1408]{1,0:T(8,128)(2,1)S(1)} %collective-permute-done.3.r_2_), channel_id=1, source_target_pairs={{0,4},{4,0},{8,12},{12,8},{16,20},{20,16},{24,28},{28,24},{1,5},{5... | collective-permute-start | bytes 811016 | tf_op jit(solution)/shard_map/ppermute | solution.py:595
  21.5 8.8 %collective-permute-start.6 = (bf16[96,1408]{1,0:T(8,128)(2,1)S(1)}, bf16[96,1408]{1,0:T(8,128)(2,1)S(1)}, u32[]{:S(2)}, u32[]{:S(2)}) collective-permute-start(bf16[96,1408]{1,0:T(8,128)(2,1)S(1)} %collective-permute-done.3.r_2_), channel_id=1, source_target_pairs={{0,8},{4,12},{8,24},{12,28},{24,16},{28,20},{16,0},{20,4},{1,9},{5... | collective-permute-start | bytes 811016 | tf_op jit(solution)/shard_map/ppermute | solution.py:611
  31.0 9.4 %collective-permute-start.12 = (bf16[96,1408]{1,0:T(8,128)(2,1)S(1)}, bf16[96,1408]{1,0:T(8,128)(2,1)S(1)}, u32[]{:S(2)}, u32[]{:S(2)}) collective-permute-start(bf16[96,1408]{1,0:T(8,128)(2,1)S(1)} %collective-permute-done.6.r_4_), channel_id=1, source_target_pairs={{0,8},{4,12},{8,24},{12,28},{24,16},{28,20},{16,0},{20,4},{1,9},{5... | collective-permute-start | bytes 811016 | tf_op jit(solution)/shard_map/ppermute | solution.py:611
  33.3 10.3 %collective-permute-start.16 = (bf16[96,1536]{1,0:T(8,128)(2,1)S(1)}, bf16[96,1536]{1,0:T(8,128)(2,1)S(1)}, u32[]{:S(2)}, u32[]{:S(2)}) collective-permute-start(bf16[96,1536]{1,0:T(8,128)(2,1)S(1)} %arrange_ff.1.r_0_), channel_id=1, source_target_pairs={{0,2},{1,3},{2,0},{3,1},{4,6},{5,7},{6,4},{7,5},{8,10},{9,11},{10,... | collective-permute-start | bytes 884744 | tf_op jit(solution)/shard_map/ppermute | solution.py:574
  41.5 8.7 %collective-permute-start.23 = (bf16[96,1536]{1,0:T(8,128)(2,1)S(1)}, bf16[96,1536]{1,0:T(8,128)(2,1)}, u32[]{:S(2)}, u32[]{:S(2)}) collective-permute-start(bf16[96,1536]{1,0:T(8,128)(2,1)S(1)} %arrange_ff.1.r_0_), channel_id=1, source_target_pairs={{0,8},{4,12},{8,24},{12,28},{24,16},{28,20},{16,0},{20,4},{1,9},{5... | collective-permute-start | bytes 884744 | tf_op jit(solution)/shard_map/ppermute | solution.py:611
  48.8 8.7 %collective-permute-start.17 = (bf16[1152,128]{1,0:T(8,128)(2,1)}, bf16[1152,128]{1,0:T(8,128)(2,1)}, u32[]{:S(2)}, u32[]{:S(2)}) collective-permute-start(bf16[1152,128]{1,0:T(8,128)(2,1)} %get-tuple-element.204.w0), channel_id=1, source_target_pairs={{0,1},{1,0},{2,3},{3,2},{4,5},{5,4},{6,7},{7,6},{8,9},{9,8},{10,11... | collective-permute-start | bytes 884744 | tf_op jit(solution)/shard_map/ppermute | solution.py:574
  50.2 9.2 %collective-permute-start.24 = (bf16[96,1536]{1,0:T(8,128)(2,1)}, bf16[96,1536]{1,0:T(8,128)(2,1)}, u32[]{:S(2)}, u32[]{:S(2)}) collective-permute-start(bf16[96,1536]{1,0:T(8,128)(2,1)} %collective-permute-done.23.r_2_), channel_id=1, source_target_pairs={{0,8},{4,12},{8,24},{12,28},{24,16},{28,20},{16,0},{20,4},{1,9},{5... | collective-permute-start | bytes 884744 | tf_op jit(solution)/shard_map/ppermute | solution.py:611
  50.9 12.1 %collective-permute-start.21 = (bf16[1152,128]{1,0:T(8,128)(2,1)}, bf16[1152,128]{1,0:T(8,128)(2,1)}, u32[]{:S(2)}, u32[]{:S(2)}) collective-permute-start(bf16[1152,128]{1,0:T(8,128)(2,1)} %get-tuple-element.204.w0), channel_id=1, source_target_pairs={{0,2},{1,3},{2,0},{3,1},{4,6},{5,7},{6,4},{7,5},{8,10},{9,11},{10,... | collective-permute-start | bytes 884744 | tf_op jit(solution)/shard_map/ppermute | solution.py:574
  59.5 10.6 %collective-permute-start.25 = (bf16[96,1536]{1,0:T(8,128)(2,1)}, bf16[96,1536]{1,0:T(8,128)(2,1)S(1)}, u32[]{:S(2)}, u32[]{:S(2)}) collective-permute-start(bf16[96,1536]{1,0:T(8,128)(2,1)} %collective-permute-done.24.r_4_), channel_id=1, source_target_pairs={{0,8},{4,12},{8,24},{12,28},{24,16},{28,20},{16,0},{20,4},{1,9},{5... | collective-permute-start | bytes 884744 | tf_op jit(solution)/shard_map/ppermute | solution.py:611
  64.3 10.7 %collective-permute-start.28 = (bf16[96,1536]{1,0:T(8,128)(2,1)}, bf16[96,1536]{1,0:T(8,128)(2,1)S(1)}, u32[]{:S(2)}, u32[]{:S(2)}) collective-permute-start(bf16[96,1536]{1,0:T(8,128)(2,1)} %collective-permute-done.23.r_2_), channel_id=1, source_target_pairs={{0,2},{1,3},{2,0},{3,1},{4,6},{5,7},{6,4},{7,5},{8,10},{9,11},{10,... | collective-permute-start | bytes 884744 | tf_op jit(solution)/shard_map/ppermute | solution.py:574
  111.8 9.9 %collective-permute-start.43 = (bf16[96,1536]{1,0:T(8,128)(2,1)S(1)}, bf16[96,1536]{1,0:T(8,128)(2,1)S(1)}, u32[]{:S(2)}, u32[]{:S(2)}) collective-permute-start(bf16[96,1536]{1,0:T(8,128)(2,1)S(1)} %get-tuple-element.235), channel_id=1, source_target_pairs={{0,8},{4,12},{8,24},{12,28},{24,16},{28,20},{16,0},{20,4},{1,9},{5... | collective-permute-start | bytes 884744 | tf_op jit(solution)/shard_map/ppermute | solution.py:611
  114.5 9.9 %collective-permute-start.42 = (bf16[96,1536]{1,0:T(8,128)(2,1)S(1)}, bf16[96,1536]{1,0:T(8,128)(2,1)S(1)}, u32[]{:S(2)}, u32[]{:S(2)}) collective-permute-start(bf16[96,1536]{1,0:T(8,128)(2,1)S(1)} %get-tuple-element.238), channel_id=1, source_target_pairs={{0,2},{1,3},{2,0},{3,1},{4,6},{5,7},{6,4},{7,5},{8,10},{9,11},{10,... | collective-permute-start | bytes 884744 | tf_op jit(solution)/shard_map/ppermute | solution.py:574
  126.0 10.0 %collective-permute-start.46 = (bf16[1200,128]{1,0:T(8,128)(2,1)S(1)}, bf16[1200,128]{1,0:T(8,128)(2,1)S(1)}, u32[]{:S(2)}, u32[]{:S(2)}) collective-permute-start(bf16[1200,128]{1,0:T(8,128)(2,1)S(1)} %add_convert_fusion), channel_id=1, source_target_pairs={{0,2},{1,3},{2,0},{3,1},{4,6},{5,7},{6,4},{7,5},{8,10},{9,11},{10,... | collective-permute-start | bytes 921608 | tf_op jit(solution)/shard_map/ppermute | solution.py:574
  132.6 10.0 %collective-permute-start.48 = (bf16[96,1536]{1,0:T(8,128)(2,1)S(1)}, bf16[96,1536]{1,0:T(8,128)(2,1)S(1)}, u32[]{:S(2)}, u32[]{:S(2)}) collective-permute-start(bf16[96,1536]{1,0:T(8,128)(2,1)S(1)} %add_convert_fusion.2), channel_id=1, source_target_pairs={{0,16},{4,20},{8,0},{12,4},{24,8},{28,12},{16,24},{20,28},{1,17},{... | collective-permute-start | bytes 884744 | tf_op jit(solution)/shard_map/ppermute | solution.py:611
  133.4 15.8 %collective-permute-start.49 = (bf16[96,1536]{1,0:T(8,128)(2,1)S(1)}, bf16[96,1536]{1,0:T(8,128)(2,1)S(1)}, u32[]{:S(2)}, u32[]{:S(2)}) collective-permute-start(bf16[96,1536]{1,0:T(8,128)(2,1)S(1)} %get-tuple-element.271), channel_id=1, source_target_pairs={{0,8},{4,12},{8,24},{12,28},{24,16},{28,20},{16,0},{20,4},{1,9},{5... | collective-permute-start | bytes 884744 | tf_op jit(solution)/shard_map/ppermute | solution.py:611
  137.3 11.9 %collective-permute-start.47 = (bf16[96,1408]{1,0:T(8,128)(2,1)S(1)}, bf16[96,1408]{1,0:T(8,128)(2,1)S(1)}, u32[]{:S(2)}, u32[]{:S(2)}) collective-permute-start(bf16[96,1408]{1,0:T(8,128)(2,1)S(1)} %get-tuple-element.269), channel_id=1, source_target_pairs={{0,4},{4,0},{8,12},{12,8},{16,20},{20,16},{24,28},{28,24},{1,5},{5... | collective-permute-start | bytes 811016 | tf_op jit(solution)/shard_map/ppermute | solution.py:595
  138.4 13.7 %collective-permute-start.45 = (bf16[416,768]{1,0:T(8,128)(2,1)S(1)}, bf16[416,768]{1,0:T(8,128)(2,1)S(1)}, u32[]{:S(2)}, u32[]{:S(2)}) collective-permute-start(bf16[416,768]{1,0:T(8,128)(2,1)S(1)} %get-tuple-element.265), channel_id=1, source_target_pairs={{0,1},{1,0},{2,3},{3,2},{4,5},{5,4},{6,7},{7,6},{8,9},{9,8},{10,11... | collective-permute-start | bytes 1916936 | tf_op jit(solution)/shard_map/ppermute | solution.py:574
  150.4 9.4 %collective-permute-start.51 = (bf16[96,1408]{1,0:T(8,128)(2,1)S(1)}, bf16[96,1408]{1,0:T(8,128)(2,1)S(1)}, u32[]{:S(2)}, u32[]{:S(2)}) collective-permute-start(bf16[96,1408]{1,0:T(8,128)(2,1)S(1)} %add_convert_fusion.6), channel_id=1, source_target_pairs={{0,16},{4,20},{8,0},{12,4},{24,8},{28,12},{16,24},{20,28},{1,17},{... | collective-permute-start | bytes 811016 | tf_op jit(solution)/shard_map/ppermute | solution.py:611
  151.5 14.6 %collective-permute-start.56 = (bf16[96,1536]{1,0:T(8,128)(2,1)S(1)}, bf16[96,1536]{1,0:T(8,128)(2,1)S(1)}, u32[]{:S(2)}, u32[]{:S(2)}) collective-permute-start(bf16[96,1536]{1,0:T(8,128)(2,1)S(1)} %get-tuple-element.288), channel_id=1, source_target_pairs={{0,16},{4,20},{8,0},{12,4},{24,8},{28,12},{16,24},{20,28},{1,17},{... | collective-permute-start | bytes 884744 | tf_op jit(solution)/shard_map/ppermute | solution.py:611
  152.2 17.9 %collective-permute-start.50 = (bf16[320,768]{1,0:T(8,128)(2,1)S(1)}, bf16[320,768]{1,0:T(8,128)(2,1)S(1)}, u32[]{:S(2)}, u32[]{:S(2)}) collective-permute-start(bf16[320,768]{1,0:T(8,128)(2,1)S(1)} %input_pair.1.sent), channel_id=1, source_target_pairs={{0,2},{1,3},{2,0},{3,1},{4,6},{5,7},{6,4},{7,5},{8,10},{9,11},{10,... | collective-permute-start | bytes 1474568 | tf_op jit(solution)/shard_map/ppermute | solution.py:574
  160.0 10.2 %collective-permute-start.53 = (bf16[96,1408]{1,0:T(8,128)(2,1)S(1)}, bf16[96,1408]{1,0:T(8,128)(2,1)S(1)}, u32[]{:S(2)}, u32[]{:S(2)}) collective-permute-start(bf16[96,1408]{1,0:T(8,128)(2,1)S(1)} %add_convert_fusion.5), channel_id=1, source_target_pairs={{0,16},{4,20},{8,0},{12,4},{24,8},{28,12},{16,24},{20,28},{1,17},{... | collective-permute-start | bytes 811016 | tf_op jit(solution)/shard_map/ppermute | solution.py:611
  170.3 10.3 %collective-permute-start.55 = (bf16[96,1408]{1,0:T(8,128)(2,1)S(1)}, bf16[96,1408]{1,0:T(8,128)(2,1)S(1)}, u32[]{:S(2)}, u32[]{:S(2)}) collective-permute-start(bf16[96,1408]{1,0:T(8,128)(2,1)S(1)} %add_convert_fusion.4), channel_id=1, source_target_pairs={{0,16},{4,20},{8,0},{12,4},{24,8},{28,12},{16,24},{20,28},{1,17},{... | collective-permute-start | bytes 811016 | tf_op jit(solution)/shard_map/ppermute | solution.py:611
  (61 other events, 432.6 us)
